TPU v7x, 32 devices: a whole 2x2x4 slice. The times are simulated.
32 devices in a mesh: dp: 8 (over z, y), mp: 4 (over x, core).
Axes of the slice: x: 2, y: 2, z: 4, core: 2. Of those that a mesh axis runs over, the one named last changes fastest.
Arguments:
- pieces: bfloat16 [1024, 7, 512], P(('dp', 'mp')), may hold values from -6 to 6
- script_tags: int32 [1024], P(('dp', 'mp')), may hold values from 0 to 15
- counts: int32 [1024], P(('dp', 'mp')), may hold values from 1 to 7
- cotangent: bfloat16 [1024, 2048], P(('dp', 'mp')), may hold values from -6 to 6
- qkv_weight: float32 [2, 3, 512, 512], P(None, None, 'dp'), may hold values from -0.25 to 0.25
- qkv_first: float32 [2, 3, 512, 512], P(None, None, 'dp'), may hold values from -0.00061035156 to 0.00061035156
- qkv_second: float32 [2, 3, 512, 512], P(None, None, 'dp'), may hold values from 1.3599255e-10 to 5.439702e-10
- out_weight: float32 [2, 512, 512], P(None, None, 'dp'), may hold values from -0.5 to 0.5
- out_first: float32 [2, 512, 512], P(None, None, 'dp'), may hold values from -0.00061035156 to 0.00061035156
- out_second: float32 [2, 512, 512], P(None, None, 'dp'), may hold values from 1.3599255e-10 to 5.439702e-10
- up_weight: float32 [2, 512, 2048], P(None, 'dp'), may hold values from -0.25 to 0.25
- up_first: float32 [2, 512, 2048], P(None, 'dp'), may hold values from -0.00061035156 to 0.00061035156
- up_second: float32 [2, 512, 2048], P(None, 'dp'), may hold values from 1.3599255e-10 to 5.439702e-10
- down_weight: float32 [2, 2048, 512], P(None, None, 'dp'), may hold values from -0.125 to 0.125
- down_first: float32 [2, 2048, 512], P(None, None, 'dp'), may hold values from -0.00061035156 to 0.00061035156
- down_second: float32 [2, 2048, 512], P(None, None, 'dp'), may hold values from 1.3599255e-10 to 5.439702e-10
- proj_weight: float32 [512, 2048], P('dp'), may hold values from -0.25 to 0.25
- proj_first: float32 [512, 2048], P('dp'), may hold values from -0.00061035156 to 0.00061035156
- proj_second: float32 [512, 2048], P('dp'), may hold values from 1.3599255e-10 to 5.439702e-10
- norm_gain: float32 [5, 512], replicated, may hold values from 0.5 to 1.5
- gain_first: float32 [5, 512], replicated, may hold values from -0.00061035156 to 0.00061035156
- gain_second: float32 [5, 512], replicated, may hold values from 1.3599255e-10 to 5.439702e-10
- norm_bias: float32 [5, 512], replicated, may hold values from -4 to 4
- bias_first: float32 [5, 512], replicated, may hold values from -0.00061035156 to 0.00061035156
- bias_second: float32 [5, 512], replicated, may hold values from 1.3599255e-10 to 5.439702e-10
- group_table: float32 [16, 512], replicated, may hold values from -6 to 6
- table_first: float32 [16, 512], replicated, may hold values from -0.00061035156 to 0.00061035156
- table_second: float32 [16, 512], replicated, may hold values from 1.3599255e-10 to 5.439702e-10
Outputs:
- embeddings: float32 [1024, 2048], P(('dp', 'mp'))
- input_grad: float32 [1024, 7, 512], P(('dp', 'mp'))
- grad_norm: float32 [], replicated
- new_qkv: float32 [2, 3, 512, 512], P(None, None, 'dp')
- new_qkv_first: float32 [2, 3, 512, 512], P(None, None, 'dp')
- new_qkv_second: float32 [2, 3, 512, 512], P(None, None, 'dp')
- new_out: float32 [2, 512, 512], P(None, None, 'dp')
- new_out_first: float32 [2, 512, 512], P(None, None, 'dp')
- new_out_second: float32 [2, 512, 512], P(None, None, 'dp')
- new_up: float32 [2, 512, 2048], P(None, 'dp')
- new_up_first: float32 [2, 512, 2048], P(None, 'dp')
- new_up_second: float32 [2, 512, 2048], P(None, 'dp')
- new_down: float32 [2, 2048, 512], P(None, None, 'dp')
- new_down_first: float32 [2, 2048, 512], P(None, None, 'dp')
- new_down_second: float32 [2, 2048, 512], P(None, None, 'dp')
- new_proj: float32 [512, 2048], P('dp')
- new_proj_first: float32 [512, 2048], P('dp')
- new_proj_second: float32 [512, 2048], P('dp')
- new_gain: float32 [5, 512], replicated
- new_gain_first: float32 [5, 512], replicated
- new_gain_second: float32 [5, 512], replicated
- new_bias: float32 [5, 512], replicated
- new_bias_first: float32 [5, 512], replicated
- new_bias_second: float32 [5, 512], replicated
- new_table: float32 [16, 512], replicated
- new_table_first: float32 [16, 512], replicated
- new_table_second: float32 [16, 512], replicated
All inputs are finite; a program needn't handle non-finite values.
Results may differ from a plain program's by a relative error of at most 0.02.
Values may be sent and summed in bfloat16 or wider, within the bound.
A program may use at most 128 MiB of HBM per device.

v0:
```python
import jax
import jax.numpy as jnp
from jax import lax
from jax.sharding import PartitionSpec as P

HD = 64
PIECES = 7
STEP = 10


norm_eps = 1e-05
beta_first = 0.9
beta_second = 0.999
adam_eps = 1e-08
learn_rate = 0.03
small_rate = 0.5
decay_rate = 0.01
clip_level = 1.0
masked_score = -1000000000.0
bfloat = jnp.bfloat16
single = jnp.float32
highest = lax.Precision.HIGHEST


def layer_norm(values, gain_row, bias_row):
    centre = jnp.mean(values, axis=-1, keepdims=True)
    offset = values - centre
    spread = jnp.mean(offset * offset, axis=-1, keepdims=True)
    return offset * lax.rsqrt(spread + norm_eps) * gain_row + bias_row


def matmul_tn(left_side, right_side):
    return lax.dot_general(
        left_side, right_side, (((0,), (0,)), ((), ())), preferred_element_type=single
    )


def matmul_nt(left_side, right_side):
    return lax.dot_general(
        left_side, right_side, (((1,), (1,)), ((), ())), preferred_element_type=single
    )


def exact_gelu(values):
    return jax.nn.gelu(values, approximate=False)


def adam_update(weight, first, second, gradient, clip_scale, decay, step_rate):
    clipped = gradient * clip_scale
    first_new = beta_first * first + (1.0 - beta_first) * clipped
    second_new = beta_second * second + (1.0 - beta_second) * clipped * clipped
    first_hat = first_new / (1.0 - beta_first**STEP)
    second_hat = second_new / (1.0 - beta_second**STEP)
    weight_new = weight - step_rate * (
        first_hat / (jnp.sqrt(second_hat) + adam_eps) + decay * weight
    )
    return (weight_new, first_new, second_new)


def split_qkv(qkv_rows, entry_count):
    heads_local = qkv_rows.shape[2] // HD
    blocks = qkv_rows.reshape(entry_count, PIECES, 3, heads_local, HD)
    return (blocks[:, :, 0], blocks[:, :, 1], blocks[:, :, 2])


def attend(qkv_rows, count_all):
    entry_count = count_all.shape[0]
    queries, keys_block, values_block = split_qkv(qkv_rows, entry_count)
    scores = jnp.einsum(
        "eqhd,ekhd->ehqk", queries, keys_block, preferred_element_type=single
    ) * HD ** (-0.5)
    keymask = jnp.arange(PIECES, dtype=jnp.int32)[None, :] < count_all[:, None]
    scores = jnp.where(keymask[:, None, None, :], scores, masked_score)
    attn_probs = jax.nn.softmax(scores, axis=-1)
    mixed_heads = jnp.einsum(
        "ehqk,ekhd->eqhd", attn_probs.astype(bfloat), values_block, preferred_element_type=single
    )
    return (attn_probs, mixed_heads.astype(bfloat).reshape(entry_count * PIECES, qkv_rows.shape[2]))


def attend_back(qkv_rows, attn_probs, grad_mixed, entry_count):
    queries, keys_block, values_block = split_qkv(qkv_rows, entry_count)
    grad_heads = grad_mixed.reshape(queries.shape)
    grad_probs = jnp.einsum(
        "eqhd,ekhd->ehqk", grad_heads, values_block, preferred_element_type=single
    )
    grad_values = jnp.einsum(
        "ehqk,eqhd->ekhd", attn_probs.astype(bfloat), grad_heads, preferred_element_type=single
    )
    grad_scores = attn_probs * (
        grad_probs - jnp.sum(grad_probs * attn_probs, axis=-1, keepdims=True)
    )
    grad_scores = grad_scores.astype(bfloat)
    grad_queries = jnp.einsum(
        "ehqk,ekhd->eqhd", grad_scores, keys_block, preferred_element_type=single
    ) * HD ** (-0.5)
    grad_keys = jnp.einsum(
        "ehqk,eqhd->ekhd", grad_scores, queries, preferred_element_type=single
    ) * HD ** (-0.5)
    stacked = jnp.stack([grad_queries, grad_keys, grad_values], axis=2)
    return stacked.astype(bfloat).reshape(entry_count * PIECES, 3, qkv_rows.shape[2])


def attention_front(stream, gain_row, bias_row, count_low, qkv_layer):
    normed = layer_norm(stream, gain_row, bias_row).astype(bfloat)
    normed_all, count_gathered = (
        lax.all_gather(normed, "mp", axis=0, tiled=True),
        lax.all_gather(count_low, "mp", axis=0, tiled=True),
    )
    count_all = count_gathered.astype(jnp.int32)
    qkv_rows = jnp.einsum(
        "rd,tdc->rtc", normed_all, qkv_layer, preferred_element_type=single
    ).astype(bfloat)
    attn_probs, mixed_heads = attend(qkv_rows, count_all)
    return (normed_all, count_all, qkv_rows, attn_probs, mixed_heads)


def attention_out(mixed_heads, out_layer):
    partial_out = jnp.dot(mixed_heads, out_layer, preferred_element_type=single)
    return lax.psum_scatter(
        partial_out.astype(jnp.bfloat16), "mp", scatter_dimension=0, tiled=True
    ).astype(jnp.float32)


def feed_front(middle, gain_row, bias_row, up_layer):
    normed = layer_norm(middle, gain_row, bias_row).astype(bfloat)
    normed_all = lax.all_gather(normed, "mp", axis=0, tiled=True)
    hidden_pre = jnp.dot(normed_all, up_layer, preferred_element_type=single)
    activated = exact_gelu(hidden_pre).astype(bfloat)
    return (normed_all, hidden_pre, activated)


def feed_out(activated, down_layer):
    partial_out = jnp.dot(activated, down_layer, preferred_element_type=single)
    return lax.psum_scatter(
        partial_out.astype(jnp.bfloat16), "mp", scatter_dimension=0, tiled=True
    ).astype(jnp.float32)


def per_device(
    pieces,
    script_tags,
    counts,
    cotangent,
    qkv_weight,
    qkv_first,
    qkv_second,
    out_weight,
    out_first,
    out_second,
    up_weight,
    up_first,
    up_second,
    down_weight,
    down_first,
    down_second,
    proj_weight,
    proj_first,
    proj_second,
    norm_gain,
    gain_first,
    gain_second,
    norm_bias,
    bias_first,
    bias_second,
    group_table,
    table_first,
    table_second,
):
    entries = pieces.shape[0]
    model_width = pieces.shape[2]
    groups = group_table.shape[0]
    layers_total = qkv_weight.shape[0]
    final_index = 2 * layers_total
    model_par = lax.axis_size("mp")
    shard_index = lax.axis_index("mp")
    head_cols = qkv_weight.shape[3] // model_par
    hidden_cols = up_weight.shape[2] // model_par
    qkv_source = lax.dynamic_slice_in_dim(qkv_weight, shard_index * head_cols, head_cols, 3)
    out_source = lax.dynamic_slice_in_dim(out_weight, shard_index * head_cols, head_cols, 1)
    up_source = lax.dynamic_slice_in_dim(up_weight, shard_index * hidden_cols, hidden_cols, 2)
    down_source = lax.dynamic_slice_in_dim(down_weight, shard_index * hidden_cols, hidden_cols, 1)
    qkv_full, out_full, up_full, down_full, proj_full = (
        lax.all_gather(qkv_source.astype(bfloat), "dp", axis=2, tiled=True),
        lax.all_gather(out_source.astype(bfloat), "dp", axis=2, tiled=True),
        lax.all_gather(up_source.astype(bfloat), "dp", axis=1, tiled=True),
        lax.all_gather(down_source.astype(bfloat), "dp", axis=2, tiled=True),
        lax.all_gather(proj_weight.astype(bfloat), "dp", axis=0, tiled=True),
    )
    onehot = (script_tags[:, None] == jnp.arange(groups, dtype=jnp.int32)[None, :]).astype(single)
    table_rows = jnp.dot(onehot, group_table, precision=highest)
    stream = (pieces.astype(single) + table_rows[:, None, :]).reshape(entries * PIECES, model_width)
    count_low = counts.astype(bfloat)
    layer_inputs = []
    for layer_index in range(layers_total):
        layer_inputs.append(stream)
        front_parts = attention_front(
            stream,
            norm_gain[2 * layer_index],
            norm_bias[2 * layer_index],
            count_low,
            qkv_full[layer_index],
        )
        middle = stream + attention_out(front_parts[4], out_full[layer_index])
        feed_parts = feed_front(
            middle,
            norm_gain[2 * layer_index + 1],
            norm_bias[2 * layer_index + 1],
            up_full[layer_index],
        )
        stream = middle + feed_out(feed_parts[2], down_full[layer_index])
    slot_mask = (jnp.arange(PIECES, dtype=jnp.int32)[None, :] < counts[:, None]).astype(single)
    count_float = counts.astype(single)

    def pool_rows(stream_rows, gain_row, bias_row):
        normed = layer_norm(stream_rows, gain_row, bias_row).reshape(entries, PIECES, model_width)
        return jnp.sum(normed * slot_mask[:, :, None], axis=1) / count_float[:, None]

    pooled, pool_pull = jax.vjp(pool_rows, stream, norm_gain[final_index], norm_bias[final_index])
    pooled_low = pooled.astype(bfloat)
    embeddings = jnp.dot(pooled_low, proj_full, preferred_element_type=single)
    grad_pooled = matmul_nt(cotangent, proj_full)
    grad_stream, gain_last, bias_last = pool_pull(grad_pooled)
    pooled_all, cotangent_all = (
        lax.all_gather(pooled_low, "mp", axis=0, tiled=True),
        lax.all_gather(cotangent, "mp", axis=0, tiled=True),
    )
    grad_proj = matmul_tn(pooled_all, cotangent_all)
    grads_qkv = [None] * layers_total
    grads_out = [None] * layers_total
    grads_up = [None] * layers_total
    grads_down = [None] * layers_total
    grads_gain = [None] * (final_index + 1)
    grads_bias = [None] * (final_index + 1)
    grads_gain[final_index] = gain_last
    grads_bias[final_index] = bias_last
    for layer_index in reversed(range(layers_total)):
        state_in = layer_inputs[layer_index]
        gain_attn = norm_gain[2 * layer_index]
        bias_attn = norm_bias[2 * layer_index]
        gain_feed = norm_gain[2 * layer_index + 1]
        bias_feed = norm_bias[2 * layer_index + 1]
        normed_all, count_all, qkv_rows, attn_probs, mixed_heads = attention_front(
            state_in, gain_attn, bias_attn, count_low, qkv_full[layer_index]
        )
        middle = state_in + attention_out(mixed_heads, out_full[layer_index])
        normed_feed, hidden_pre, activated = feed_front(
            middle, gain_feed, bias_feed, up_full[layer_index]
        )
        grad_out_low = grad_stream.astype(bfloat)
        grad_out_all = lax.all_gather(grad_out_low, "mp", axis=0, tiled=True)
        grads_down[layer_index] = matmul_tn(activated, grad_out_all)
        grad_act = matmul_nt(grad_out_all, down_full[layer_index])
        gelu_pull = jax.vjp(exact_gelu, hidden_pre)[1]
        grad_hidden = gelu_pull(grad_act)[0].astype(bfloat)
        grads_up[layer_index] = matmul_tn(normed_feed, grad_hidden)
        grad_normed_part = matmul_nt(grad_hidden, up_full[layer_index])
        grad_normed = lax.psum_scatter(
            grad_normed_part.astype(jnp.bfloat16), "mp", scatter_dimension=0, tiled=True
        ).astype(jnp.float32)
        feed_pull = jax.vjp(layer_norm, middle, gain_feed, bias_feed)[1]
        grad_mid_norm, grads_gain[2 * layer_index + 1], grads_bias[2 * layer_index + 1] = feed_pull(
            grad_normed
        )
        grad_middle = grad_stream + grad_mid_norm
        grad_mid_low = grad_middle.astype(bfloat)
        grad_mid_all = lax.all_gather(grad_mid_low, "mp", axis=0, tiled=True)
        grads_out[layer_index] = matmul_tn(mixed_heads, grad_mid_all)
        grad_mixed = matmul_nt(grad_mid_all, out_full[layer_index]).astype(bfloat)
        grad_qkv_rows = attend_back(qkv_rows, attn_probs, grad_mixed, count_all.shape[0])
        grads_qkv[layer_index] = jnp.einsum(
            "rd,rtc->tdc", normed_all, grad_qkv_rows, preferred_element_type=single
        )
        grad_attn_part = jnp.einsum(
            "rtc,tdc->rd", grad_qkv_rows, qkv_full[layer_index], preferred_element_type=single
        )
        grad_attn = lax.psum_scatter(
            grad_attn_part.astype(jnp.bfloat16), "mp", scatter_dimension=0, tiled=True
        ).astype(jnp.float32)
        attn_pull = jax.vjp(layer_norm, state_in, gain_attn, bias_attn)[1]
        grad_state_norm, grads_gain[2 * layer_index], grads_bias[2 * layer_index] = attn_pull(
            grad_attn
        )
        grad_stream = grad_middle + grad_state_norm
    grad_entries = grad_stream.reshape(entries, PIECES, model_width)
    grad_table = lax.dot_general(
        onehot, jnp.sum(grad_entries, axis=1), (((0,), (0,)), ((), ())), precision=highest
    )
    grad_gain = jnp.stack(grads_gain, axis=0)
    grad_bias = jnp.stack(grads_bias, axis=0)
    reduced_qkv, reduced_out, reduced_up, reduced_down, reduced_proj = (
        lax.psum_scatter(jnp.stack(grads_qkv, axis=0), "dp", scatter_dimension=2, tiled=True),
        lax.psum_scatter(jnp.stack(grads_out, axis=0), "dp", scatter_dimension=2, tiled=True),
        lax.psum_scatter(jnp.stack(grads_up, axis=0), "dp", scatter_dimension=1, tiled=True),
        lax.psum_scatter(jnp.stack(grads_down, axis=0), "dp", scatter_dimension=2, tiled=True),
        lax.psum_scatter(grad_proj, "dp", scatter_dimension=0, tiled=True),
    )
    proj_cols = reduced_proj.shape[1] // model_par
    proj_share = lax.dynamic_slice_in_dim(reduced_proj, shard_index * proj_cols, proj_cols, 1)
    square_sum = (
        jnp.sum(reduced_qkv * reduced_qkv)
        + jnp.sum(reduced_out * reduced_out)
        + jnp.sum(reduced_up * reduced_up)
        + jnp.sum(reduced_down * reduced_down)
        + jnp.sum(proj_share * proj_share)
    )
    full_qkv, full_out, full_up, full_down = (
        lax.all_gather(reduced_qkv.astype(jnp.bfloat16), "mp", axis=3, tiled=True).astype(
            reduced_qkv.dtype
        ),
        lax.all_gather(reduced_out.astype(jnp.bfloat16), "mp", axis=1, tiled=True).astype(
            reduced_out.dtype
        ),
        lax.all_gather(reduced_up.astype(jnp.bfloat16), "mp", axis=2, tiled=True).astype(
            reduced_up.dtype
        ),
        lax.all_gather(reduced_down.astype(jnp.bfloat16), "mp", axis=1, tiled=True).astype(
            reduced_down.dtype
        ),
    )
    gain_total, bias_total, table_total, square_total = lax.psum(
        (grad_gain, grad_bias, grad_table, square_sum), ("dp", "mp")
    )
    grad_norm = jnp.sqrt(
        square_total
        + jnp.sum(gain_total * gain_total)
        + jnp.sum(bias_total * bias_total)
        + jnp.sum(table_total * table_total)
    )
    clip_scale = jnp.minimum(1.0, clip_level / (grad_norm + 1e-06))
    new_qkv = adam_update(
        qkv_weight, qkv_first, qkv_second, full_qkv, clip_scale, decay_rate, learn_rate
    )
    new_out = adam_update(
        out_weight, out_first, out_second, full_out, clip_scale, decay_rate, learn_rate
    )
    new_up = adam_update(
        up_weight, up_first, up_second, full_up, clip_scale, decay_rate, learn_rate
    )
    new_down = adam_update(
        down_weight, down_first, down_second, full_down, clip_scale, decay_rate, learn_rate
    )
    new_proj = adam_update(
        proj_weight, proj_first, proj_second, reduced_proj, clip_scale, decay_rate, learn_rate
    )
    new_gain = adam_update(
        norm_gain, gain_first, gain_second, gain_total, clip_scale, 0.0, small_rate
    )
    new_bias = adam_update(
        norm_bias, bias_first, bias_second, bias_total, clip_scale, 0.0, small_rate
    )
    new_table = adam_update(
        group_table, table_first, table_second, table_total, clip_scale, 0.0, small_rate
    )
    return (
        embeddings,
        grad_entries,
        grad_norm,
        new_qkv[0],
        new_qkv[1],
        new_qkv[2],
        new_out[0],
        new_out[1],
        new_out[2],
        new_up[0],
        new_up[1],
        new_up[2],
        new_down[0],
        new_down[1],
        new_down[2],
        new_proj[0],
        new_proj[1],
        new_proj[2],
        new_gain[0],
        new_gain[1],
        new_gain[2],
        new_bias[0],
        new_bias[1],
        new_bias[2],
        new_table[0],
        new_table[1],
        new_table[2],
    )


def solution(mesh):
    return jax.shard_map(
        per_device,
        mesh=mesh,
        in_specs=(
            P(("dp", "mp"), None, None),
            P(("dp", "mp")),
            P(("dp", "mp")),
            P(("dp", "mp"), None),
            P(None, None, "dp", None),
            P(None, None, "dp", None),
            P(None, None, "dp", None),
            P(None, None, "dp"),
            P(None, None, "dp"),
            P(None, None, "dp"),
            P(None, "dp", None),
            P(None, "dp", None),
            P(None, "dp", None),
            P(None, None, "dp"),
            P(None, None, "dp"),
            P(None, None, "dp"),
            P("dp", None),
            P("dp", None),
            P("dp", None),
            P(),
            P(),
            P(),
            P(),
            P(),
            P(),
            P(),
            P(),
            P(),
        ),
        out_specs=(
            P(("dp", "mp"), None),
            P(("dp", "mp"), None, None),
            P(),
            P(None, None, "dp", None),
            P(None, None, "dp", None),
            P(None, None, "dp", None),
            P(None, None, "dp"),
            P(None, None, "dp"),
            P(None, None, "dp"),
            P(None, "dp", None),
            P(None, "dp", None),
            P(None, "dp", None),
            P(None, None, "dp"),
            P(None, None, "dp"),
            P(None, None, "dp"),
            P("dp", None),
            P("dp", None),
            P("dp", None),
            P(),
            P(),
            P(),
            P(),
            P(),
            P(),
            P(),
            P(),
            P(),
        ),
        check_vma=False,
    )
```

profile of v0, /device:TPU:0, one launch (start us, length us, event | category | flops | bytes accessed | tf_op | source)
XLA Modules:
  0.0 886.2 jit_solution(8003821247950941970)
XLA Ops:
  15.3 10.8 %all_gather.67 = bf16[896,512]{1,0:T(8,128)(2,1)S(1)} all-gather(bf16[224,512]{1,0:T(8,128)(2,1)S(1)} %add_convert_fusion.5), channel_id=1, replica_groups=mesh['dp'=8,'mp'=4] {'mp'}, dimensions={0}, use_global_device_ids=true | all-gather | bytes 1146880 | tf_op jit(solution)/shard_map/all_gather | solution.py:107
  27.2 32.2 %all_gather.68 = bf16[2,3,512,128]{3,2,1,0:T(8,128)(2,1)S(1)} all-gather(bf16[2,3,64,128]{3,2,1,0:T(8,128)(2,1)S(1)} %dynamic-slice_convert_fusion.2), channel_id=1, replica_groups=mesh['dp'=8,'mp'=4] {'dp'}, dimensions={2}, use_global_device_ids=true | all-gather | bytes 884736 | tf_op jit(solution)/shard_map/all_gather | solution.py:184
  65.0 5.6 all-reduce
  76.1 30.7 %all_gather.70 = bf16[2,128,512]{1,2,0:T(8,128)(2,1)S(1)} all-gather(bf16[2,128,64]{1,2,0:T(8,128)(2,1)S(1)} %dynamic-slice_convert_fusion.3), channel_id=1, replica_groups=mesh['dp'=8,'mp'=4] {'dp'}, dimensions={2}, use_global_device_ids=true | all-gather | bytes 294912 | tf_op jit(solution)/shard_map/all_gather | solution.py:185
  111.7 21.6 %reduce-scatter.11.cloned.1.call-done = bf16[224,512]{1,0:T(8,128)(2,1)} async-done(((bf16[896,512]{1,0:T(8,128)(2,1)}), bf16[224,512]{1,0:T(8,128)(2,1)}) %reduce-scatter.11.cloned.1.call-update) | async-done | bytes 229392 | tf_op jit(solution)/shard_map/reduce_scatter | solution.py:120
  134.7 8.9 %all_gather.71 = bf16[896,512]{1,0:T(8,128)(2,1)S(1)} all-gather(bf16[224,512]{1,0:T(8,128)(2,1)S(1)} %add_convert_fusion.4), channel_id=1, replica_groups=mesh['dp'=8,'mp'=4] {'mp'}, dimensions={0}, use_global_device_ids=true | all-gather | bytes 1146880 | tf_op jit(solution)/shard_map/all_gather | solution.py:127
  143.6 9.0 %all-gather.4.cloned.1.call-done = bf16[2,512,512]{2,1,0:T(8,128)(2,1)} async-done(((bf16[2,64,512]{2,1,0:T(8,128)(2,1)}), bf16[2,512,512]{2,1,0:T(8,128)(2,1)}) %all-gather.4.cloned.1.call-update) | async-done | bytes 1048592 | tf_op jit(solution)/shard_map/all_gather | solution.py:186
  152.6 6.8 multiply_convert_fusion.1
  159.4 34.8 %all-gather.6.cloned.1.call-done = bf16[2,512,512]{1,2,0:T(8,128)(2,1)} async-done(((bf16[2,512,64]{1,2,0:T(8,128)(2,1)}), bf16[2,512,512]{1,2,0:T(8,128)(2,1)}) %all-gather.6.cloned.1.call-update) | async-done | bytes 1048592 | tf_op jit(solution)/shard_map/all_gather | solution.py:187
  194.2 2.9 convolution_convert_fusion.5
  197.2 22.7 %reduce-scatter.13.cloned.1.call-done = bf16[224,512]{1,0:T(8,128)(2,1)} async-done(((bf16[896,512]{1,0:T(8,128)(2,1)}), bf16[224,512]{1,0:T(8,128)(2,1)}) %reduce-scatter.13.cloned.1.call-update) | async-done | bytes 229392 | tf_op jit(solution)/shard_map/reduce_scatter | solution.py:135
  221.3 9.4 %all_gather.74 = bf16[896,512]{1,0:T(8,128)(2,1)S(1)} all-gather(bf16[224,512]{1,0:T(8,128)(2,1)S(1)} %add_convert_fusion.3), channel_id=1, replica_groups=mesh['dp'=8,'mp'=4] {'mp'}, dimensions={0}, use_global_device_ids=true | all-gather | bytes 1146880 | tf_op jit(solution)/shard_map/all_gather | solution.py:107
  233.1 2.9 reshape.361
  236.0 1.9 fusion.106
  237.9 2.1 fusion.113
  245.3 23.8 %reduce-scatter.15.cloned.1.call-done = bf16[224,512]{1,0:T(8,128)(2,1)} async-done(((bf16[896,512]{1,0:T(8,128)(2,1)}), bf16[224,512]{1,0:T(8,128)(2,1)}) %reduce-scatter.15.cloned.1.call-update) | async-done | bytes 229392 | tf_op jit(solution)/shard_map/reduce_scatter | solution.py:120
  270.6 8.9 %all_gather.75 = bf16[896,512]{1,0:T(8,128)(2,1)S(1)} all-gather(bf16[224,512]{1,0:T(8,128)(2,1)S(1)} %add_convert_fusion.2), channel_id=1, replica_groups=mesh['dp'=8,'mp'=4] {'mp'}, dimensions={0}, use_global_device_ids=true | all-gather | bytes 1146880 | tf_op jit(solution)/shard_map/all_gather | solution.py:127
  279.5 7.0 multiply_convert_fusion
  289.3 7.9 all-gather.8.cloned.1.call-done
  297.3 2.4 convolution_divide_fusion
  301.6 12.1 %reduce-scatter.17.cloned.1.call-done = bf16[224,512]{1,0:T(8,128)(2,1)} async-done(((bf16[896,512]{1,0:T(8,128)(2,1)}), bf16[224,512]{1,0:T(8,128)(2,1)}) %reduce-scatter.17.cloned.1.call-update) | async-done | bytes 229392 | tf_op jit(solution)/shard_map/reduce_scatter | solution.py:135
  315.8 1.9 fusion.99
  317.8 9.1 %all_gather.77 = bf16[896,512]{1,0:T(8,128)(2,1)S(1)} all-gather(bf16[224,512]{1,0:T(8,128)(2,1)S(1)} %add_convert_fusion.6), channel_id=1, replica_groups=mesh['dp'=8,'mp'=4] {'mp'}, dimensions={0}, use_global_device_ids=true | all-gather | bytes 1146880 | tf_op jit(solution)/shard_map/all_gather | solution.py:251
  330.7 24.6 %reduce-scatter.19.cloned.1.call-done = bf16[224,512]{1,0:T(8,128)(2,1)} async-done(((bf16[896,512]{1,0:T(8,128)(2,1)}), bf16[224,512]{1,0:T(8,128)(2,1)}) %reduce-scatter.19.cloned.1.call-update) | async-done | bytes 229392 | tf_op jit(solution)/shard_map/reduce_scatter | solution.py:258
  357.0 1.8 fusion.62
  360.0 8.9 %all_gather.78 = bf16[896,512]{1,0:T(8,128)(2,1)S(1)} all-gather(bf16[224,512]{1,0:T(8,128)(2,1)S(1)} %get-tuple-element.195), channel_id=1, replica_groups=mesh['dp'=8,'mp'=4] {'mp'}, dimensions={0}, use_global_device_ids=true | all-gather | bytes 1146880 | tf_op jit(solution)/shard_map/all_gather | solution.py:267
  370.1 1.9 reshape.364
  372.0 2.3 multiply_reduce_fusion.1
  380.6 2.2 copy.210
  382.7 2.0 stack.77
  384.7 2.2 copy.212
  386.9 2.0 stack.78
  390.8 2.8 bitcast_convert_fusion.1
  393.7 24.5 %reduce-scatter.21.cloned.1.call-done = bf16[224,512]{1,0:T(8,128)(2,1)} async-done(((bf16[896,512]{1,0:T(8,128)(2,1)}), bf16[224,512]{1,0:T(8,128)(2,1)}) %reduce-scatter.21.cloned.1.call-update) | async-done | bytes 229392 | tf_op jit(solution)/shard_map/reduce_scatter | solution.py:277
  420.9 8.9 %all_gather.79 = bf16[896,512]{1,0:T(8,128)(2,1)S(1)} all-gather(bf16[224,512]{1,0:T(8,128)(2,1)S(1)} %fusion.72), channel_id=1, replica_groups=mesh['dp'=8,'mp'=4] {'mp'}, dimensions={0}, use_global_device_ids=true | all-gather | bytes 1146880 | tf_op jit(solution)/shard_map/all_gather | solution.py:251
  429.9 3.0 add_convert_fusion
  435.5 24.6 %reduce-scatter.23.cloned.1.call-done = bf16[224,512]{1,0:T(8,128)(2,1)} async-done(((bf16[896,512]{1,0:T(8,128)(2,1)}), bf16[224,512]{1,0:T(8,128)(2,1)}) %reduce-scatter.23.cloned.1.call-update) | async-done | bytes 229392 | tf_op jit(solution)/shard_map/reduce_scatter | solution.py:258
  461.2 1.8 fusion.64
  463.0 2.0 fusion.96
  465.0 9.3 %all_gather.80 = bf16[896,512]{1,0:T(8,128)(2,1)S(1)} all-gather(bf16[224,512]{1,0:T(8,128)(2,1)S(1)} %get-tuple-element.191), channel_id=1, replica_groups=mesh['dp'=8,'mp'=4] {'mp'}, dimensions={0}, use_global_device_ids=true | all-gather | bytes 1146880 | tf_op jit(solution)/shard_map/all_gather | solution.py:267
  475.4 1.9 reshape.365
  477.3 1.9 multiply_reduce_fusion
  484.0 2.0 stack.80
  488.0 2.0 stack.81
  494.3 2.8 bitcast_convert_fusion
  497.2 2.3 convolution_bitcast_fusion.2
  502.8 7.3 all_gather.82
  511.5 5.6 all_gather.81
  517.1 2.7 fusion.115
  520.2 2.3 convolution_bitcast_fusion
  525.9 2.5 copy.223
  528.4 2.1 convolution_bitcast_fusion.5
  530.7 2.2 copy.221
  542.9 107.1 %reduce-scatter.27.cloned.1.call-done = f32[2,64,512]{2,1,0:T(8,128)} async-done(((f32[2,512,512]{2,1,0:T(8,128)}), f32[2,64,512]{2,1,0:T(8,128)}) %reduce-scatter.27.cloned.1.call-update) | async-done | bytes 262160 | tf_op jit(solution)/shard_map/reduce_scatter | solution.py:294
  651.7 130.5 %reduce-scatter.29.cloned.1.call-done = f32[64,2048]{1,0:T(8,128)} async-done(((f32[512,2048]{1,0:T(8,128)}), f32[64,2048]{1,0:T(8,128)}) %reduce-scatter.29.cloned.1.call-update) | async-done | bytes 524304 | tf_op jit(solution)/shard_map/reduce_scatter | solution.py:296
  783.7 1.9 multiply_reduce_fusion.13
  787.1 1.8 multiply_reduce_fusion.11
  792.2 7.1 all_gather.85
  799.3 40.8 %all-reduce.4 = (f32[]{:T(128)}, f32[5,512]{1,0:T(8,128)S(1)}, f32[5,512]{1,0:T(8,128)S(1)}, f32[16,512]{1,0:T(8,128)S(1)}) all-reduce(f32[]{:T(128)S(6)} %add.380, f32[5,512]{1,0:T(8,128)S(1)} %stack.96, f32[5,512]{1,0:T(8,128)S(1)} %stack.97, f32[16,512]{1,0:T(8,128)S(1)} %fusion.76), channel_id=1, replica_groups=mesh['dp'=8,'mp'=4] {'dp','mp'}, use_global_device_ids=true, to_apply=%region_45.46 | all-reduce | flops 13313 | bytes 106504 | tf_op jit(solution)/shard_map/psum | solution.py:321
  844.7 7.2 all_gather.83
  851.9 5.4 all_gather.84
  857.4 7.3 all_gather.86
  869.6 2.2 multiply_subtract_fusion.1
  872.7 2.2 multiply_subtract_fusion
  (390 shorter events, 108.9 us)
Async XLA Ops:
  8.0 5.0 copy-start.64
  8.0 5.6 copy-start.66
  8.1 125.2 %reduce-scatter.11.cloned.1.call-start = ((), (), s32[]{:S(2)}) async-start(), calls=%async_computation.10 | async-start | bytes 1146880 | tf_op jit(solution)/shard_map/reduce_scatter | solution.py:120
  26.0 33.4 %copy-start.4 = (bf16[896,512]{1,0:T(8,128)(2,1)}, bf16[896,512]{1,0:T(8,128)(2,1)S(1)}, u32[]{:S(2)}) copy-start(bf16[896,512]{1,0:T(8,128)(2,1)S(1)} %all_gather.67) | copy-start | bytes 2752516
  59.4 171.3 %copy-start.8 = (bf16[2,3,512,128]{3,2,1,0:T(8,128)(2,1)}, bf16[2,3,512,128]{3,2,1,0:T(8,128)(2,1)S(1)}, u32[]{:S(2)}) copy-start(bf16[2,3,512,128]{3,2,1,0:T(8,128)(2,1)S(1)} %all_gather.68) | copy-start | bytes 2359300
  62.3 9.7 %copy-start.11 = (bf16[128,7,1,2,64]{4,3,1,0,2:T(2,128)(2,1)}, bf16[128,7,1,2,64]{4,3,1,0,2:T(2,128)(2,1)S(1)}, u32[]{:S(2)}) copy-start(bf16[128,7,1,2,64]{4,3,1,0,2:T(2,128)(2,1)S(1)} %get-tuple-element.215) | copy-start | bytes 688132
  62.3 9.7 %copy-start.13 = (bf16[128,7,1,2,64]{4,3,1,0,2:T(2,128)(2,1)}, bf16[128,7,1,2,64]{4,3,1,0,2:T(2,128)(2,1)S(1)}, u32[]{:S(2)}) copy-start(bf16[128,7,1,2,64]{4,3,1,0,2:T(2,128)(2,1)S(1)} %get-tuple-element.214) | copy-start | bytes 688132
  75.2 36.5 %copy-start.18 = (bf16[896,128]{1,0:T(8,128)(2,1)}, bf16[896,128]{1,0:T(8,128)(2,1)S(1)}, u32[]{:S(2)}) copy-start(bf16[896,128]{1,0:T(8,128)(2,1)S(1)} %reshape.360) | copy-start | bytes 688132
  106.8 262.1 %copy-start.9 = (bf16[2,128,512]{1,2,0:T(8,128)(2,1)}, bf16[2,128,512]{1,2,0:T(8,128)(2,1)S(1)}, u32[]{:S(2)}) copy-start(bf16[2,128,512]{1,2,0:T(8,128)(2,1)S(1)} %all_gather.70) | copy-start | bytes 786436
  108.2 26.4 %copy-start.85 = (f32[1,512]{1,0:T(1,128)S(1)}, f32[1,512]{1,0:T(1,128)}, u32[]{:S(2)}) copy-start(f32[1,512]{1,0:T(1,128)} %get-tuple-element.230) | copy-start | bytes 6148
  108.2 44.5 %all-gather.4.cloned.1.call-start = ((), (), s32[]{:S(2)}) async-start(), calls=%async_computation.11 | async-start | bytes 1179648 | tf_op jit(solution)/shard_map/all_gather | solution.py:186
  109.9 84.3 %all-gather.6.cloned.1.call-start = ((), (), s32[]{:S(2)}) async-start(), calls=%async_computation.12 | async-start | bytes 1179648 | tf_op jit(solution)/shard_map/all_gather | solution.py:187
  111.6 108.3 %reduce-scatter.13.cloned.1.call-start = ((), (), s32[]{:S(2)}) async-start(), calls=%async_computation.13 | async-start | bytes 1146880 | tf_op jit(solution)/shard_map/reduce_scatter | solution.py:135
  143.6 15.8 %copy-start.36 = (bf16[896,512]{1,0:T(8,128)(2,1)}, bf16[896,512]{1,0:T(8,128)(2,1)S(1)}, u32[]{:S(2)}) copy-start(bf16[896,512]{1,0:T(8,128)(2,1)S(1)} %all_gather.71) | copy-start | bytes 2752516
  197.1 24.0 %copy-start.84 = (f32[1,512]{1,0:T(1,128)S(1)}, f32[1,512]{1,0:T(1,128)}, u32[]{:S(2)}) copy-start(f32[1,512]{1,0:T(1,128)} %get-tuple-element.229) | copy-start | bytes 6148
  197.1 72.0 %reduce-scatter.15.cloned.1.call-start = ((), (), s32[]{:S(2)}) async-start(), calls=%async_computation.14 | async-start | bytes 1146880 | tf_op jit(solution)/shard_map/reduce_scatter | solution.py:120
  243.1 27.1 %copy-start.20 = (bf16[896,128]{1,0:T(8,128)(2,1)}, bf16[896,128]{1,0:T(8,128)(2,1)S(1)}, u32[]{:S(2)}) copy-start(bf16[896,128]{1,0:T(8,128)(2,1)S(1)} %reshape.362) | copy-start | bytes 688132
  244.4 26.0 %copy-start.83 = (f32[1,512]{1,0:T(1,128)S(1)}, f32[1,512]{1,0:T(1,128)}, u32[]{:S(2)}) copy-start(f32[1,512]{1,0:T(1,128)} %get-tuple-element.228) | copy-start | bytes 6148
  244.5 52.8 %all-gather.8.cloned.1.call-start = ((), (), s32[]{:S(2)}) async-start(), calls=%async_computation.16 | async-start | bytes 2359296 | tf_op jit(solution)/shard_map/all_gather | solution.py:188
  245.3 68.4 %reduce-scatter.17.cloned.1.call-start = ((), (), s32[]{:S(2)}) async-start(), calls=%async_computation.15 | async-start | bytes 1146880 | tf_op jit(solution)/shard_map/reduce_scatter | solution.py:135
  270.4 16.1 %copy-start.79 = (f32[224]{0:T(256)}, f32[224]{0:T(256)S(1)}, u32[]{:S(2)}) copy-start(f32[224]{0:T(256)S(1)} %multiply_reduce_fusion.7) | copy-start | bytes 2692
  279.5 7.0 copy-start.38
  279.5 7.9 copy-start.96
  286.5 10.7 %copy-start.91 = (f32[32]{0:T(128)S(1)}, f32[32]{0:T(128)}, u32[]{:S(2)}) copy-start(f32[32]{0:T(128)} %get-tuple-element.233) | copy-start | bytes 388
  287.5 9.8 %copy-start.47 = (bf16[32,2048]{1,0:T(8,128)(2,1)S(1)}, bf16[32,2048]{1,0:T(8,128)(2,1)}, u32[]{:S(2)}) copy-start(bf16[32,2048]{1,0:T(8,128)(2,1)} %param.31) | copy-start | bytes 393220
  289.1 66.2 %reduce-scatter.19.cloned.1.call-start = ((), (), s32[]{:S(2)}) async-start(), calls=%async_computation.17 | async-start | bytes 1146880 | tf_op jit(solution)/shard_map/reduce_scatter | solution.py:258
  299.6 16.1 %copy-start.45 = (f32[32,512]{1,0:T(8,128)}, f32[32,512]{1,0:T(8,128)S(1)}, u32[]{:S(2)}) copy-start(f32[32,512]{1,0:T(8,128)S(1)} %convolution_divide_fusion) | copy-start | bytes 196612
  299.7 15.3 %copy-start.70 = (f32[1,512]{1,0:T(1,128)S(1)}, f32[1,512]{1,0:T(1,128)}, u32[]{:S(2)}) copy-start(f32[1,512]{1,0:T(1,128)} %get-tuple-element.222) | copy-start | bytes 6148
  314.8 12.2 %copy-start.107 = (f32[896,512]{1,0:T(8,128)S(1)}, f32[896,512]{1,0:T(8,128)}, u32[]{:S(2)}) copy-start(f32[896,512]{1,0:T(8,128)} %get-tuple-element.239) | copy-start | bytes 5505028
  315.8 11.1 %copy-start.97 = (bf16[2,512,512]{1,2,0:T(8,128)(2,1)S(1)}, bf16[2,512,512]{1,2,0:T(8,128)(2,1)}, u32[]{:S(2)}) copy-start(bf16[2,512,512]{1,2,0:T(8,128)(2,1)} %all-gather.6.cloned.1.call-done) | copy-start | bytes 3145732
  315.8 11.1 %copy-start.106 = (f32[896,512]{1,0:T(8,128)S(1)}, f32[896,512]{1,0:T(8,128)}, u32[]{:S(2)}) copy-start(f32[896,512]{1,0:T(8,128)} %get-tuple-element.202) | copy-start | bytes 5505028
  329.1 28.0 %copy-start.80 = (f32[224]{0:T(256)S(1)}, f32[224]{0:T(256)}, u32[]{:S(2)}) copy-start(f32[224]{0:T(256)} %copy-done.79) | copy-start | bytes 2692
  330.7 87.6 %reduce-scatter.21.cloned.1.call-start = ((), (), s32[]{:S(2)}) async-start(), calls=%async_computation.18 | async-start | bytes 1146880 | tf_op jit(solution)/shard_map/reduce_scatter | solution.py:277
  390.8 28.6 %copy-start.1 = (bf16[896,3,128]{2,0,1:T(8,128)(2,1)}, bf16[896,3,128]{2,0,1:T(8,128)(2,1)S(1)}, u32[]{:S(2)}) copy-start(bf16[896,3,128]{2,0,1:T(8,128)(2,1)S(1)} %constant_dynamic-update-slice_fusion) | copy-start | bytes 2064388
  393.7 66.4 %reduce-scatter.23.cloned.1.call-start = ((), (), s32[]{:S(2)}) async-start(), calls=%async_computation.19 | async-start | bytes 1146880 | tf_op jit(solution)/shard_map/reduce_scatter | solution.py:258
  419.4 10.4 %copy-start.98 = (bf16[2,512,512]{1,2,0:T(8,128)(2,1)S(1)}, bf16[2,512,512]{1,2,0:T(8,128)(2,1)}, u32[]{:S(2)}) copy-start(bf16[2,512,512]{1,2,0:T(8,128)(2,1)} %all-gather.6.cloned.1.call-done) | copy-start | bytes 3145732
  419.4 10.4 %copy-start.105 = (f32[896,512]{1,0:T(8,128)S(1)}, f32[896,512]{1,0:T(8,128)}, u32[]{:S(2)}) copy-start(f32[896,512]{1,0:T(8,128)} %get-tuple-element.208) | copy-start | bytes 5505028
  429.8 3.0 copy-start.40
  429.9 4.0 copy-start.95
  435.4 102.0 %reduce-scatter.25.cloned.1.call-start = ((), (), s32[]{:S(2)}) async-start(), calls=%async_computation.20 | async-start | bytes 1146880 | tf_op jit(solution)/shard_map/reduce_scatter | solution.py:277
  463.0 11.3 %copy-start.10 = (bf16[2,128,512]{1,2,0:T(8,128)(2,1)S(1)}, bf16[2,128,512]{1,2,0:T(8,128)(2,1)}, u32[]{:S(2)}) copy-start(bf16[2,128,512]{1,2,0:T(8,128)(2,1)} %copy-done.9) | copy-start | bytes 786436
  465.0 12.3 %copy-start.30 = (f32[128,2,7,7]{2,3,1,0:T(8,128)S(1)}, f32[128,2,7,7]{2,3,1,0:T(8,128)}, u32[]{:S(2)}) copy-start(f32[128,2,7,7]{2,3,1,0:T(8,128)} %copy-done.29) | copy-start | bytes 150532
  465.0 12.3 %copy-start.57 = (f32[128,2,7]{2,1,0:T(2,128)S(1)}, f32[128,2,7]{2,1,0:T(2,128)}, u32[]{:S(2)}) copy-start(f32[128,2,7]{2,1,0:T(2,128)} %copy-done.56) | copy-start | bytes 21508
  494.3 5.3 copy-start.3
  497.2 152.8 %reduce-scatter.27.cloned.1.call-start = ((), (), s32[]{:S(2)}) async-start(), calls=%async_computation.21 | async-start | bytes 2359296 | tf_op jit(solution)/shard_map/reduce_scatter | solution.py:294
  501.9 9.3 %copy-start.46 = (f32[32,512]{1,0:T(8,128)S(1)}, f32[32,512]{1,0:T(8,128)}, u32[]{:S(2)}) copy-start(f32[32,512]{1,0:T(8,128)} %copy-done.45) | copy-start | bytes 196612
  501.9 9.6 %copy-start.92 = (f32[32]{0:T(128)S(1)}, f32[32]{0:T(128)}, u32[]{:S(2)}) copy-start(f32[32]{0:T(128)} %get-tuple-element.233) | copy-start | bytes 388
  501.9 280.3 %reduce-scatter.29.cloned.1.call-start = ((), (), s32[]{:S(2)}) async-start(), calls=%async_computation.22 | async-start | bytes 4718592 | tf_op jit(solution)/shard_map/reduce_scatter | solution.py:296
  519.8 3.7 copy-start.2
  519.9 263.9 %all-reduce.8.cloned.1.call-start = ((), (), s32[]{:S(2)}) async-start(), calls=%async_computation.23 | async-start | bytes 8388608
  520.2 3.4 copy-start.6
  534.4 3.1 copy-start.69
  534.4 4.2 copy-start.82
  534.4 4.2 copy-start.72
  536.2 3.6 copy-start.22
  651.7 213.0 %copy-start.61 = (f32[16,512]{1,0:T(8,128)S(1)}, f32[16,512]{1,0:T(8,128)}, u32[]{:S(2)}) copy-start(f32[16,512]{1,0:T(8,128)} %param.53) | copy-start | bytes 98308
  783.7 82.4 %copy-start.35 = (f32[2,3,64,512]{3,2,1,0:T(8,128)S(1)}, f32[2,3,64,512]{3,2,1,0:T(8,128)}, u32[]{:S(2)}) copy-start(f32[2,3,64,512]{3,2,1,0:T(8,128)} %param.32) | copy-start | bytes 2359300
  783.7 82.4 %copy-start.43 = (f32[2,3,64,512]{3,2,1,0:T(8,128)S(1)}, f32[2,3,64,512]{3,2,1,0:T(8,128)}, u32[]{:S(2)}) copy-start(f32[2,3,64,512]{3,2,1,0:T(8,128)} %param.33) | copy-start | bytes 2359300
  783.7 82.4 %copy-start.44 = (f32[2,3,64,512]{3,2,1,0:T(8,128)S(1)}, f32[2,3,64,512]{3,2,1,0:T(8,128)}, u32[]{:S(2)}) copy-start(f32[2,3,64,512]{3,2,1,0:T(8,128)} %param.34) | copy-start | bytes 2359300
  840.1 4.5 copy-start.62
  869.6 3.0 copy-start.28
  872.6 3.0 copy-start.17
  872.6 3.0 copy-start.42
  872.7 3.0 copy-start.49
  (58 other events, 108.9 us)
Sparse Core Ops, SparseCore 0:
  108.3 24.9 reduce-scatter.10
  197.3 22.5 reduce-scatter.12
  244.6 24.4 reduce-scatter.14
  289.2 24.4 reduce-scatter.16
  330.8 24.4 reduce-scatter.18
  393.8 24.4 reduce-scatter.20
  435.5 24.4 reduce-scatter.22
  497.3 24.6 reduce-scatter.24
  525.5 124.4 reduce-scatter.26
  653.5 128.6 reduce-scatter.28
Sparse Core Ops, SparseCore 1:
  111.4 41.2 all-gather.3
  155.3 38.9 all-gather.5
  247.6 49.6 all-gather.7
  534.4 182.0 all-reduce.7
where the time goes:
time: 895 us; the launch traced here: 886 us
  waiting for transfers between devices  443 us (49%)
  blocking collectives  224 us (25%)
  matrix products  72.3 us (8%)
  local copies, waits for them, and re-layouts  67.2 us (8%)
  other arithmetic  53 us (6%)
  between operations  26.1 us (3%)
    reduce_scatter x1, waiting for transfers between devices, per_device(): lax.psum_scatter(grad_proj, 'dp', scatter_dimension=0, tiled=True)  130 us
    reduce_scatter x1, waiting for transfers between devices, per_device(): lax.psum_scatter(jnp.stack(grads_up, axis=0), 'dp', scatter_dimension=1,...  107 us
    reduce_scatter x2, waiting for transfers between devices, per_device(): lax.psum_scatter(grad_normed_part.astype(jnp.bfloat16), 'mp', scatter_dim...  49.1 us
    reduce_scatter x2, waiting for transfers between devices, attention_out(): lax.psum_scatter(partial_out.astype(jnp.bfloat16), 'mp', scatter_dimensio...  45.4 us
    psum x1, blocking collectives, per_device(): lax.psum((grad_gain, grad_bias, grad_table, square_sum), ('dp', 'mp'))  40.8 us
    all_gather x1, waiting for transfers between devices, per_device(): lax.all_gather(down_source.astype(bfloat), 'dp', axis=2, tiled=True)  34.8 us
    reduce_scatter x2, waiting for transfers between devices, feed_out(): lax.psum_scatter(partial_out.astype(jnp.bfloat16), 'mp', scatter_dimensio...  34.7 us
    all_gather x1, blocking collectives, per_device(): lax.all_gather(qkv_source.astype(bfloat), 'dp', axis=2, tiled=True)  32.2 us
  transfers between devices with their start and end apart: 14, of which 12 were waited for; matrix products, arithmetic and copies ran while one was open for 7% of the time, Pallas kernels for 0%

commit v1 on v0

v1 whole, which is shorter than its diff:
```python
import functools
import math

import jax
import jax.numpy as jnp
from jax import lax
from jax.experimental import pallas as pl
from jax.experimental.pallas import tpu as pltpu
from jax.sharding import PartitionSpec as P

HD = 64
PIECES = 7
SLOTS = 8
STEP = 10
BLOCKS = 4
SMALL_ROWS = 32

norm_eps = 1e-05
beta_first = 0.9
beta_second = 0.999
adam_eps = 1e-08
learn_rate = 0.03
small_rate = 0.5
decay_rate = 0.01
clip_level = 1.0
masked_score = -1000000000.0
bfloat = jnp.bfloat16
single = jnp.float32
highest = lax.Precision.HIGHEST
MESH = pl.DeviceIdType.MESH
VMEM = pltpu.VMEM


def place():
    along, across = lax.axis_index("dp"), lax.axis_index("mp")
    return lax.div(along, 2), lax.rem(along, 2), lax.div(across, 2), lax.rem(across, 2)


def device(z, y, x, c):
    return (z * 2 + y, x * 2 + c)


def remote(src, dst, send_sem, recv_sem, target):
    return pltpu.make_async_remote_copy(
        src_ref=src, dst_ref=dst, send_sem=send_sem, recv_sem=recv_sem, device_id=target, device_id_type=MESH
    )


def await_arrival(dst, send_sem, recv_sem, target):
    remote(dst, dst, send_sem, recv_sem, target).wait_recv()


def greet(z_count):
    z, y, x, c = place()
    barrier = pltpu.get_barrier_semaphore()

    def signal(target):
        pl.semaphore_signal(barrier, inc=1, device_id=target, device_id_type=MESH)

    signal(device(z, 1 - y, x, c))
    signal(device(z, y, 1 - x, c))
    signal(device(z, y, x, 1 - c))

    @pl.when(z > 0)
    def _():
        signal(device(z - 1, y, x, c))

    @pl.when(z < z_count - 1)
    def _():
        signal(device(z + 1, y, x, c))

    pl.semaphore_wait(barrier, 3 + jnp.minimum(z, 1) + jnp.minimum(z_count - 1 - z, 1))


def loop(low, high, body):
    if high - low <= 8:
        for step in range(low, high):
            body(step)
    else:

        def wrapped(step, carry):
            body(step)
            return carry

        lax.fori_loop(low, high, wrapped, 0)


def shared_gather(index):
    return index % 3 == 1


def gather_kernel(dims, w_ref, out_ref, local_sem, right_sem, left_sem, y_sem, x_sem, c_sem, recv_sem, c_recv):
    mats, z_count = dims
    z, y, x, c = place()
    greet(z_count)
    home = pltpu.make_async_copy(
        w_ref.at[:, pl.ds(2 * c, 2)], out_ref.at[:, pl.ds(2 * c, 2), z, y], local_sem
    )
    home.start()

    def span(index):
        if shared_gather(index):
            return pl.ds(2 * c, 2)
        return pl.ds(2 * c + x, 1)

    def spot(index, zz, yy):
        return out_ref.at[index, span(index), zz, yy]

    def to_right(index, zz, src):
        return remote(src, spot(index, zz, y), right_sem.at[index, zz], recv_sem.at[index, 0, zz, y], device(z + 1, y, x, c))

    def to_left(index, zz, src):
        return remote(src, spot(index, zz, y), left_sem.at[index, zz], recv_sem.at[index, 0, zz, y], device(z - 1, y, x, c))

    def to_y(index, zz, src):
        return remote(src, spot(index, zz, y), y_sem.at[index, zz], recv_sem.at[index, 0, zz, y], device(z, 1 - y, x, c))

    def to_x(index, zz, yy):
        return remote(
            spot(index, zz, yy), spot(index, zz, yy), x_sem.at[index, zz, yy], recv_sem.at[index, 1, zz, yy], device(z, y, 1 - x, c)
        )

    def to_c(index):
        pair = out_ref.at[index, pl.ds(2 * c, 2)]
        return remote(pair, pair, c_sem.at[index], c_recv.at[index], device(z, y, x, 1 - c))

    def arrived(index, zz, yy):
        await_arrival(spot(index, zz, yy), y_sem.at[index, zz], recv_sem.at[index, 0, zz, yy], device(z, 1 - y, x, c))

    def own(index):
        src = w_ref.at[index, span(index)]

        @pl.when(z < z_count - 1)
        def _():
            to_right(index, z, src).start()

        @pl.when(z > 0)
        def _():
            to_left(index, z, src).start()

        to_y(index, z, src).start()

    def line(index):
        def hop(away):
            @pl.when(z - away >= 0)
            def _():
                zz = z - away
                arrived(index, zz, y)

                @pl.when(z < z_count - 1)
                def _():
                    to_right(index, zz, spot(index, zz, y)).start()

                to_y(index, zz, spot(index, zz, y)).start()
                if not shared_gather(index):
                    to_x(index, zz, y).start()

            @pl.when(z + away < z_count)
            def _():
                zz = z + away
                arrived(index, zz, y)

                @pl.when(z > 0)
                def _():
                    to_left(index, zz, spot(index, zz, y)).start()

                to_y(index, zz, spot(index, zz, y)).start()
                if not shared_gather(index):
                    to_x(index, zz, y).start()

        loop(1, z_count, hop)

    def beside(index):
        def one(zz):
            arrived(index, zz, 1 - y)
            if not shared_gather(index):
                to_x(index, zz, 1 - y).start()

        one(z)

        def hop(away):
            @pl.when(z - away >= 0)
            def _():
                one(z - away)

            @pl.when(z + away < z_count)
            def _():
                one(z + away)

        loop(1, z_count, hop)

    def opposite(index):
        if not shared_gather(index):

            def one(zz, yy):
                block = out_ref.at[index, pl.ds(2 * c + 1 - x, 1), zz, yy]
                await_arrival(block, x_sem.at[index, zz, yy], recv_sem.at[index, 1, zz, yy], device(z, y, 1 - x, c))

            def each(zz):
                @pl.when(zz != z)
                def _():
                    one(zz, y)

                one(zz, 1 - y)

            loop(0, z_count, each)
        to_c(index).start()

    def finish(index):
        pair = out_ref.at[index, pl.ds(2 * (1 - c), 2)]
        await_arrival(pair, c_sem.at[index], c_recv.at[index], device(z, y, x, 1 - c))

    for tick in range(mats + 3):
        if tick == 0:
            own(0)
            own(1)
        elif tick + 1 < mats:
            own(tick + 1)
        if tick < mats:
            line(tick)
        if tick == 0:
            home.wait()
        if 1 <= tick <= mats:
            beside(tick - 1)
        if 2 <= tick <= mats + 1:
            opposite(tick - 2)
        if 3 <= tick:
            finish(tick - 3)

    for index in range(mats):

        def each(zz):
            @pl.when(jnp.logical_and(zz <= z, z < z_count - 1))
            def _():
                to_right(index, zz, spot(index, zz, y)).wait_send()

            @pl.when(jnp.logical_and(zz >= z, z > 0))
            def _():
                to_left(index, zz, spot(index, zz, y)).wait_send()

            to_y(index, zz, spot(index, zz, y)).wait_send()
            if not shared_gather(index):

                @pl.when(zz != z)
                def _():
                    to_x(index, zz, y).wait_send()

                to_x(index, zz, 1 - y).wait_send()

        loop(0, z_count, each)
        to_c(index).wait_send()


def gather_weights(packed, dp):
    mats, blocks, rows, width = packed.shape
    z_count = dp // 2
    dma = pltpu.SemaphoreType.DMA
    return pl.pallas_call(
        functools.partial(gather_kernel, (mats, z_count)),
        out_shape=jax.ShapeDtypeStruct((mats, blocks, z_count, 2, rows, width), bfloat),
        in_specs=[pl.BlockSpec(memory_space=pl.ANY)],
        out_specs=pl.BlockSpec(memory_space=pl.ANY),
        scratch_shapes=[
            dma,
            dma((mats, z_count)),
            dma((mats, z_count)),
            dma((mats, z_count)),
            dma((mats, z_count, 2)),
            dma((mats,)),
            dma((mats, 2, z_count, 2)),
            dma((mats,)),
        ],
        compiler_params=pltpu.CompilerParams(collective_id=1, has_side_effects=True),
        name="gather_weights",
    )(packed)


def dot_nn(left_side, right_side):
    return lax.dot_general(left_side, right_side, (((1,), (0,)), ((), ())), preferred_element_type=single)


def dot_nt(left_side, right_side):
    return lax.dot_general(left_side, right_side, (((1,), (1,)), ((), ())), preferred_element_type=single)


def dot_tn(left_side, right_side):
    return lax.dot_general(left_side, right_side, (((0,), (0,)), ((), ())), preferred_element_type=single)


def normalize(values):
    centre = jnp.mean(values, axis=-1, keepdims=True)
    offset = values - centre
    spread = jnp.mean(offset * offset, axis=-1, keepdims=True)
    scale = lax.rsqrt(spread + norm_eps)
    return offset * scale, scale


def normalize_back(grad, unit, scale, gain_row):
    grad_unit = grad * gain_row
    first = jnp.mean(grad_unit, axis=-1, keepdims=True)
    second = jnp.mean(grad_unit * unit, axis=-1, keepdims=True)
    return scale * (grad_unit - first - unit * second)


def compute_kernel(
    layers, pieces_ref, meta_ref, cot_ref, w_ref, gain_ref, bias_ref, table_ref,
    emb_ref, dx_ref, grad_ref, small_ref,
    x_ref, unit_ref, scale_ref, a_ref, b_ref, qkv_ref, prob_ref, o_ref, g_ref, slope_ref, dqkv_ref, do_ref, acc_ref, turn_ref,
):
    entries, _, width = pieces_ref.shape
    rows = entries * SLOTS
    half = rows // 2
    groups = table_ref.shape[0]
    pairs = width // 128
    final = 2 * layers
    proj = 3 * layers

    tags_row = meta_ref[0:1, :]
    counts_row = meta_ref[1:2, :]
    columns = meta_ref[...].T
    tags_col = columns[:, 0:1]
    counts_col = columns[:, 1:2]

    group_col = lax.broadcasted_iota(jnp.int32, (rows, groups), 1).astype(single)
    onehot = (group_col == tags_col).astype(single)
    x_ref[0] = lax.dot_general(
        onehot, table_ref[...], (((1,), (0,)), ((), ())), precision=highest, preferred_element_type=single
    )
    for entry in range(entries):
        at = entry * SLOTS
        x_ref[0, at : at + PIECES, :] = x_ref[0, at : at + PIECES, :] + pieces_ref[entry].astype(single)

    row_at = lax.broadcasted_iota(jnp.int32, (half, 2 * half), 0)
    key_at = lax.rem(lax.broadcasted_iota(jnp.int32, (half, 2 * half), 1), half)
    same = lax.div(row_at, SLOTS) == lax.div(key_at, SLOTS)
    key_slot = lax.rem(key_at, SLOTS).astype(single)
    low_lane = lax.broadcasted_iota(jnp.int32, (half, 128), 1) < HD

    def key_mask(part):
        piece = counts_row[:, part * half : (part + 1) * half]
        counts_here = jnp.concatenate([piece, piece], axis=1)
        return jnp.logical_and(same, key_slot < counts_here)

    def split_pair(values):
        zero = jnp.zeros_like(values)
        return jnp.concatenate([jnp.where(low_lane, values, zero), jnp.where(low_lane, zero, values)], axis=0)

    def forward(layer, carry):
        values = x_ref[layer]
        unit, scale = normalize(values)
        unit_ref[2 * layer] = unit
        scale_ref[2 * layer] = scale
        a = (unit * gain_ref[2 * layer] + bias_ref[2 * layer]).astype(bfloat)
        a_ref[layer] = a
        for part in range(3):
            qkv_ref[layer, part] = dot_nn(a, w_ref[3 * layer, part]).astype(bfloat)
        for part in range(2):
            mask = key_mask(part)
            here = slice(part * half, (part + 1) * half)
            for pair in range(pairs):
                lanes = slice(pair * 128, (pair + 1) * 128)
                q = qkv_ref[layer, 0, here, lanes]
                keys = split_pair(qkv_ref[layer, 1, here, lanes])
                vals = split_pair(qkv_ref[layer, 2, here, lanes])
                scores = dot_nt(q, keys) * HD ** (-0.5)
                scores = jnp.where(mask, scores, masked_score)
                probs = []
                for head in range(2):
                    mine = scores[:, head * half : (head + 1) * half]
                    top = jnp.max(mine, axis=-1, keepdims=True)
                    raised = jnp.exp(mine - top)
                    probs.append(raised / jnp.sum(raised, axis=-1, keepdims=True))
                prob = jnp.concatenate(probs, axis=1)
                prob_ref[layer, part * pairs + pair] = prob
                o_ref[layer, here, lanes] = dot_nn(prob.astype(bfloat), vals).astype(bfloat)
        middle = values + dot_nt(o_ref[layer], w_ref[3 * layer, 3])
        unit, scale = normalize(middle)
        unit_ref[2 * layer + 1] = unit
        scale_ref[2 * layer + 1] = scale
        b_ref[layer] = (unit * gain_ref[2 * layer + 1] + bias_ref[2 * layer + 1]).astype(bfloat)
        acc_ref[...] = middle

        def hidden(block, carry):
            u = dot_nn(b_ref[layer], w_ref[3 * layer + 1, block])
            gate = 0.5 * (1.0 + lax.erf(u * math.sqrt(0.5)))
            g = (u * gate).astype(bfloat)
            g_ref[layer, block] = g
            slope_ref[layer, block] = gate + u * (jnp.exp(-0.5 * u * u) * (1.0 / math.sqrt(2.0 * math.pi)))
            acc_ref[...] += dot_nt(g, w_ref[3 * layer + 2, block])
            return carry

        lax.fori_loop(0, BLOCKS, hidden, 0)
        x_ref[layer + 1] = acc_ref[...]
        return carry

    lax.fori_loop(0, layers, forward, 0)

    unit, scale = normalize(x_ref[layers])
    normed = unit * gain_ref[final] + bias_ref[final]
    slot_col = lax.rem(lax.broadcasted_iota(jnp.int32, (rows, 1), 0), SLOTS).astype(single)
    used_col = (slot_col < counts_col).astype(single)
    pooled = jnp.sum((normed * used_col).reshape(entries, SLOTS, width), axis=1)
    counts_entry = counts_col.reshape(entries, SLOTS, 1)[:, 0, :]
    pooled_low = (pooled / counts_entry).astype(bfloat)
    grad_pooled = jnp.zeros((entries, width), single)
    for block in range(BLOCKS):
        lanes = slice(block * width, (block + 1) * width)
        emb_ref[:, lanes] = dot_nn(pooled_low, w_ref[proj, block])
        grad_ref[proj, block] = dot_tn(pooled_low, cot_ref[:, lanes]).astype(bfloat)
        grad_pooled += dot_nt(cot_ref[:, lanes], w_ref[proj, block])
    grad_pooled = grad_pooled / counts_entry
    grad_normed = jnp.broadcast_to(grad_pooled[:, None, :], (entries, SLOTS, width)).reshape(rows, width) * used_col
    small_ref[...] = jnp.zeros_like(small_ref)
    small_ref[pl.ds(final, 1), :] = jnp.sum(grad_normed * unit, axis=0, keepdims=True)
    small_ref[pl.ds(SLOTS + final, 1), :] = jnp.sum(grad_normed, axis=0, keepdims=True)
    acc_ref[...] = normalize_back(grad_normed, unit, scale, gain_ref[final])

    def backward(step, carry):
        layer = layers - 1 - step
        grad_next = acc_ref[...]
        a_ref_here = a_ref[layer]
        dz = grad_next.astype(bfloat)
        do_ref[...] = dz
        turn_ref[0] = grad_next.T.astype(bfloat)
        turn_ref[1] = b_ref[layer].astype(single).T.astype(bfloat)
        acc_ref[...] = jnp.zeros_like(acc_ref)

        def hidden(block, carry):
            grad_ref[3 * layer + 2, block] = dot_nn(turn_ref[0], g_ref[layer, block]).astype(bfloat)
            grad_act = dot_nn(do_ref[...], w_ref[3 * layer + 2, block])
            du = (grad_act * slope_ref[layer, block]).astype(bfloat)
            grad_ref[3 * layer + 1, block] = dot_nn(turn_ref[1], du).astype(bfloat)
            acc_ref[...] += dot_nt(du, w_ref[3 * layer + 1, block])
            return carry

        lax.fori_loop(0, BLOCKS, hidden, 0)
        grad_b = acc_ref[...]
        unit = unit_ref[2 * layer + 1]
        small_ref[pl.ds(2 * layer + 1, 1), :] = jnp.sum(grad_b * unit, axis=0, keepdims=True)
        small_ref[pl.ds(SLOTS + 2 * layer + 1, 1), :] = jnp.sum(grad_b, axis=0, keepdims=True)
        grad_middle = grad_next + normalize_back(grad_b, unit, scale_ref[2 * layer + 1], gain_ref[2 * layer + 1])
        acc_ref[...] = grad_middle
        dy = grad_middle.astype(bfloat)
        grad_ref[3 * layer, 3] = dot_nn(grad_middle.T.astype(bfloat), o_ref[layer]).astype(bfloat)
        do_ref[...] = dot_nn(dy, w_ref[3 * layer, 3]).astype(bfloat)
        for part in range(2):
            here = slice(part * half, (part + 1) * half)
            for pair in range(pairs):
                lanes = slice(pair * 128, (pair + 1) * 128)
                q = qkv_ref[layer, 0, here, lanes]
                keys = split_pair(qkv_ref[layer, 1, here, lanes])
                vals = split_pair(qkv_ref[layer, 2, here, lanes])
                do = do_ref[here, lanes]
                prob = prob_ref[layer, part * pairs + pair]
                grad_prob = dot_nt(do, vals)
                product = grad_prob * prob
                scored = []
                for head in range(2):
                    spans = slice(head * half, (head + 1) * half)
                    total = jnp.sum(product[:, spans], axis=-1, keepdims=True)
                    scored.append(product[:, spans] - prob[:, spans] * total)
                ds = jnp.concatenate(scored, axis=1)
                ds_low = ds.astype(bfloat)
                dv = dot_tn(prob.astype(bfloat), do)
                dk = dot_tn(ds_low, q)
                dq = dot_nn(ds_low, keys)
                dqkv_ref[0, here, lanes] = (dq * HD ** (-0.5)).astype(bfloat)
                dqkv_ref[1, here, lanes] = (jnp.where(low_lane, dk[:half], dk[half:]) * HD ** (-0.5)).astype(bfloat)
                dqkv_ref[2, here, lanes] = jnp.where(low_lane, dv[:half], dv[half:]).astype(bfloat)
        turned = a_ref_here.astype(single).T.astype(bfloat)
        grad_a = jnp.zeros((rows, width), single)
        for part in range(3):
            grad_ref[3 * layer, part] = dot_nn(turned, dqkv_ref[part]).astype(bfloat)
            grad_a += dot_nt(dqkv_ref[part], w_ref[3 * layer, part])
        unit = unit_ref[2 * layer]
        small_ref[pl.ds(2 * layer, 1), :] = jnp.sum(grad_a * unit, axis=0, keepdims=True)
        small_ref[pl.ds(SLOTS + 2 * layer, 1), :] = jnp.sum(grad_a, axis=0, keepdims=True)
        acc_ref[...] += normalize_back(grad_a, unit, scale_ref[2 * layer], gain_ref[2 * layer])
        return carry

    lax.fori_loop(0, layers, backward, 0)
    for entry in range(entries):
        at = entry * SLOTS
        dx_ref[entry] = acc_ref[at : at + PIECES, :]
    group_row = lax.broadcasted_iota(jnp.int32, (groups, rows), 0).astype(single)
    spread = (group_row == tags_row).astype(single)
    small_ref[2 * SLOTS : 2 * SLOTS + groups, :] = lax.dot_general(
        spread, acc_ref[...], (((1,), (0,)), ((), ())), precision=highest, preferred_element_type=single
    )


def compute(pieces, meta, cotangent, weights, gain, bias, table, layers):
    entries, _, width = pieces.shape
    rows = entries * SLOTS
    pairs = width // 128
    vmem = pl.BlockSpec(memory_space=VMEM)
    return pl.pallas_call(
        functools.partial(compute_kernel, layers),
        out_shape=(
            jax.ShapeDtypeStruct(cotangent.shape, single),
            jax.ShapeDtypeStruct(pieces.shape, single),
            jax.ShapeDtypeStruct(weights.shape, bfloat),
            jax.ShapeDtypeStruct((SMALL_ROWS, width), single),
        ),
        in_specs=[vmem] * 7,
        out_specs=(vmem, vmem, vmem, vmem),
        scratch_shapes=[
            VMEM((layers + 1, rows, width), single),
            VMEM((2 * layers, rows, width), single),
            VMEM((2 * layers, rows, 1), single),
            VMEM((layers, rows, width), bfloat),
            VMEM((layers, rows, width), bfloat),
            VMEM((layers, 3, rows, width), bfloat),
            VMEM((layers, 2 * pairs, rows // 2, rows), single),
            VMEM((layers, rows, width), bfloat),
            VMEM((layers, BLOCKS, rows, width), bfloat),
            VMEM((layers, BLOCKS, rows, width), single),
            VMEM((3, rows, width), bfloat),
            VMEM((rows, width), bfloat),
            VMEM((rows, width), single),
            VMEM((2, width, rows), bfloat),
        ],
        compiler_params=pltpu.CompilerParams(vmem_limit_bytes=60 * 2**20),
        name="forward_backward",
    )(pieces, meta, cotangent, weights, gain, bias, table)


def shared_reduce(index):
    return lax.rem(index, 2) == 1


def reduce_kernel(
    dims, grad_ref, small_ref,
    out_ref, total_ref, norm_ref,
    acc, c_buf, x_buf, y_buf, l_buf, r_buf, f_buf, part_ref, s_x, s_y, s_c, s_z, s_cur, n_buf,
    load_sem, c_ss, c_rs, x_ss, x_rs, y_ss, y_rs, z_ss, l_rs, r_rs, fx_ss, fx_rs, fc_ss, fc_rs, s_ss, s_rs, n_ss, n_rs,
):
    mats, z_count = dims
    z, y, x, c = place()
    units = mats * z_count
    rows = out_ref.shape[2]
    dp = 2 * z_count
    me = z * 2 + y

    barrier = pltpu.get_barrier_semaphore()

    def signal(target):
        pl.semaphore_signal(barrier, inc=1, device_id=target, device_id_type=MESH)

    def greet_dp(step, carry):
        other = lax.rem(me + step, dp)
        pl.semaphore_signal(barrier, inc=1, device_id=(other, x * 2 + c), device_id_type=MESH)
        return carry

    lax.fori_loop(1, dp, greet_dp, 0)
    signal(device(z, y, 1 - x, c))
    signal(device(z, y, x, 1 - c))
    pl.semaphore_wait(barrier, dp + 1)

    right, left = device(z + 1, y, x, c), device(z - 1, y, x, c)
    y_side, x_side, c_side = device(z, 1 - y, x, c), device(z, y, 1 - x, c), device(z, y, x, 1 - c)

    load = pltpu.make_async_copy(grad_ref.at[:, pl.ds(2 * c, 2)], acc, load_sem)
    load.start()

    def order(unit):
        index = mats - 1 - lax.div(unit, z_count)
        turn = lax.rem(unit, z_count)
        target = jnp.where(lax.rem(turn, 2) == 0, lax.div(turn, 2), z_count - 1 - lax.div(turn, 2))
        return index, target

    def to_c(unit):
        index, target = order(unit)
        return remote(
            grad_ref.at[index, pl.ds(2 * (1 - c), 2), target], c_buf.at[index, :, target], c_ss.at[index, target], c_rs.at[index, target], c_side
        )

    def to_x(index, target):
        return remote(acc.at[index, 1 - x, target], x_buf.at[index, target], x_ss.at[index, target], x_rs.at[index, target], x_side)

    def both(shared, make):
        @pl.when(shared)
        def _():
            make(pl.ds(0, 2))

        @pl.when(jnp.logical_not(shared))
        def _():
            make(pl.ds(x, 1))

    def to_y(index, target, span):
        return remote(
            acc.at[index, span, target, 1 - y], y_buf.at[index, span, target], y_ss.at[index, target], y_rs.at[index, target], y_side
        )

    def to_z(index, target, span, buf, sems, side):
        return remote(acc.at[index, span, target, y], buf.at[index, span, target], z_ss.at[index, target], sems.at[index, target], side)

    def add(ref, at, extra):
        ref[at] = (ref[at].astype(single) + extra.astype(single)).astype(bfloat)

    def stage_c(unit):
        index, target = order(unit)
        to_c(unit).wait_recv()
        for block in range(2):
            add(acc, (index, block, target), c_buf[index, block, target])
        shared = shared_reduce(index)

        @pl.when(shared)
        def _():
            to_y(index, target, pl.ds(0, 2)).start()

        @pl.when(jnp.logical_not(shared))
        def _():
            to_x(index, target).start()

    def stage_x(unit):
        index, target = order(unit)

        @pl.when(jnp.logical_not(shared_reduce(index)))
        def _():
            to_x(index, target).wait_recv()
            add(acc, (index, x, target), x_buf[index, target])
            to_y(index, target, pl.ds(x, 1)).start()

    def stage_y(unit):
        index, target = order(unit)

        def make(span):
            to_y(index, target, span).wait_recv()
            add(acc, (index, span, target, y), y_buf[index, span, target])

            @pl.when(jnp.logical_and(z == 0, target != 0))
            def _():
                to_z(index, target, span, l_buf, l_rs, right).start()

            @pl.when(jnp.logical_and(z == z_count - 1, target != z_count - 1))
            def _():
                to_z(index, target, span, r_buf, r_rs, left).start()

        both(shared_reduce(index), make)

    def stage_z(unit):
        index, target = order(unit)

        def make(span):
            at = (index, span, target, y)
            from_left = jnp.logical_and(z > 0, target >= z)
            from_right = jnp.logical_and(z < z_count - 1, target <= z)

            @pl.when(from_left)
            def _():
                to_z(index, target, span, l_buf, l_rs, right).wait_recv()

            @pl.when(from_right)
            def _():
                to_z(index, target, span, r_buf, r_rs, left).wait_recv()

            @pl.when(jnp.logical_and(from_left, target > z))
            def _():
                add(acc, at, l_buf[index, span, target])
                to_z(index, target, span, l_buf, l_rs, right).start()

            @pl.when(jnp.logical_and(from_right, target < z))
            def _():
                add(acc, at, r_buf[index, span, target])
                to_z(index, target, span, r_buf, r_rs, left).start()

            @pl.when(target == z)
            def _():
                part_ref[...] = acc[index, :, target, y].astype(single)

                @pl.when(from_left)
                def _():
                    part_ref[span] = part_ref[span] + l_buf[index, span, target].astype(single)

                @pl.when(from_right)
                def _():
                    part_ref[span] = part_ref[span] + r_buf[index, span, target].astype(single)

        both(shared_reduce(index), make)

        @pl.when(target == z)
        def _():
            @pl.when(shared_reduce(index))
            def _():
                f_buf[index, 0] = part_ref[...].astype(bfloat)

            @pl.when(jnp.logical_not(shared_reduce(index)))
            def _():
                out_ref[index, pl.ds(2 * c + x, 1)] = part_ref[pl.ds(x, 1)].astype(bfloat)

            start_final(index)

    def final_shared(index):
        return remote(f_buf.at[index, 0], f_buf.at[index, 1], fx_ss.at[index], fx_rs.at[index], x_side)

    def final_split(index):
        mine = out_ref.at[index, 2 * c + x]
        return remote(mine, mine, fx_ss.at[index], fx_rs.at[index], x_side)

    def final_c(index):
        pair = out_ref.at[index, pl.ds(2 * c, 2)]
        return remote(pair, pair, fc_ss.at[index], fc_rs.at[index], c_side)

    def on_type(index, shared_do, split_do):
        @pl.when(shared_reduce(index))
        def _():
            shared_do()

        @pl.when(jnp.logical_not(shared_reduce(index)))
        def _():
            split_do()

    def start_final(index):
        on_type(index, lambda: final_shared(index).start(), lambda: final_split(index).start())

    def stage_f(unit):
        index, target = order(unit)

        @pl.when(target == z)
        def _():
            @pl.when(shared_reduce(index))
            def _():
                final_shared(index).wait_recv()
                total = f_buf[index, 0].astype(single) + f_buf[index, 1].astype(single)
                out_ref[index, pl.ds(2 * c, 2)] = total.astype(bfloat)

            @pl.when(jnp.logical_not(shared_reduce(index)))
            def _():
                final_split(index).wait_recv()

            final_c(index).start()

    def small_step(stage):
        if stage == 0:
            remote(small_ref, s_c, s_ss.at[0], s_rs.at[0], c_side).start()
        elif stage == 1:
            remote(small_ref, s_c, s_ss.at[0], s_rs.at[0], c_side).wait_recv()
            s_cur[0] = small_ref[...] + s_c[...]
            remote(s_cur.at[0], s_x, s_ss.at[1], s_rs.at[1], x_side).start()
        elif stage == 2:
            remote(s_cur.at[0], s_x, s_ss.at[1], s_rs.at[1], x_side).wait_recv()
            s_cur[1] = s_cur[0] + s_x[...]
            remote(s_cur.at[1], s_y, s_ss.at[2], s_rs.at[2], y_side).start()
        elif stage == 3:
            remote(s_cur.at[1], s_y, s_ss.at[2], s_rs.at[2], y_side).wait_recv()
            s_z[z] = s_cur[1] + s_y[...]

            def send(step, carry):
                other = lax.rem(z + step, z_count)
                remote(s_z.at[z], s_z.at[z], s_ss.at[3 + other], s_rs.at[3 + z], device(other, y, x, c)).start()
                return carry

            lax.fori_loop(1, z_count, send, 0)
        else:

            def wait(step, carry):
                other = lax.rem(z + step, z_count)
                remote(s_z.at[other], s_z.at[other], s_ss.at[3 + other], s_rs.at[3 + other], device(other, y, x, c)).wait_recv()
                return carry

            lax.fori_loop(1, z_count, wait, 0)

            def gather(step, carry):
                return carry + s_z[step]

            total_ref[...] = lax.fori_loop(0, z_count, gather, jnp.zeros(total_ref.shape, single))

    small_step(0)

    def start_c(unit, carry):
        to_c(unit).start()
        return carry

    lax.fori_loop(0, units, start_c, 0)
    load.wait()
    small_step(1)

    lags = (0, 2, 4, 6, 8)
    stages = (stage_c, stage_x, stage_y, stage_z, stage_f)

    def tick(step, carry):
        for lag, stage in zip(lags, stages):
            unit = step - lag

            @pl.when(jnp.logical_and(unit >= 0, unit < units))
            def _():
                stage(unit)

        return carry

    lax.fori_loop(0, units, tick, 0)
    small_step(2)
    lax.fori_loop(units, units + lags[2], tick, 0)
    small_step(3)
    lax.fori_loop(units + lags[2], units + lags[-1], tick, 0)
    small_step(4)

    def arrive(index, carry):
        pair = out_ref.at[index, pl.ds(2 * (1 - c), 2)]
        remote(pair, pair, fc_ss.at[index], fc_rs.at[index], c_side).wait_recv()
        return carry

    lax.fori_loop(0, mats, arrive, 0)

    def squares(index, carry):
        values = out_ref[index].astype(single)
        return carry + jnp.sum(jnp.sum(values * values, axis=0), axis=0, keepdims=True)

    squared = lax.fori_loop(0, mats, squares, jnp.zeros((1, out_ref.shape[3]), single))
    n_buf[me] = jnp.broadcast_to(squared, n_buf.shape[1:])

    def send_norm(step, carry):
        other = lax.rem(me + step, dp)
        remote(n_buf.at[me], n_buf.at[me], n_ss.at[other], n_rs.at[me], (other, x * 2 + c)).start()
        return carry

    lax.fori_loop(1, dp, send_norm, 0)

    def wait_norm(step, carry):
        other = lax.rem(me + step, dp)
        remote(n_buf.at[other], n_buf.at[other], n_ss.at[other], n_rs.at[other], (other, x * 2 + c)).wait_recv()
        return carry

    lax.fori_loop(1, dp, wait_norm, 0)

    def sum_norm(step, carry):
        return carry + n_buf[step]

    spread = lax.fori_loop(0, dp, sum_norm, jnp.zeros(n_buf.shape[1:], single))
    smalls = total_ref[...]
    norm_ref[...] = jnp.broadcast_to(
        jnp.sum(spread[0:1], axis=1, keepdims=True) + jnp.sum(jnp.sum(smalls * smalls, axis=0, keepdims=True), axis=1, keepdims=True),
        norm_ref.shape,
    )

    def done_unit(unit, carry):
        index, target = order(unit)
        to_c(unit).wait_send()

        @pl.when(jnp.logical_not(shared_reduce(index)))
        def _():
            to_x(index, target).wait_send()

        def make(span):
            to_y(index, target, span).wait_send()

            @pl.when(target != z)
            def _():
                to_z(index, target, span, l_buf, l_rs, y_side).wait_send()

        both(shared_reduce(index), make)
        return carry

    lax.fori_loop(0, units, done_unit, 0)

    def done_mat(index, carry):
        on_type(index, lambda: final_shared(index).wait_send(), lambda: final_split(index).wait_send())
        final_c(index).wait_send()
        return carry

    lax.fori_loop(0, mats, done_mat, 0)
    remote(small_ref, s_c, s_ss.at[0], s_rs.at[0], c_side).wait_send()
    remote(s_cur.at[0], s_x, s_ss.at[1], s_rs.at[1], x_side).wait_send()
    remote(s_cur.at[1], s_y, s_ss.at[2], s_rs.at[2], y_side).wait_send()

    def done_z(step, carry):
        other = lax.rem(z + step, z_count)
        remote(s_z.at[z], s_z.at[z], s_ss.at[3 + other], s_rs.at[3 + z], device(other, y, x, c)).wait_send()
        return carry

    lax.fori_loop(1, z_count, done_z, 0)

    def done_norm(step, carry):
        other = lax.rem(me + step, dp)
        remote(n_buf.at[me], n_buf.at[me], n_ss.at[other], n_rs.at[me], (other, x * 2 + c)).wait_send()
        return carry

    lax.fori_loop(1, dp, done_norm, 0)


def reduce_gradients(grads, small, dp):
    mats, blocks, z_count, _, rows, width = grads.shape
    dma = pltpu.SemaphoreType.DMA
    vmem = pl.BlockSpec(memory_space=VMEM)
    return pl.pallas_call(
        functools.partial(reduce_kernel, (mats, z_count)),
        out_shape=(
            jax.ShapeDtypeStruct((mats, blocks, rows, width), bfloat),
            jax.ShapeDtypeStruct(small.shape, single),
            jax.ShapeDtypeStruct((8, 128), single),
        ),
        in_specs=[pl.BlockSpec(memory_space=pl.ANY), vmem],
        out_specs=(vmem, vmem, vmem),
        scratch_shapes=[
            VMEM((mats, 2, z_count, 2, rows, width), bfloat),
            VMEM((mats, 2, z_count, 2, rows, width), bfloat),
            VMEM((mats, z_count, 2, rows, width), bfloat),
            VMEM((mats, 2, z_count, rows, width), bfloat),
            VMEM((mats, 2, z_count, rows, width), bfloat),
            VMEM((mats, 2, z_count, rows, width), bfloat),
            VMEM((mats, 2, 2, rows, width), bfloat),
            VMEM((2, rows, width), single),
            VMEM(small.shape, single),
            VMEM(small.shape, single),
            VMEM(small.shape, single),
            VMEM((z_count, *small.shape), single),
            VMEM((2, *small.shape), single),
            VMEM((dp, 8, width), single),
            dma,
            dma((mats, z_count)),
            dma((mats, z_count)),
            dma((mats, z_count)),
            dma((mats, z_count)),
            dma((mats, z_count)),
            dma((mats, z_count)),
            dma((mats, z_count)),
            dma((mats, z_count)),
            dma((mats, z_count)),
            dma((mats,)),
            dma((mats,)),
            dma((mats,)),
            dma((mats,)),
            dma((3 + z_count,)),
            dma((3 + z_count,)),
            dma((dp,)),
            dma((dp,)),
        ],
        compiler_params=pltpu.CompilerParams(collective_id=2, has_side_effects=True, vmem_limit_bytes=60 * 2**20),
        name="reduce_gradients",
    )(grads, small)


def adam_update(weight, first, second, gradient, clip_scale, decay, step_rate):
    clipped = gradient * clip_scale
    first_new = beta_first * first + (1.0 - beta_first) * clipped
    second_new = beta_second * second + (1.0 - beta_second) * clipped * clipped
    first_hat = first_new / (1.0 - beta_first**STEP)
    second_hat = second_new / (1.0 - beta_second**STEP)
    weight_new = weight - step_rate * (first_hat / (jnp.sqrt(second_hat) + adam_eps) + decay * weight)
    return (weight_new, first_new, second_new)


def pack(qkv, out, up, down, proj):
    layers, _, rows, width = qkv.shape
    parts = []
    front = jnp.concatenate([qkv, jnp.swapaxes(out, 1, 2)[:, None]], axis=1)
    rise = jnp.swapaxes(up.reshape(layers, rows, BLOCKS, width), 1, 2)
    fall = jnp.swapaxes(jnp.swapaxes(down, 1, 2).reshape(layers, rows, BLOCKS, width), 1, 2)
    body = jnp.stack([front, rise, fall], axis=1).reshape(3 * layers, BLOCKS, rows, width)
    last = jnp.swapaxes(proj.reshape(rows, BLOCKS, width), 0, 1)[None]
    return jnp.concatenate([body, last], axis=0)


def unpack(packed, layers):
    _, _, rows, width = packed.shape
    body = packed[: 3 * layers].reshape(layers, 3, BLOCKS, rows, width)
    qkv = body[:, 0, :3]
    out = jnp.swapaxes(body[:, 0, 3], 1, 2)
    up = jnp.swapaxes(body[:, 1], 1, 2).reshape(layers, rows, BLOCKS * width)
    down = jnp.swapaxes(jnp.swapaxes(body[:, 2], 1, 2).reshape(layers, rows, BLOCKS * width), 1, 2)
    proj = jnp.swapaxes(packed[3 * layers], 0, 1).reshape(rows, BLOCKS * width)
    return qkv, out, up, down, proj


def per_device(
    pieces, script_tags, counts, cotangent,
    qkv_weight, qkv_first, qkv_second,
    out_weight, out_first, out_second,
    up_weight, up_first, up_second,
    down_weight, down_first, down_second,
    proj_weight, proj_first, proj_second,
    norm_gain, gain_first, gain_second,
    norm_bias, bias_first, bias_second,
    group_table, table_first, table_second,
):
    layers = qkv_weight.shape[0]
    width = pieces.shape[2]
    dp = lax.axis_size("dp")
    norms = norm_gain.shape[0]
    groups = group_table.shape[0]
    packed = pack(
        qkv_weight.astype(bfloat), out_weight.astype(bfloat), up_weight.astype(bfloat), down_weight.astype(bfloat), proj_weight.astype(bfloat)
    )
    gathered = gather_weights(packed, dp)
    mats = gathered.shape[0]
    weights = gathered.reshape(mats, BLOCKS, width, width)
    meta = jnp.stack([jnp.repeat(script_tags, SLOTS), jnp.repeat(counts, SLOTS)]).astype(single)
    meta = jnp.concatenate([meta, jnp.zeros((SLOTS - 2, meta.shape[1]), single)], axis=0)
    embeddings, input_grad, grads, small = compute(
        pieces, meta, cotangent, weights,
        norm_gain.reshape(norms, 1, width), norm_bias.reshape(norms, 1, width), group_table, layers,
    )
    reduced, small_total, square_total = reduce_gradients(grads.reshape(gathered.shape), small, dp)
    grad_norm = jnp.sqrt(square_total[0, 0])
    clip_scale = jnp.minimum(1.0, clip_level / (grad_norm + 1e-06))
    grad_qkv, grad_out, grad_up, grad_down, grad_proj = unpack(reduced.astype(single), layers)
    grad_gain = small_total[:norms]
    grad_bias = small_total[SLOTS : SLOTS + norms]
    grad_table = small_total[2 * SLOTS : 2 * SLOTS + groups]
    big = functools.partial(adam_update, clip_scale=clip_scale, decay=decay_rate, step_rate=learn_rate)
    little = functools.partial(adam_update, clip_scale=clip_scale, decay=0.0, step_rate=small_rate)
    return (
        embeddings,
        input_grad,
        grad_norm,
        *big(qkv_weight, qkv_first, qkv_second, grad_qkv),
        *big(out_weight, out_first, out_second, grad_out),
        *big(up_weight, up_first, up_second, grad_up),
        *big(down_weight, down_first, down_second, grad_down),
        *big(proj_weight, proj_first, proj_second, grad_proj),
        *little(norm_gain, gain_first, gain_second, grad_gain),
        *little(norm_bias, bias_first, bias_second, grad_bias),
        *little(group_table, table_first, table_second, grad_table),
    )


def solution(mesh):
    entry_split = ("dp", "mp")
    weight_specs = (P(None, None, "dp", None), P(None, None, "dp"), P(None, "dp", None), P(None, None, "dp"), P("dp", None))
    state = tuple(spec for spec in weight_specs for _ in range(3)) + (P(),) * 9
    return jax.shard_map(
        per_device,
        mesh=mesh,
        in_specs=(P(entry_split, None, None), P(entry_split), P(entry_split), P(entry_split, None)) + state,
        out_specs=(P(entry_split, None), P(entry_split, None, None), P()) + state,
        check_vma=False,
    )
```

time: 895 us -> 324 us (0.36)
  waiting for transfers between devices: 443 us -> 0 us
  Pallas kernels: 0 us -> 286 us
  blocking collectives: 224 us -> 0 us
  matrix products: 72.3 us -> 0 us
  local copies, waits for them, and re-layouts: 67.2 us -> 17.9 us
  other arithmetic: 53 us -> 16.2 us
  between operations: 26.1 us -> 2.88 us
    reduce_scatter x10 -> x0, waiting for transfers between devices: 391 us -> none  [the longest x1 130 us: per_device(): lax.psum_scatter(grad_proj, 'dp', scatter_dimension=0, tiled=True)]
    pallas_call x0 -> x3, Pallas kernels: none -> 286 us  [the longest x1 153 us: reduce_gradients(): pl.pallas_call(functools.partial(reduce_kernel, (mats, z_count)), out_sha...]
    all_gather x16 -> x0, blocking collectives: 177 us -> none  [the longest x1 32.2 us: per_device(): lax.all_gather(qkv_source.astype(bfloat), 'dp', axis=2, tiled=True)]
    dot_general x39 -> x0, matrix products: 69 us -> none  [the longest x2 13.8 us: feed_front(): hidden_pre = jnp.dot(normed_all, up_layer, preferred_element_type=single)]
    all_gather x3 -> x0, waiting for transfers between devices: 51.7 us -> none  [the longest x1 34.8 us: per_device(): lax.all_gather(down_source.astype(bfloat), 'dp', axis=2, tiled=True)]
    psum x1 -> x0, blocking collectives: 40.8 us -> none  [per_device(): lax.psum((grad_gain, grad_bias, grad_table, square_sum), ('dp', 'mp'))]
    reduce_sum x29 -> x0, other arithmetic: 30.3 us -> none  [the longest x9 11.2 us: layer_norm(): return offset * lax.rsqrt(spread + norm_eps) * gain_row + bias_row]
    another operation x13 -> x4, local copies, waits for them, and re-layouts: 17.4 us -> 0.38 us  [the longest x2 0.2 us: pack(): jnp.stack([front, rise, fall], axis=1)]
  transfers between devices with their start and end apart: 14 -> 0, of which waited for: 12 -> 0; matrix products, arithmetic and copies ran while one was open for 7% -> 0% of each run, Pallas kernels for 0% -> 0%
where the time goes in v1:
time: 324 us; the launch traced here: 323 us
  Pallas kernels  286 us (88%)
  local copies, waits for them, and re-layouts  17.9 us (6%)
  other arithmetic  16.2 us (5%)
    pallas_call x1, Pallas kernels, reduce_gradients(): pl.pallas_call(functools.partial(reduce_kernel, (mats, z_count)), out_sha...  153 us
    pallas_call x1, Pallas kernels, gather_weights(): pl.pallas_call(functools.partial(gather_kernel, (mats, z_count)), out_sha...  94.3 us
    pallas_call x1, Pallas kernels, compute(): pl.pallas_call(functools.partial(compute_kernel, layers), out_shape=(jax....  38.8 us
    sub x7, other arithmetic, adam_update(): weight - step_rate * (first_hat / (jnp.sqrt(second_hat) + adam_eps) + dec...  11.5 us
    unnamed x52, local copies, waits for them, and re-layouts  9.46 us

profile of v1, /device:TPU:0, one launch (start us, length us, event | category | flops | bytes accessed | tf_op | source)
XLA Modules:
  0.0 323.4 jit_solution(4842813456130604226)
XLA Ops:
  0.7 0.0 copy-start.3
  0.7 1.4 reshape.106.gain_ref
  2.1 1.3 reshape.107.bias_ref
  3.4 0.7 broadcast_in_dim.13
  4.1 0.1 stack_reshape.6
  4.2 0.7 broadcast_in_dim.14
  4.9 0.1 stack_reshape.7
  5.0 0.6 concatenate.9.meta_ref
  5.7 1.0 convert_bitcast_fusion
  6.6 1.8 copy.70.pieces_ref
  8.4 1.2 convert_element_type.26
  9.6 0.0 copy-done.3
  9.6 0.0 copy-start.2
  9.6 0.1 convert_element_type.22
  9.7 0.1 maximum_bitcast_fusion
  9.7 0.1 copy-done.1
  9.8 0.1 convert_element_type.24
  9.9 1.0 copy-done.2
  10.9 0.1 convert_element_type.25
  10.9 0.1 bitcast_bitcast_fusion
  11.0 0.2 pad_maximum_fusion.1
  11.2 0.1 copy.68
  11.3 1.4 pad_maximum_fusion.w_ref
  12.8 94.3 %gather_weights.1 = bf16[7,4,4,2,64,512]{5,4,3,2,1,0:T(8,128)(2,1)} custom-call(bf16[7,4,64,512]{3,2,1,0:T(8,128)(2,1)} %pad_maximum_fusion.w_ref), custom_call_target="tpu_custom_call" | custom-call | tf_op jit(solution)/shard_map/gather_weights/pallas_call | solution.py:258
  107.0 38.8 %forward_backward.1 = (f32[32,2048]{1,0:T(8,128)}, f32[32,7,512]{2,1,0:T(8,128)}, bf16[7,4,512,512]{3,2,1,0:T(8,128)(2,1)}, f32[32,512]{1,0:T(8,128)}) custom-call(bf16[32,7,512]{2,1,0:T(8,128)(2,1)} %copy.70.pieces_ref, f32[8,256]{1,0:T(8,128)} %concatenate.9.meta_ref, bf16[32,2048]{1,0:T(8,128)(2,1)} %cot_ref.1, bf16[7,4,512,512]{3,2,1,0:T(8,128)(2,1)} %bitcast.104, ...), custom_call_target="tpu_custom_call" | custom-call | tf_op jit(solution)/shard_map/forward_backward/pallas_call | solution.py:497
  145.8 2.1 copy.76
  147.9 0.0 copy-start.23
  147.9 0.0 copy-start.24
  147.9 0.0 copy-start.16
  147.9 0.0 copy-start.19
  147.9 0.0 copy-start.20
  147.9 153.3 %reduce_gradients.1 = (bf16[7,4,64,512]{3,2,1,0:T(8,128)(2,1)}, f32[32,512]{1,0:T(8,128)}, f32[8,128]{1,0:T(8,128)}) custom-call(bf16[7,4,4,2,64,512]{5,4,3,2,1,0:T(8,128)(2,1)} %bitcast.105, f32[32,512]{1,0:T(8,128)} %get-tuple-element.37.small_ref), custom_call_target="tpu_custom_call" | custom-call | tf_op jit(solution)/shard_map/reduce_gradients/pallas_call | solution.py:886
  301.3 1.2 slice.30
  303.2 0.0 copy-done.17
  303.2 0.0 copy-done.18
  303.2 0.0 copy-done.21
  303.2 0.0 copy-done.22
  303.2 0.0 copy-done.23
  303.2 0.0 copy-done.24
  303.3 1.4 multiply_subtract_fusion.6
  304.6 0.0 copy-done.16
  304.6 0.0 copy-done.19
  304.7 1.4 multiply_subtract_fusion.5
  306.1 1.9 slice.40
  308.0 1.0 multiply_subtract_fusion.4
  309.0 0.7 copy-done
  309.8 0.5 convert_element_type.27
  310.3 0.0 copy-start.4
  310.3 0.0 copy-start.12
  310.3 0.0 copy-start.13
  310.4 0.9 copy-done.4
  311.3 0.2 copy-done.12
  311.5 0.2 copy-done.13
  311.6 1.4 multiply_subtract_fusion.3
  313.0 0.2 fusion.2
  313.3 0.9 copy-done.10
  314.2 0.2 copy-done.11
  314.4 1.8 multiply_subtract_fusion.2
  316.2 0.1 copy.83
  316.3 0.1 copy.82
  316.4 1.0 copy-done.5
  317.5 0.3 copy-done.6
  317.8 2.2 multiply_subtract_fusion.1
  320.0 2.2 multiply_subtract_fusion
  (25 shorter events, 0.1 us)
Async XLA Ops:
  0.7 8.9 %copy-start.3 = (f32[2,3,64,512]{3,2,1,0:T(8,128)S(1)}, f32[2,3,64,512]{3,2,1,0:T(8,128)}, u32[]{:S(2)}) copy-start(f32[2,3,64,512]{3,2,1,0:T(8,128)} %param.32) | copy-start | bytes 2359300
  8.4 1.4 copy-start.1
  9.6 1.3 copy-start.2
  147.9 155.3 %copy-start.17 = (f32[5,512]{1,0:T(8,128)S(1)}, f32[5,512]{1,0:T(8,128)}, u32[]{:S(2)}) copy-start(f32[5,512]{1,0:T(8,128)} %param.47) | copy-start | bytes 30724
  147.9 155.3 %copy-start.18 = (f32[5,512]{1,0:T(8,128)S(1)}, f32[5,512]{1,0:T(8,128)}, u32[]{:S(2)}) copy-start(f32[5,512]{1,0:T(8,128)} %param.50) | copy-start | bytes 30724
  147.9 155.3 %copy-start.21 = (f32[5,512]{1,0:T(8,128)S(1)}, f32[5,512]{1,0:T(8,128)}, u32[]{:S(2)}) copy-start(f32[5,512]{1,0:T(8,128)} %param.51) | copy-start | bytes 30724
  147.9 155.4 %copy-start.22 = (f32[5,512]{1,0:T(8,128)S(1)}, f32[5,512]{1,0:T(8,128)}, u32[]{:S(2)}) copy-start(f32[5,512]{1,0:T(8,128)} %param.52) | copy-start | bytes 30724
  147.9 155.4 %copy-start.23 = (f32[5,512]{1,0:T(8,128)S(1)}, f32[5,512]{1,0:T(8,128)}, u32[]{:S(2)}) copy-start(f32[5,512]{1,0:T(8,128)} %param.49) | copy-start | bytes 30724
  147.9 155.4 %copy-start.24 = (f32[5,512]{1,0:T(8,128)S(1)}, f32[5,512]{1,0:T(8,128)}, u32[]{:S(2)}) copy-start(f32[5,512]{1,0:T(8,128)} %param.48) | copy-start | bytes 30724
  147.9 156.7 %copy-start.16 = (f32[16,512]{1,0:T(8,128)S(1)}, f32[16,512]{1,0:T(8,128)}, u32[]{:S(2)}) copy-start(f32[16,512]{1,0:T(8,128)} %table_ref.1) | copy-start | bytes 98308
  147.9 156.7 %copy-start.19 = (f32[16,512]{1,0:T(8,128)S(1)}, f32[16,512]{1,0:T(8,128)}, u32[]{:S(2)}) copy-start(f32[16,512]{1,0:T(8,128)} %param.54) | copy-start | bytes 98308
  147.9 156.7 %copy-start.20 = (f32[16,512]{1,0:T(8,128)S(1)}, f32[16,512]{1,0:T(8,128)}, u32[]{:S(2)}) copy-start(f32[16,512]{1,0:T(8,128)} %param.55) | copy-start | bytes 98308
  306.1 1.9 copy-start.9
  306.1 1.9 copy-start.14
  306.1 1.9 copy-start.15
  308.0 1.8 copy-start
  310.3 1.0 copy-start.4
  310.3 1.2 copy-start.12
  310.3 1.3 copy-start.13
  313.0 1.1 copy-start.10
  313.0 1.4 copy-start.11
  316.2 1.2 copy-start.5
  316.2 1.5 copy-start.6
  317.8 2.2 copy-start.7
  317.8 2.2 copy-start.8

commit v2 on v1

v2 whole, which is shorter than its diff:
```python
import functools
import math

import jax
import jax.numpy as jnp
from jax import lax
from jax.experimental import pallas as pl
from jax.experimental.pallas import tpu as pltpu
from jax.sharding import PartitionSpec as P

HD = 64
PIECES = 7
SLOTS = 8
STEP = 10
BLOCKS = 4
SMALL_ROWS = 32

norm_eps = 1e-05
beta_first = 0.9
beta_second = 0.999
adam_eps = 1e-08
learn_rate = 0.03
small_rate = 0.5
decay_rate = 0.01
clip_level = 1.0
masked_score = -1000000000.0
bfloat = jnp.bfloat16
single = jnp.float32
highest = lax.Precision.HIGHEST
MESH = pl.DeviceIdType.MESH
VMEM = pltpu.VMEM


def place():
    along, across = lax.axis_index("dp"), lax.axis_index("mp")
    return lax.div(along, 2), lax.rem(along, 2), lax.div(across, 2), lax.rem(across, 2)


def device(z, y, x, c):
    return (z * 2 + y, x * 2 + c)


def remote(src, dst, send_sem, recv_sem, target):
    return pltpu.make_async_remote_copy(
        src_ref=src, dst_ref=dst, send_sem=send_sem, recv_sem=recv_sem, device_id=target, device_id_type=MESH
    )


def await_arrival(dst, send_sem, recv_sem, target):
    remote(dst, dst, send_sem, recv_sem, target).wait_recv()


def greet(z_count, whole_dp):
    z, y, x, c = place()
    barrier = pltpu.get_barrier_semaphore()

    def signal(target):
        pl.semaphore_signal(barrier, inc=1, device_id=target, device_id_type=MESH)

    signal(device(z, y, 1 - x, c))
    signal(device(z, y, x, 1 - c))
    if whole_dp:
        dp = 2 * z_count

        def one(step):
            signal((lax.rem(z * 2 + y + step, dp), x * 2 + c))

        loop(1, dp, one)
        pl.semaphore_wait(barrier, dp + 1)
    else:
        signal(device(z, 1 - y, x, c))

        def one(step):
            signal(device(lax.rem(z + step, z_count), y, x, c))

        loop(1, z_count, one)
        pl.semaphore_wait(barrier, z_count + 2)


def when(condition, body):
    if isinstance(condition, bool):
        if condition:
            body()
    else:
        pl.when(condition)(body)


def otherwise(condition):
    return not condition if isinstance(condition, bool) else jnp.logical_not(condition)


def loop(low, high, body):
    if high - low <= 8:
        for step in range(low, high):
            body(step)
    else:

        def wrapped(step, carry):
            body(step)
            return carry

        lax.fori_loop(low, high, wrapped, 0)


def dot_nn(left_side, right_side):
    return lax.dot_general(left_side, right_side, (((1,), (0,)), ((), ())), preferred_element_type=single)


def dot_nt(left_side, right_side):
    return lax.dot_general(left_side, right_side, (((1,), (1,)), ((), ())), preferred_element_type=single)


def dot_tn(left_side, right_side):
    return lax.dot_general(left_side, right_side, (((0,), (0,)), ((), ())), preferred_element_type=single)


def normalize(values):
    centre = jnp.mean(values, axis=-1, keepdims=True)
    offset = values - centre
    spread = jnp.mean(offset * offset, axis=-1, keepdims=True)
    scale = lax.rsqrt(spread + norm_eps)
    return offset * scale, scale


def normalize_back(grad, unit, scale, gain_row):
    grad_unit = grad * gain_row
    first = jnp.mean(grad_unit, axis=-1, keepdims=True)
    second = jnp.mean(grad_unit * unit, axis=-1, keepdims=True)
    return scale * (grad_unit - first - unit * second)


def shared_gather(index, zz):
    return lax.rem(index + zz, 4) == 0


def shared_reduce(index, target):
    return lax.rem(index + target, 2) == 1


AHEAD = 2
LAGS = (1, 2, 3)
REDUCE = (0, 2, 4, 6, 8)


def step_kernel(
    layers, z_count,
    pieces_ref, meta_ref, cot_ref, shard_ref, gain_ref, bias_ref, table_ref,
    emb_ref, dx_ref, out_ref, total_ref, norm_ref,
    w_ref, grad_ref, z_buf, f_buf, part_ref,
    x_ref, unit_ref, scale_ref, a_ref, b_ref, qkv_ref, prob_ref, o_ref, g_ref, slope_ref, dqkv_ref, do_ref, acc_ref, turn_ref, dpool_ref,
    small_ref, s_c, s_x, s_y, s_z, s_cur, n_buf,
    gx_ss, gc_ss, g_rs, gc_rs,
    c_ss, c_rs, x_ss, x_rs, y_ss, y_rs, z_ss, z_rs, fx_ss, fx_rs, fc_ss, fc_rs, s_ss, s_rs, n_ss, n_rs, credit,
):
    mats = 3 * layers + 1
    proj = 3 * layers
    final = 2 * layers
    entries, _, width = pieces_ref.shape
    rows = entries * SLOTS
    half = rows // 2
    groups = table_ref.shape[0]
    pairs = width // 128
    dp = 2 * z_count
    z, y, x, c = place()
    me = z * 2 + y
    y_side, x_side, c_side = device(z, 1 - y, x, c), device(z, y, 1 - x, c), device(z, y, x, 1 - c)
    greet(z_count, True)


    def matrix_at(turn):
        early = 3 * (layers - 1)
        return jnp.where(turn < early, turn, jnp.where(turn == early, proj, turn - 1))

    def by_type(index, zz, body):
        shared = shared_gather(index, zz)
        when(shared, lambda: body(pl.ds(2 * c, 2), False))
        when(otherwise(shared), lambda: body(pl.ds(2 * c + x, 1), True))

    def gather_z(index, other, span):
        return remote(
            shard_ref.at[index, span], w_ref.at[index, span, z, y], z_ss.at[index, other], g_rs.at[index, 0, z, y], device(other, y, x, c)
        )

    def gather_y(index, zz, span, src=None):
        spot = w_ref.at[index, span, zz, y]
        return remote(spot if src is None else src, spot, y_ss.at[index, zz], g_rs.at[index, 0, zz, y], y_side)

    def gather_x(index, zz, yy, span):
        spot = w_ref.at[index, span, zz, yy]
        return remote(spot, spot, gx_ss.at[index, zz, yy], g_rs.at[index, 1, zz, yy], x_side)

    def gather_c(index):
        pair = w_ref.at[index, pl.ds(2 * c, 2)]
        return remote(pair, pair, gc_ss.at[index], gc_rs.at[index], c_side)

    def arrived(index, zz, yy, span):
        await_arrival(w_ref.at[index, span, zz, yy], y_ss.at[index, zz], g_rs.at[index, 0, zz, yy], y_side)

    def own(index):
        def send(span, cross):
            gather_y(index, z, span, shard_ref.at[index, span]).start()

            def one(other):
                pl.when(other != z)(lambda: gather_z(index, other, span).start())

            loop(0, z_count, one)

        by_type(index, z, send)

    def line(index):
        def one(zz):
            def pass_on(span, cross):
                arrived(index, zz, y, span)
                gather_y(index, zz, span).start()
                if cross:
                    gather_x(index, zz, y, span).start()

            pl.when(z != zz)(lambda: by_type(index, zz, pass_on))

        loop(0, z_count, one)

    def beside(index):
        def one(zz):
            def pass_on(span, cross):
                arrived(index, zz, 1 - y, span)
                if cross:
                    gather_x(index, zz, 1 - y, span).start()

            by_type(index, zz, pass_on)

        loop(0, z_count, one)

    def opposite(index):
        def each(zz):
            def one(yy):
                block = w_ref.at[index, pl.ds(2 * c + 1 - x, 1), zz, yy]
                await_arrival(block, gx_ss.at[index, zz, yy], g_rs.at[index, 1, zz, yy], x_side)

            def two():
                pl.when(zz != z)(lambda: one(y))
                one(1 - y)

            when(otherwise(shared_gather(index, zz)), two)

        loop(0, z_count, each)
        gather_c(index).start()

    def finish(index):
        pair = w_ref.at[index, pl.ds(2 * (1 - c), 2)]
        await_arrival(pair, gc_ss.at[index], gc_rs.at[index], c_side)

    def gather_sent(index):
        def each(zz):
            def done(span, cross):
                gather_y(index, zz, span).wait_send()
                if cross:
                    pl.when(zz != z)(lambda: gather_x(index, zz, y, span).wait_send())
                    gather_x(index, zz, 1 - y, span).wait_send()

                def one(other):
                    pl.when(other != z)(lambda: gather_z(index, other, span).wait_send())

                pl.when(zz == z)(lambda: loop(0, z_count, one))

            by_type(index, zz, done)

        loop(0, z_count, each)
        gather_c(index).wait_send()

    def block_of(index, block):
        return w_ref[index, block].reshape(width, width)

    def put_grad(index, block, values):
        grad_ref[index, block] = values.astype(bfloat).reshape(grad_ref.shape[2:])


    units = mats * z_count
    pair_c = pl.ds(2 * c, 2)

    def order(unit):
        return mats - 1 - lax.div(unit, z_count), lax.rem(unit, z_count)

    def local(span):
        return pl.ds(2 * c, 2) if span is None else pl.ds(2 * c + x, 1)

    def near(span):
        return pl.ds(0, 2) if span is None else pl.ds(x, 1)

    def to_c(index, target):
        return remote(
            grad_ref.at[index, pl.ds(2 * (1 - c), 2), target], w_ref.at[index, pl.ds(0, 2), target],
            c_ss.at[index, target], c_rs.at[index, target], c_side,
        )

    def to_x(index, target):
        return remote(
            grad_ref.at[index, 2 * c + 1 - x, target], w_ref.at[index, 2, target], x_ss.at[index, target], x_rs.at[index, target], x_side
        )

    def to_y(index, target, span):
        return remote(
            grad_ref.at[index, local(span), target, 1 - y], w_ref.at[index, 3, target, near(span)],
            y_ss.at[index, target], y_rs.at[index, target], y_side,
        )

    def to_z(index, target, span):
        return remote(
            grad_ref.at[index, local(span), target, y], z_buf.at[index, near(span), z],
            z_ss.at[index, target], z_rs.at[index, z], device(target, y, x, c),
        )

    def from_z(index, source, span):
        await_arrival(z_buf.at[index, near(span), source], z_ss.at[index, source], z_rs.at[index, source], device(source, y, x, c))

    def both(shared, body):
        when(shared, lambda: body(None))
        when(otherwise(shared), lambda: body(1))

    def add(ref, at, extra):
        ref[at] = (ref[at].astype(single) + extra.astype(single)).astype(bfloat)

    def give_credit(index):
        for kind, side in enumerate((c_side, x_side, y_side)):
            pl.semaphore_signal(credit.at[kind, index], inc=1, device_id=side, device_id_type=MESH)

    def start_matrix(index):
        give_credit(index)
        pl.semaphore_wait(credit.at[0, index], 1)
        loop(0, z_count, lambda target: to_c(index, target).start())

    def stage_c(unit):
        index, target = order(unit)
        to_c(index, target).wait_recv()
        for block in range(2):
            add(grad_ref, (index, 2 * c + block, target), w_ref[index, block, target])
        shared = shared_reduce(index, target)

        @pl.when(target == 0)
        def _():
            pl.semaphore_wait(credit.at[1, index], 1)
            pl.semaphore_wait(credit.at[2, index], 1)

        when(shared, lambda: to_y(index, target, None).start())
        when(otherwise(shared), lambda: to_x(index, target).start())

    def stage_x(unit):
        index, target = order(unit)

        @pl.when(otherwise(shared_reduce(index, target)))
        def _():
            to_x(index, target).wait_recv()
            add(grad_ref, (index, 2 * c + x, target), w_ref[index, 2, target])
            to_y(index, target, 1).start()

    def stage_y(unit):
        index, target = order(unit)

        def make(span):
            to_y(index, target, span).wait_recv()
            add(grad_ref, (index, local(span), target, y), w_ref[index, 3, target, near(span)])
            pl.when(target != z)(lambda: to_z(index, target, span).start())

        both(shared_reduce(index, target), make)

    def final_shared(index):
        return remote(f_buf.at[index, 0], f_buf.at[index, 1], fx_ss.at[index], fx_rs.at[index], x_side)

    def final_split(index):
        mine = out_ref.at[index, 2 * c + x]
        return remote(mine, mine, fx_ss.at[index], fx_rs.at[index], x_side)

    def final_c(index):
        pair = out_ref.at[index, pl.ds(2 * c, 2)]
        return remote(pair, pair, fc_ss.at[index], fc_rs.at[index], c_side)

    def stage_z(step):
        index = mats - 1 - step

        def make(span):
            def one(source):
                pl.when(source != z)(lambda: from_z(index, source, span))

            loop(0, z_count, one)
            part_ref[near(span)] = grad_ref[index, local(span), z, y].astype(single)

            def more(source):
                @pl.when(source != z)
                def _():
                    part_ref[near(span)] = part_ref[near(span)] + z_buf[index, near(span), source].astype(single)

            loop(0, z_count, more)

        shared = shared_reduce(index, z)
        both(shared, make)

        @pl.when(shared)
        def _():
            f_buf[index, 0] = part_ref[...].astype(bfloat)
            final_shared(index).start()

        @pl.when(otherwise(shared))
        def _():
            out_ref[index, pl.ds(2 * c + x, 1)] = part_ref[pl.ds(x, 1)].astype(bfloat)
            final_split(index).start()

    def stage_f(step):
        index = mats - 1 - step
        shared = shared_reduce(index, z)

        @pl.when(shared)
        def _():
            final_shared(index).wait_recv()
            total = f_buf[index, 0].astype(single) + f_buf[index, 1].astype(single)
            out_ref[index, pl.ds(2 * c, 2)] = total.astype(bfloat)

        @pl.when(otherwise(shared))
        def _():
            final_split(index).wait_recv()

        final_c(index).start()

    def reduce_tick(step):
        for lag, stage in zip(REDUCE, (stage_c, stage_x, stage_y)):
            unit = step - lag
            pl.when(jnp.logical_and(unit >= 0, unit < units))(functools.partial(stage, unit))
        for lag, stage in zip(REDUCE[3:], (stage_z, stage_f)):
            turn = step - lag
            whole = lax.div(turn, z_count)
            pl.when(jnp.logical_and(jnp.logical_and(turn >= 0, turn < units), turn == whole * z_count + z_count - 1))(
                functools.partial(stage, whole)
            )

    def spread_ticks(first, count, turn, turns):
        each = -(-count // turns)

        def one(step):
            mine = turn * each + step
            pl.when(mine < count)(lambda: reduce_tick(first + mine))

        loop(0, each, one)

    def small_step(stage):
        if stage == 0:
            remote(small_ref, s_c, s_ss.at[0], s_rs.at[0], c_side).start()
        elif stage == 1:
            remote(small_ref, s_c, s_ss.at[0], s_rs.at[0], c_side).wait_recv()
            s_cur[0] = small_ref[...] + s_c[...]
            remote(s_cur.at[0], s_x, s_ss.at[1], s_rs.at[1], x_side).start()
        elif stage == 2:
            remote(s_cur.at[0], s_x, s_ss.at[1], s_rs.at[1], x_side).wait_recv()
            s_cur[1] = s_cur[0] + s_x[...]
            remote(s_cur.at[1], s_y, s_ss.at[2], s_rs.at[2], y_side).start()
        elif stage == 3:
            remote(s_cur.at[1], s_y, s_ss.at[2], s_rs.at[2], y_side).wait_recv()
            s_z[z] = s_cur[1] + s_y[...]

            def send(step, carry):
                other = lax.rem(z + step, z_count)
                remote(s_z.at[z], s_z.at[z], s_ss.at[3 + other], s_rs.at[3 + z], device(other, y, x, c)).start()
                return carry

            lax.fori_loop(1, z_count, send, 0)
        else:

            def wait(step, carry):
                other = lax.rem(z + step, z_count)
                remote(s_z.at[other], s_z.at[other], s_ss.at[3 + other], s_rs.at[3 + other], device(other, y, x, c)).wait_recv()
                return carry

            lax.fori_loop(1, z_count, wait, 0)

            def gather(step, carry):
                return carry + s_z[step]

            total_ref[...] = lax.fori_loop(0, z_count, gather, jnp.zeros(total_ref.shape, single))


    def home(index, carry):
        for block in range(2):
            w_ref[index, 2 * c + block, z, y] = shard_ref[index, 2 * c + block]
        return carry

    lax.fori_loop(0, mats, home, 0)
    for first in range(AHEAD):
        own(matrix_at(first))

    tags_row = meta_ref[0:1, :]
    counts_row = meta_ref[1:2, :]
    columns = meta_ref[...].T
    tags_col = columns[:, 0:1]
    counts_col = columns[:, 1:2]

    group_col = lax.broadcasted_iota(jnp.int32, (rows, groups), 1).astype(single)
    onehot = (group_col == tags_col).astype(single)
    x_ref[...] = lax.dot_general(
        onehot, table_ref[...], (((1,), (0,)), ((), ())), precision=highest, preferred_element_type=single
    )
    for entry in range(entries):
        at = entry * SLOTS
        x_ref[at : at + PIECES, :] = x_ref[at : at + PIECES, :] + pieces_ref[entry].astype(single)

    row_at = lax.broadcasted_iota(jnp.int32, (half, 2 * half), 0)
    key_at = lax.rem(lax.broadcasted_iota(jnp.int32, (half, 2 * half), 1), half)
    same = lax.div(row_at, SLOTS) == lax.div(key_at, SLOTS)
    key_slot = lax.rem(key_at, SLOTS).astype(single)
    low_lane = lax.broadcasted_iota(jnp.int32, (half, 128), 1) < HD

    def key_mask(part):
        piece = counts_row[:, part * half : (part + 1) * half]
        counts_here = jnp.concatenate([piece, piece], axis=1)
        return jnp.logical_and(same, key_slot < counts_here)

    def split_pair(values):
        zero = jnp.zeros_like(values)
        return jnp.concatenate([jnp.where(low_lane, values, zero), jnp.where(low_lane, zero, values)], axis=0)

    def front(layer):
        values = x_ref[...]
        unit, scale = normalize(values)
        unit_ref[2 * layer] = unit
        scale_ref[2 * layer] = scale
        a = (unit * gain_ref[2 * layer] + bias_ref[2 * layer]).astype(bfloat)
        a_ref[layer] = a
        for part in range(3):
            qkv_ref[layer, part] = dot_nn(a, block_of(3 * layer, part)).astype(bfloat)
        for part in range(2):
            mask = key_mask(part)
            here = slice(part * half, (part + 1) * half)
            for pair in range(pairs):
                lanes = slice(pair * 128, (pair + 1) * 128)
                q = qkv_ref[layer, 0, here, lanes]
                keys = split_pair(qkv_ref[layer, 1, here, lanes])
                vals = split_pair(qkv_ref[layer, 2, here, lanes])
                scores = dot_nt(q, keys) * HD ** (-0.5)
                scores = jnp.where(mask, scores, masked_score)
                probs = []
                for head in range(2):
                    mine = scores[:, head * half : (head + 1) * half]
                    top = jnp.max(mine, axis=-1, keepdims=True)
                    raised = jnp.exp(mine - top)
                    probs.append(raised / jnp.sum(raised, axis=-1, keepdims=True))
                prob = jnp.concatenate(probs, axis=1)
                prob_ref[layer, part * pairs + pair] = prob
                o_ref[layer, here, lanes] = dot_nn(prob.astype(bfloat), vals).astype(bfloat)
        middle = values + dot_nt(o_ref[layer], block_of(3 * layer, 3))
        unit, scale = normalize(middle)
        unit_ref[2 * layer + 1] = unit
        scale_ref[2 * layer + 1] = scale
        b_ref[layer] = (unit * gain_ref[2 * layer + 1] + bias_ref[2 * layer + 1]).astype(bfloat)
        x_ref[...] = middle

    def rise(layer):
        def hidden(block, carry):
            u = dot_nn(b_ref[layer], block_of(3 * layer + 1, block))
            gate = 0.5 * (1.0 + lax.erf(u * math.sqrt(0.5)))
            g_ref[layer, block] = (u * gate).astype(bfloat)
            slope_ref[layer, block] = gate + u * (jnp.exp(-0.5 * u * u) * (1.0 / math.sqrt(2.0 * math.pi)))
            return carry

        lax.fori_loop(0, BLOCKS, hidden, 0)

    def fall(layer):
        def hidden(block, carry):
            x_ref[...] += dot_nt(g_ref[layer, block], block_of(3 * layer + 2, block))
            return carry

        lax.fori_loop(0, BLOCKS, hidden, 0)

    def project():
        total = jnp.zeros((entries, width), single)
        for block in range(BLOCKS):
            total += dot_nt(cot_ref[:, block * width : (block + 1) * width], block_of(proj, block))
        dpool_ref[...] = total

    depth = LAGS[-1]

    def gather_tick(step, carry):
        @pl.when(step + AHEAD < mats)
        def _():
            own(matrix_at(step + AHEAD))

        for lag, stage in zip((0, *LAGS), (line, beside, opposite, finish)):
            turn = step - lag
            pl.when(jnp.logical_and(turn >= 0, turn < mats))(lambda: stage(matrix_at(turn)))
        index = matrix_at(step - depth)
        layer = lax.div(index, 3)
        ready = jnp.logical_and(step >= depth, index < proj)
        for kind, work in enumerate((front, rise, fall)):
            pl.when(jnp.logical_and(ready, lax.rem(index, 3) == kind))(lambda: work(layer))
        pl.when(jnp.logical_and(step >= depth, index == proj))(project)
        return carry

    lax.fori_loop(0, mats + depth, gather_tick, 0)


    unit, scale = normalize(x_ref[...])
    normed = unit * gain_ref[final] + bias_ref[final]
    slot_col = lax.rem(lax.broadcasted_iota(jnp.int32, (rows, 1), 0), SLOTS).astype(single)
    used_col = (slot_col < counts_col).astype(single)
    pooled = jnp.sum((normed * used_col).reshape(entries, SLOTS, width), axis=1)
    counts_entry = counts_col.reshape(entries, SLOTS, 1)[:, 0, :]
    pooled_low = (pooled / counts_entry).astype(bfloat)
    for block in range(BLOCKS):
        lanes = slice(block * width, (block + 1) * width)
        emb_ref[:, lanes] = dot_nn(pooled_low, block_of(proj, block))
        put_grad(proj, block, dot_tn(pooled_low, cot_ref[:, lanes]))
    lax.fori_loop(0, mats, lambda index, carry: (gather_sent(index), carry)[1], 0)
    start_matrix(proj)
    grad_pooled = dpool_ref[...] / counts_entry
    grad_normed = jnp.broadcast_to(grad_pooled[:, None, :], (entries, SLOTS, width)).reshape(rows, width) * used_col
    small_ref[...] = jnp.zeros_like(small_ref)
    small_ref[pl.ds(final, 1), :] = jnp.sum(grad_normed * unit, axis=0, keepdims=True)
    small_ref[pl.ds(SLOTS + final, 1), :] = jnp.sum(grad_normed, axis=0, keepdims=True)
    acc_ref[...] = normalize_back(grad_normed, unit, scale, gain_ref[final])

    def backward(step, carry):
        layer = layers - 1 - step
        tick = 3 * z_count * step
        grad_next = acc_ref[...]
        do_ref[...] = grad_next.astype(bfloat)
        turn_ref[0] = grad_next.T.astype(bfloat)
        turn_ref[1] = b_ref[layer].astype(single).T.astype(bfloat)
        x_ref[...] = jnp.zeros_like(x_ref)

        def hidden(block, carry):
            put_grad(3 * layer + 2, block, dot_nn(turn_ref[0], g_ref[layer, block]))
            grad_act = dot_nn(do_ref[...], block_of(3 * layer + 2, block))
            du = (grad_act * slope_ref[layer, block]).astype(bfloat)
            put_grad(3 * layer + 1, block, dot_nn(turn_ref[1], du))
            x_ref[...] += dot_nt(du, block_of(3 * layer + 1, block))
            spread_ticks(tick, z_count, block, BLOCKS)
            return carry

        lax.fori_loop(0, BLOCKS, hidden, 0)
        start_matrix(3 * layer + 2)
        start_matrix(3 * layer + 1)
        grad_b = x_ref[...]
        unit = unit_ref[2 * layer + 1]
        small_ref[pl.ds(2 * layer + 1, 1), :] = jnp.sum(grad_b * unit, axis=0, keepdims=True)
        small_ref[pl.ds(SLOTS + 2 * layer + 1, 1), :] = jnp.sum(grad_b, axis=0, keepdims=True)
        grad_middle = grad_next + normalize_back(grad_b, unit, scale_ref[2 * layer + 1], gain_ref[2 * layer + 1])
        acc_ref[...] = grad_middle
        dy = grad_middle.astype(bfloat)
        put_grad(3 * layer, 3, dot_nn(grad_middle.T.astype(bfloat), o_ref[layer]))
        do_ref[...] = dot_nn(dy, block_of(3 * layer, 3)).astype(bfloat)

        def attend(pair, carry):
            lanes = pl.ds(pl.multiple_of(pair * 128, 128), 128)
            for part in range(2):
                here = slice(part * half, (part + 1) * half)
                q = qkv_ref[layer, 0, here, lanes]
                keys = split_pair(qkv_ref[layer, 1, here, lanes])
                vals = split_pair(qkv_ref[layer, 2, here, lanes])
                do = do_ref[here, lanes]
                prob = prob_ref[layer, part * pairs + pair]
                grad_prob = dot_nt(do, vals)
                product = grad_prob * prob
                scored = []
                for head in range(2):
                    spans = slice(head * half, (head + 1) * half)
                    total = jnp.sum(product[:, spans], axis=-1, keepdims=True)
                    scored.append(product[:, spans] - prob[:, spans] * total)
                ds_low = jnp.concatenate(scored, axis=1).astype(bfloat)
                dv = dot_tn(prob.astype(bfloat), do)
                dk = dot_tn(ds_low, q)
                dq = dot_nn(ds_low, keys)
                dqkv_ref[0, here, lanes] = (dq * HD ** (-0.5)).astype(bfloat)
                dqkv_ref[1, here, lanes] = (jnp.where(low_lane, dk[:half], dk[half:]) * HD ** (-0.5)).astype(bfloat)
                dqkv_ref[2, here, lanes] = jnp.where(low_lane, dv[:half], dv[half:]).astype(bfloat)
            spread_ticks(tick + z_count, 2 * z_count, pair, pairs)
            return carry

        lax.fori_loop(0, pairs, attend, 0)
        turned = a_ref[layer].astype(single).T.astype(bfloat)
        grad_a = jnp.zeros((rows, width), single)
        for part in range(3):
            put_grad(3 * layer, part, dot_nn(turned, dqkv_ref[part]))
            grad_a += dot_nt(dqkv_ref[part], block_of(3 * layer, part))
        start_matrix(3 * layer)
        unit = unit_ref[2 * layer]
        small_ref[pl.ds(2 * layer, 1), :] = jnp.sum(grad_a * unit, axis=0, keepdims=True)
        small_ref[pl.ds(SLOTS + 2 * layer, 1), :] = jnp.sum(grad_a, axis=0, keepdims=True)
        acc_ref[...] += normalize_back(grad_a, unit, scale_ref[2 * layer], gain_ref[2 * layer])
        return carry

    lax.fori_loop(0, layers, backward, 0)
    group_row = lax.broadcasted_iota(jnp.int32, (groups, rows), 0).astype(single)
    spread = (group_row == tags_row).astype(single)
    small_ref[2 * SLOTS : 2 * SLOTS + groups, :] = lax.dot_general(
        spread, acc_ref[...], (((1,), (0,)), ((), ())), precision=highest, preferred_element_type=single
    )
    small_step(0)
    for entry in range(entries):
        at = entry * SLOTS
        dx_ref[entry] = acc_ref[at : at + PIECES, :]

    def tail_tick(step, carry):
        reduce_tick(step)
        return carry

    last = units - z_count
    small_step(1)
    lax.fori_loop(last, last + 2, tail_tick, 0)
    small_step(2)
    lax.fori_loop(last + 2, last + 4, tail_tick, 0)
    small_step(3)
    lax.fori_loop(last + 4, units + REDUCE[-1], tail_tick, 0)
    small_step(4)

    def arrive(index, carry):
        pair = out_ref.at[index, pl.ds(2 * (1 - c), 2)]
        remote(pair, pair, fc_ss.at[index], fc_rs.at[index], c_side).wait_recv()
        return carry

    lax.fori_loop(0, mats, arrive, 0)

    def squares(index, carry):
        values = out_ref[index].astype(single)
        return carry + jnp.sum(jnp.sum(values * values, axis=0), axis=0, keepdims=True)

    squared = lax.fori_loop(0, mats, squares, jnp.zeros((1, out_ref.shape[3]), single))
    n_buf[me] = jnp.broadcast_to(squared, n_buf.shape[1:])

    def send_norm(step, carry):
        other = lax.rem(me + step, dp)
        remote(n_buf.at[me], n_buf.at[me], n_ss.at[other], n_rs.at[me], (other, x * 2 + c)).start()
        return carry

    lax.fori_loop(1, dp, send_norm, 0)

    def wait_norm(step, carry):
        other = lax.rem(me + step, dp)
        remote(n_buf.at[other], n_buf.at[other], n_ss.at[other], n_rs.at[other], (other, x * 2 + c)).wait_recv()
        return carry

    lax.fori_loop(1, dp, wait_norm, 0)

    def sum_norm(step, carry):
        return carry + n_buf[step]

    spread = lax.fori_loop(0, dp, sum_norm, jnp.zeros(n_buf.shape[1:], single))
    smalls = total_ref[...]
    norm_ref[...] = jnp.broadcast_to(
        jnp.sum(spread[0:1], axis=1, keepdims=True) + jnp.sum(jnp.sum(smalls * smalls, axis=0, keepdims=True), axis=1, keepdims=True),
        norm_ref.shape,
    )

    def done_unit(unit, carry):
        index, target = order(unit)
        to_c(index, target).wait_send()
        shared = shared_reduce(index, target)
        when(otherwise(shared), lambda: to_x(index, target).wait_send())

        def make(span):
            to_y(index, target, span).wait_send()
            pl.when(target != z)(lambda: to_z(index, target, span).wait_send())

        both(shared, make)
        return carry

    lax.fori_loop(0, units, done_unit, 0)

    def done_mat(index, carry):
        shared = shared_reduce(index, z)
        when(shared, lambda: final_shared(index).wait_send())
        when(otherwise(shared), lambda: final_split(index).wait_send())
        final_c(index).wait_send()
        return carry

    lax.fori_loop(0, mats, done_mat, 0)
    remote(small_ref, s_c, s_ss.at[0], s_rs.at[0], c_side).wait_send()
    remote(s_cur.at[0], s_x, s_ss.at[1], s_rs.at[1], x_side).wait_send()
    remote(s_cur.at[1], s_y, s_ss.at[2], s_rs.at[2], y_side).wait_send()

    def done_z(step, carry):
        other = lax.rem(z + step, z_count)
        remote(s_z.at[z], s_z.at[z], s_ss.at[3 + other], s_rs.at[3 + z], device(other, y, x, c)).wait_send()
        return carry

    lax.fori_loop(1, z_count, done_z, 0)

    def done_norm(step, carry):
        other = lax.rem(me + step, dp)
        remote(n_buf.at[me], n_buf.at[me], n_ss.at[other], n_rs.at[me], (other, x * 2 + c)).wait_send()
        return carry

    lax.fori_loop(1, dp, done_norm, 0)


def train_step(pieces, meta, cotangent, packed, gain, bias, table, layers, dp):
    entries, _, width = pieces.shape
    mats, blocks, shard_rows, _ = packed.shape
    rows = entries * SLOTS
    pairs = width // 128
    z_count = dp // 2
    small = (SMALL_ROWS, width)
    vmem = pl.BlockSpec(memory_space=VMEM)
    dma = pltpu.SemaphoreType.DMA
    whole = (mats, blocks, z_count, 2, shard_rows, width)
    return pl.pallas_call(
        functools.partial(step_kernel, layers, z_count),
        out_shape=(
            jax.ShapeDtypeStruct(cotangent.shape, single),
            jax.ShapeDtypeStruct(pieces.shape, single),
            jax.ShapeDtypeStruct(packed.shape, bfloat),
            jax.ShapeDtypeStruct(small, single),
            jax.ShapeDtypeStruct((8, 128), single),
        ),
        in_specs=[vmem] * 7,
        out_specs=(vmem,) * 5,
        scratch_shapes=[
            VMEM(whole, bfloat),
            VMEM(whole, bfloat),
            VMEM((mats, 2, z_count, shard_rows, width), bfloat),
            VMEM((mats, 2, 2, shard_rows, width), bfloat),
            VMEM((2, shard_rows, width), single),
            VMEM((rows, width), single),
            VMEM((2 * layers, rows, width), single),
            VMEM((2 * layers, rows, 1), single),
            VMEM((layers, rows, width), bfloat),
            VMEM((layers, rows, width), bfloat),
            VMEM((layers, 3, rows, width), bfloat),
            VMEM((layers, 2 * pairs, rows // 2, rows), single),
            VMEM((layers, rows, width), bfloat),
            VMEM((layers, BLOCKS, rows, width), bfloat),
            VMEM((layers, BLOCKS, rows, width), single),
            VMEM((3, rows, width), bfloat),
            VMEM((rows, width), bfloat),
            VMEM((rows, width), single),
            VMEM((2, width, rows), bfloat),
            VMEM((entries, width), single),
            VMEM(small, single),
            VMEM(small, single),
            VMEM(small, single),
            VMEM(small, single),
            VMEM((z_count, *small), single),
            VMEM((2, *small), single),
            VMEM((dp, 8, width), single),
            dma((mats, z_count, 2)),
            dma((mats,)),
            dma((mats, 2, z_count, 2)),
            dma((mats,)),
            *[dma((mats, z_count))] * 8,
            *[dma((mats,))] * 4,
            dma((3 + z_count,)),
            dma((3 + z_count,)),
            dma((dp,)),
            dma((dp,)),
            pltpu.SemaphoreType.REGULAR((3, mats)),
        ],
        compiler_params=pltpu.CompilerParams(collective_id=1, has_side_effects=True, vmem_limit_bytes=60 * 2**20),
        name="train_step",
    )(pieces, meta, cotangent, packed, gain, bias, table)


def adam_update(weight, first, second, gradient, clip_scale, decay, step_rate):
    clipped = gradient * clip_scale
    first_new = beta_first * first + (1.0 - beta_first) * clipped
    second_new = beta_second * second + (1.0 - beta_second) * clipped * clipped
    first_hat = first_new / (1.0 - beta_first**STEP)
    second_hat = second_new / (1.0 - beta_second**STEP)
    weight_new = weight - step_rate * (first_hat / (jnp.sqrt(second_hat) + adam_eps) + decay * weight)
    return (weight_new, first_new, second_new)


def pack(qkv, out, up, down, proj):
    layers, _, rows, width = qkv.shape
    parts = []
    front = jnp.concatenate([qkv, jnp.swapaxes(out, 1, 2)[:, None]], axis=1)
    rise = jnp.swapaxes(up.reshape(layers, rows, BLOCKS, width), 1, 2)
    fall = jnp.swapaxes(jnp.swapaxes(down, 1, 2).reshape(layers, rows, BLOCKS, width), 1, 2)
    body = jnp.stack([front, rise, fall], axis=1).reshape(3 * layers, BLOCKS, rows, width)
    last = jnp.swapaxes(proj.reshape(rows, BLOCKS, width), 0, 1)[None]
    return jnp.concatenate([body, last], axis=0)


def unpack(packed, layers):
    _, _, rows, width = packed.shape
    body = packed[: 3 * layers].reshape(layers, 3, BLOCKS, rows, width)
    qkv = body[:, 0, :3]
    out = jnp.swapaxes(body[:, 0, 3], 1, 2)
    up = jnp.swapaxes(body[:, 1], 1, 2).reshape(layers, rows, BLOCKS * width)
    down = jnp.swapaxes(jnp.swapaxes(body[:, 2], 1, 2).reshape(layers, rows, BLOCKS * width), 1, 2)
    proj = jnp.swapaxes(packed[3 * layers], 0, 1).reshape(rows, BLOCKS * width)
    return qkv, out, up, down, proj


def per_device(
    pieces, script_tags, counts, cotangent,
    qkv_weight, qkv_first, qkv_second,
    out_weight, out_first, out_second,
    up_weight, up_first, up_second,
    down_weight, down_first, down_second,
    proj_weight, proj_first, proj_second,
    norm_gain, gain_first, gain_second,
    norm_bias, bias_first, bias_second,
    group_table, table_first, table_second,
):
    layers = qkv_weight.shape[0]
    width = pieces.shape[2]
    dp = lax.axis_size("dp")
    norms = norm_gain.shape[0]
    groups = group_table.shape[0]
    packed = pack(
        qkv_weight.astype(bfloat), out_weight.astype(bfloat), up_weight.astype(bfloat), down_weight.astype(bfloat), proj_weight.astype(bfloat)
    )
    meta = jnp.stack([jnp.repeat(script_tags, SLOTS), jnp.repeat(counts, SLOTS)]).astype(single)
    meta = jnp.concatenate([meta, jnp.zeros((SLOTS - 2, meta.shape[1]), single)], axis=0)
    embeddings, input_grad, reduced, small_total, square_total = train_step(
        pieces, meta, cotangent, packed,
        norm_gain.reshape(norms, 1, width), norm_bias.reshape(norms, 1, width), group_table, layers, dp,
    )
    grad_norm = jnp.sqrt(square_total[0, 0])
    clip_scale = jnp.minimum(1.0, clip_level / (grad_norm + 1e-06))
    grad_qkv, grad_out, grad_up, grad_down, grad_proj = unpack(reduced.astype(single), layers)
    grad_gain = small_total[:norms]
    grad_bias = small_total[SLOTS : SLOTS + norms]
    grad_table = small_total[2 * SLOTS : 2 * SLOTS + groups]
    big = functools.partial(adam_update, clip_scale=clip_scale, decay=decay_rate, step_rate=learn_rate)
    little = functools.partial(adam_update, clip_scale=clip_scale, decay=0.0, step_rate=small_rate)
    return (
        embeddings,
        input_grad,
        grad_norm,
        *big(qkv_weight, qkv_first, qkv_second, grad_qkv),
        *big(out_weight, out_first, out_second, grad_out),
        *big(up_weight, up_first, up_second, grad_up),
        *big(down_weight, down_first, down_second, grad_down),
        *big(proj_weight, proj_first, proj_second, grad_proj),
        *little(norm_gain, gain_first, gain_second, grad_gain),
        *little(norm_bias, bias_first, bias_second, grad_bias),
        *little(group_table, table_first, table_second, grad_table),
    )


def solution(mesh):
    entry_split = ("dp", "mp")
    weight_specs = (P(None, None, "dp", None), P(None, None, "dp"), P(None, "dp", None), P(None, None, "dp"), P("dp", None))
    state = tuple(spec for spec in weight_specs for _ in range(3)) + (P(),) * 9
    return jax.shard_map(
        per_device,
        mesh=mesh,
        in_specs=(P(entry_split, None, None), P(entry_split), P(entry_split), P(entry_split, None)) + state,
        out_specs=(P(entry_split, None), P(entry_split, None, None), P()) + state,
        check_vma=False,
    )
```

time: 324 us -> 238 us (0.73)
  Pallas kernels: 286 us -> 200 us
    pallas_call x3 -> x1, Pallas kernels: 286 us -> 200 us  [train_step(): pl.pallas_call(functools.partial(step_kernel, layers, z_count), out_shape...]
    unnamed x52 -> x55, local copies, waits for them, and re-layouts: 9.46 us -> 10.2 us
where the time goes in v2:
time: 238 us; the launch traced here: 237 us
  Pallas kernels  200 us (84%)
  local copies, waits for them, and re-layouts  18.6 us (8%)
  other arithmetic  16.2 us (7%)
  between operations  2.87 us (1%)
    pallas_call x1, Pallas kernels, train_step(): pl.pallas_call(functools.partial(step_kernel, layers, z_count), out_shape...  200 us
    sub x7, other arithmetic, adam_update(): weight - step_rate * (first_hat / (jnp.sqrt(second_hat) + adam_eps) + dec...  11.5 us
    unnamed x55, local copies, waits for them, and re-layouts  10.2 us

profile of v2, /device:TPU:0, one launch (start us, length us, event | category | flops | bytes accessed | tf_op | source)
XLA Modules:
  0.0 237.4 jit_solution(10779999496961685401)
XLA Ops:
  0.7 0.0 copy-start.3
  0.7 1.4 reshape.99.gain_ref
  2.1 1.3 reshape.100.bias_ref
  3.4 0.7 broadcast_in_dim.13
  4.1 0.1 stack_reshape.6
  4.2 0.7 broadcast_in_dim.14
  4.9 0.1 stack_reshape.7
  5.0 0.6 concatenate.9.meta_ref
  5.7 1.0 convert_bitcast_fusion
  6.6 1.8 copy.70.pieces_ref
  8.4 1.2 convert_element_type.26
  9.6 0.0 copy-done.3
  9.6 0.0 copy-start.2
  9.6 0.1 convert_element_type.22
  9.7 0.1 maximum_bitcast_fusion
  9.7 0.1 copy-done.1
  9.8 0.1 convert_element_type.24
  9.9 1.0 copy-done.2
  10.9 0.1 convert_element_type.25
  10.9 0.1 bitcast_bitcast_fusion
  11.0 0.2 pad_maximum_fusion.1
  11.2 0.1 copy.68
  11.3 1.4 pad_maximum_fusion.shard_ref
  12.8 0.0 copy-start.24
  12.8 0.0 copy-start.25
  12.8 0.0 copy-start.17
  12.8 0.0 copy-start.20
  12.8 0.0 copy-start.21
  12.8 199.7 %train_step.1 = (f32[32,2048]{1,0:T(8,128)}, f32[32,7,512]{2,1,0:T(8,128)}, bf16[7,4,64,512]{3,2,1,0:T(8,128)(2,1)}, f32[32,512]{1,0:T(8,128)}, f32[8,128]{1,0:T(8,128)}) custom-call(bf16[32,7,512]{2,1,0:T(8,128)(2,1)} %copy.70.pieces_ref, f32[8,256]{1,0:T(8,128)} %concatenate.9.meta_ref, bf16[32,2048]{1,0:T(8,128)(2,1)} %cot_ref.1, ...), custom_call_target="tpu_custom_call" | custom-call | tf_op jit(solution)/shard_map/train_step/pallas_call | solution.py:800
  212.5 1.2 slice.30
  214.4 0.0 copy-done.18
  214.4 0.0 copy-done.19
  214.4 0.0 copy-done.22
  214.4 0.0 copy-done.23
  214.5 0.0 copy-done.24
  214.5 0.0 copy-done.25
  214.5 1.4 multiply_subtract_fusion.6
  215.9 0.0 copy-done.17
  215.9 1.4 multiply_subtract_fusion.5
  217.3 2.1 copy.76
  219.4 1.9 slice.40
  221.3 1.0 multiply_subtract_fusion.4
  222.3 0.7 copy-done
  223.1 0.5 convert_element_type.27
  223.6 0.0 copy-start.4
  223.6 0.0 copy-start.12
  223.6 0.0 copy-start.13
  223.7 0.9 copy-done.4
  224.6 0.2 copy-done.12
  224.8 0.2 copy-done.13
  224.9 1.4 multiply_subtract_fusion.3
  226.3 0.2 fusion.2
  226.6 0.9 copy-done.10
  227.5 0.2 copy-done.11
  227.7 1.8 multiply_subtract_fusion.2
  229.5 0.1 copy.83
  229.6 0.1 copy.82
  229.7 1.0 copy-done.5
  230.8 0.3 copy-done.6
  231.1 2.2 multiply_subtract_fusion.1
  233.3 0.0 copy-done.8
  233.3 2.2 multiply_subtract_fusion
  235.5 0.0 copy-done.14
  235.5 0.7 copy.90
  (26 shorter events, 0.1 us)
Async XLA Ops:
  0.7 8.9 %copy-start.3 = (f32[2,3,64,512]{3,2,1,0:T(8,128)S(1)}, f32[2,3,64,512]{3,2,1,0:T(8,128)}, u32[]{:S(2)}) copy-start(f32[2,3,64,512]{3,2,1,0:T(8,128)} %param.32) | copy-start | bytes 2359300
  8.4 1.4 copy-start.1
  9.6 1.3 copy-start.2
  12.8 201.7 %copy-start.18 = (f32[5,512]{1,0:T(8,128)S(1)}, f32[5,512]{1,0:T(8,128)}, u32[]{:S(2)}) copy-start(f32[5,512]{1,0:T(8,128)} %param.47) | copy-start | bytes 30724
  12.8 201.7 %copy-start.19 = (f32[5,512]{1,0:T(8,128)S(1)}, f32[5,512]{1,0:T(8,128)}, u32[]{:S(2)}) copy-start(f32[5,512]{1,0:T(8,128)} %param.50) | copy-start | bytes 30724
  12.8 201.7 %copy-start.22 = (f32[5,512]{1,0:T(8,128)S(1)}, f32[5,512]{1,0:T(8,128)}, u32[]{:S(2)}) copy-start(f32[5,512]{1,0:T(8,128)} %param.51) | copy-start | bytes 30724
  12.8 201.7 %copy-start.23 = (f32[5,512]{1,0:T(8,128)S(1)}, f32[5,512]{1,0:T(8,128)}, u32[]{:S(2)}) copy-start(f32[5,512]{1,0:T(8,128)} %param.52) | copy-start | bytes 30724
  12.8 201.7 %copy-start.24 = (f32[5,512]{1,0:T(8,128)S(1)}, f32[5,512]{1,0:T(8,128)}, u32[]{:S(2)}) copy-start(f32[5,512]{1,0:T(8,128)} %param.49) | copy-start | bytes 30724
  12.8 201.7 %copy-start.25 = (f32[5,512]{1,0:T(8,128)S(1)}, f32[5,512]{1,0:T(8,128)}, u32[]{:S(2)}) copy-start(f32[5,512]{1,0:T(8,128)} %param.48) | copy-start | bytes 30724
  12.8 203.1 %copy-start.17 = (f32[16,512]{1,0:T(8,128)S(1)}, f32[16,512]{1,0:T(8,128)}, u32[]{:S(2)}) copy-start(f32[16,512]{1,0:T(8,128)} %table_ref.1) | copy-start | bytes 98308
  12.8 203.1 %copy-start.20 = (f32[16,512]{1,0:T(8,128)S(1)}, f32[16,512]{1,0:T(8,128)}, u32[]{:S(2)}) copy-start(f32[16,512]{1,0:T(8,128)} %param.54) | copy-start | bytes 98308
  12.8 203.1 %copy-start.21 = (f32[16,512]{1,0:T(8,128)S(1)}, f32[16,512]{1,0:T(8,128)}, u32[]{:S(2)}) copy-start(f32[16,512]{1,0:T(8,128)} %param.55) | copy-start | bytes 98308
  219.4 1.9 copy-start.9
  219.4 1.9 copy-start.15
  219.4 1.9 copy-start.16
  221.3 1.8 copy-start
  223.6 1.0 copy-start.4
  223.6 1.2 copy-start.12
  223.6 1.3 copy-start.13
  226.3 1.1 copy-start.10
  226.3 1.4 copy-start.11
  229.5 1.2 copy-start.5
  229.5 1.5 copy-start.6
  231.1 2.2 copy-start.7
  231.1 2.2 copy-start.8
  233.3 2.2 copy-start.14

commit v3 on v2

--- a/solution.py
+++ b/solution.py
@@ -50,7 +50,7 @@
     remote(dst, dst, send_sem, recv_sem, target).wait_recv()
 
 
-def greet(z_count, whole_dp):
+def greet(z_count):
     z, y, x, c = place()
     barrier = pltpu.get_barrier_semaphore()
 
@@ -59,22 +59,15 @@
 
     signal(device(z, y, 1 - x, c))
     signal(device(z, y, x, 1 - c))
-    if whole_dp:
-        dp = 2 * z_count
-
-        def one(step):
-            signal((lax.rem(z * 2 + y + step, dp), x * 2 + c))
-
-        loop(1, dp, one)
-        pl.semaphore_wait(barrier, dp + 1)
-    else:
-        signal(device(z, 1 - y, x, c))
-
-        def one(step):
-            signal(device(lax.rem(z + step, z_count), y, x, c))
-
-        loop(1, z_count, one)
-        pl.semaphore_wait(barrier, z_count + 2)
+    dp = 2 * z_count
+
+    def one(step):
+        other = lax.rem(z * 2 + y + step, dp)
+        signal((other, x * 2 + c))
+        signal((other, x * 2 + 1 - c))
+
+    loop(1, dp, one)
+    return lambda: pl.semaphore_wait(barrier, 2 * dp)
 
 
 def when(condition, body):
@@ -139,32 +132,81 @@
 
 AHEAD = 2
 LAGS = (1, 2, 3)
-REDUCE = (0, 2, 4, 6, 8)
+REDUCE = (0, 3, 6, 8, 9, 11)
+SHIFT = 0
+MARKS = (2, 5, 8, 11)
 
 
 def step_kernel(
     layers, z_count,
-    pieces_ref, meta_ref, cot_ref, shard_ref, gain_ref, bias_ref, table_ref,
-    emb_ref, dx_ref, out_ref, total_ref, norm_ref,
+    pieces_hbm, tags_hbm, counts_hbm, cot_hbm, qkv_hbm, outward_hbm, rise_hbm, fall_hbm, proj_hbm, gain_hbm, bias_hbm, table_hbm,
+    emb_hbm, dx_hbm, out_ref, total_ref, norm_ref,
+    pieces_ref, tags_ref, counts_ref, cot_ref, gain_ref, bias_ref, table_ref, emb_ref, dx_ref, sum_ref,
     w_ref, grad_ref, z_buf, f_buf, part_ref,
     x_ref, unit_ref, scale_ref, a_ref, b_ref, qkv_ref, prob_ref, o_ref, g_ref, slope_ref, dqkv_ref, do_ref, acc_ref, turn_ref, dpool_ref,
     small_ref, s_c, s_x, s_y, s_z, s_cur, n_buf,
     gx_ss, gc_ss, g_rs, gc_rs,
     c_ss, c_rs, x_ss, x_rs, y_ss, y_rs, z_ss, z_rs, fx_ss, fx_rs, fc_ss, fc_rs, s_ss, s_rs, n_ss, n_rs, credit,
+    in_sem, load_sem, store_sem,
 ):
     mats = 3 * layers + 1
     proj = 3 * layers
     final = 2 * layers
-    entries, _, width = pieces_ref.shape
+    _, entries, width = pieces_ref.shape
     rows = entries * SLOTS
     half = rows // 2
+    group = entries // 2
     groups = table_ref.shape[0]
     pairs = width // 128
     dp = 2 * z_count
+    shard_rows = out_ref.shape[2]
     z, y, x, c = place()
     me = z * 2 + y
     y_side, x_side, c_side = device(z, 1 - y, x, c), device(z, y, 1 - x, c), device(z, y, x, 1 - c)
-    greet(z_count, True)
+    all_here = greet(z_count)
+
+
+    inputs = [
+        pltpu.make_async_copy(src, dst, in_sem.at[at])
+        for at, (src, dst) in enumerate(
+            (
+                (tags_hbm, tags_ref), (counts_hbm, counts_ref), (pieces_hbm, pieces_ref), (table_hbm, table_ref),
+                (gain_hbm, gain_ref), (bias_hbm, bias_ref), (cot_hbm, cot_ref),
+            )
+        )
+    ]
+
+    def shard_slot(index, block):
+        at = 2 * index + block
+        return slope_ref.at[at % layers, at // layers % BLOCKS, pl.ds(at // (layers * BLOCKS) * shard_rows, shard_rows)]
+
+    def load(index, block, src):
+        return pltpu.make_async_copy(src, shard_slot(index, block), load_sem.at[index, block])
+
+    def each_load(act):
+        for first in range(mats):
+            index = gather_order[first]
+            layer, kind = divmod(index, 3)
+            for block in range(2):
+                if index == proj or kind:
+                    source = proj_hbm if index == proj else (rise_hbm, fall_hbm)[kind - 1].at[layer]
+                    act(index, block, load(index, block, source.at[:, pl.ds(pl.multiple_of((2 * c + block) * width, width), width)]))
+                else:
+                    choice = (qkv_hbm.at[layer, block], qkv_hbm.at[layer, 2] if block == 0 else outward_hbm.at[layer])
+                    for core in range(2):
+                        pl.when(c == core)(functools.partial(act, index, block, load(index, block, choice[core])))
+
+    gather_order = [*range(3 * (layers - 1)), proj, *range(3 * (layers - 1), proj)]
+
+    def place_block(index, block, copy):
+        copy.wait()
+        w_ref[index, 2 * c + block, z, y] = shard_slot(index, block)[...].astype(bfloat)
+
+    each_load(lambda index, block, copy: copy.start())
+    for copy in inputs:
+        copy.start()
+    each_load(place_block)
+    all_here()
 
 
     def matrix_at(turn):
@@ -178,12 +220,12 @@
 
     def gather_z(index, other, span):
         return remote(
-            shard_ref.at[index, span], w_ref.at[index, span, z, y], z_ss.at[index, other], g_rs.at[index, 0, z, y], device(other, y, x, c)
+            w_ref.at[index, span, z, y], w_ref.at[index, span, z, y], z_ss.at[index, other], g_rs.at[index, 0, z, y], device(other, y, x, c)
         )
 
-    def gather_y(index, zz, span, src=None):
+    def gather_y(index, zz, span):
         spot = w_ref.at[index, span, zz, y]
-        return remote(spot if src is None else src, spot, y_ss.at[index, zz], g_rs.at[index, 0, zz, y], y_side)
+        return remote(spot, spot, y_ss.at[index, zz], g_rs.at[index, 0, zz, y], y_side)
 
     def gather_x(index, zz, yy, span):
         spot = w_ref.at[index, span, zz, yy]
@@ -198,7 +240,7 @@
 
     def own(index):
         def send(span, cross):
-            gather_y(index, z, span, shard_ref.at[index, span]).start()
+            gather_y(index, z, span).start()
 
             def one(other):
                 pl.when(other != z)(lambda: gather_z(index, other, span).start())
@@ -288,29 +330,46 @@
 
     def to_c(index, target):
         return remote(
-            grad_ref.at[index, pl.ds(2 * (1 - c), 2), target], w_ref.at[index, pl.ds(0, 2), target],
+            grad_ref.at[index, pl.ds(2 * (1 - c), 2), target], w_ref.at[index, pl.ds(2 * c, 2), target],
             c_ss.at[index, target], c_rs.at[index, target], c_side,
         )
 
+    def from_c(index, target):
+        await_arrival(w_ref.at[index, pl.ds(2 * (1 - c), 2), target], c_ss.at[index, target], c_rs.at[index, target], c_side)
+
     def to_x(index, target):
         return remote(
-            grad_ref.at[index, 2 * c + 1 - x, target], w_ref.at[index, 2, target], x_ss.at[index, target], x_rs.at[index, target], x_side
+            grad_ref.at[index, 2 * c + 1 - x, target], w_ref.at[index, 2 * c, target], x_ss.at[index, target], x_rs.at[index, target], x_side
         )
 
     def to_y(index, target, span):
         return remote(
-            grad_ref.at[index, local(span), target, 1 - y], w_ref.at[index, 3, target, near(span)],
+            grad_ref.at[index, local(span), target, 1 - y], w_ref.at[index, 2 * c + 1, target, near(span)],
             y_ss.at[index, target], y_rs.at[index, target], y_side,
         )
 
+    relays = z_count >= 4
+
+    def at_far_end(target):
+        return jnp.logical_and(relays, jnp.abs(target - z) == z_count - 1)
+
+    def passes_on(target):
+        up = jnp.logical_and(target == z_count - 1, z == 1)
+        down = jnp.logical_and(target == 0, z == z_count - 2)
+        return jnp.logical_and(relays, jnp.logical_or(up, down))
+
     def to_z(index, target, span):
+        far = at_far_end(target)
+        there = jnp.where(far, jnp.where(z == 0, 1, z_count - 2), target)
+        slot = jnp.where(far, there, z)
         return remote(
-            grad_ref.at[index, local(span), target, y], z_buf.at[index, near(span), z],
-            z_ss.at[index, target], z_rs.at[index, z], device(target, y, x, c),
+            grad_ref.at[index, local(span), target, y], z_buf.at[index, near(span), slot],
+            z_ss.at[index, target], z_rs.at[index, slot], device(there, y, x, c),
         )
 
     def from_z(index, source, span):
-        await_arrival(z_buf.at[index, near(span), source], z_ss.at[index, source], z_rs.at[index, source], device(source, y, x, c))
+        other = jnp.where(source == z, jnp.where(z == 1, 0, z_count - 1), source)
+        await_arrival(z_buf.at[index, near(span), source], z_ss.at[index, source], z_rs.at[index, source], device(other, y, x, c))
 
     def both(shared, body):
         when(shared, lambda: body(None))
@@ -319,20 +378,21 @@
     def add(ref, at, extra):
         ref[at] = (ref[at].astype(single) + extra.astype(single)).astype(bfloat)
 
-    def give_credit(index):
-        for kind, side in enumerate((c_side, x_side, y_side)):
+    def give_credit(index, kinds):
+        for kind in kinds:
+            side = (c_side, x_side, y_side)[kind]
             pl.semaphore_signal(credit.at[kind, index], inc=1, device_id=side, device_id_type=MESH)
 
     def start_matrix(index):
-        give_credit(index)
+        give_credit(index, (0,))
         pl.semaphore_wait(credit.at[0, index], 1)
         loop(0, z_count, lambda target: to_c(index, target).start())
 
     def stage_c(unit):
         index, target = order(unit)
-        to_c(index, target).wait_recv()
+        from_c(index, target)
         for block in range(2):
-            add(grad_ref, (index, 2 * c + block, target), w_ref[index, block, target])
+            add(grad_ref, (index, 2 * c + block, target), w_ref[index, 2 * (1 - c) + block, target])
         shared = shared_reduce(index, target)
 
         @pl.when(target == 0)
@@ -349,7 +409,7 @@
         @pl.when(otherwise(shared_reduce(index, target)))
         def _():
             to_x(index, target).wait_recv()
-            add(grad_ref, (index, 2 * c + x, target), w_ref[index, 2, target])
+            add(grad_ref, (index, 2 * c + x, target), w_ref[index, 2 * c, target])
             to_y(index, target, 1).start()
 
     def stage_y(unit):
@@ -357,10 +417,20 @@
 
         def make(span):
             to_y(index, target, span).wait_recv()
-            add(grad_ref, (index, local(span), target, y), w_ref[index, 3, target, near(span)])
-            pl.when(target != z)(lambda: to_z(index, target, span).start())
+            add(grad_ref, (index, local(span), target, y), w_ref[index, 2 * c + 1, target, near(span)])
+            pl.when(jnp.logical_and(target != z, jnp.logical_not(passes_on(target))))(lambda: to_z(index, target, span).start())
 
         both(shared_reduce(index, target), make)
+
+    def stage_r(unit):
+        index, target = order(unit)
+
+        def make(span):
+            from_z(index, z, span)
+            add(grad_ref, (index, local(span), target, y), z_buf[index, near(span), z])
+            to_z(index, target, span).start()
+
+        pl.when(passes_on(target))(lambda: both(shared_reduce(index, target), make))
 
     def final_shared(index):
         return remote(f_buf.at[index, 0], f_buf.at[index, 1], fx_ss.at[index], fx_rs.at[index], x_side)
@@ -377,14 +447,18 @@
         index = mats - 1 - step
 
         def make(span):
+            def sends(source):
+                far = jnp.logical_and(relays, jnp.abs(source - z) == z_count - 1)
+                return jnp.logical_and(source != z, jnp.logical_not(far))
+
             def one(source):
-                pl.when(source != z)(lambda: from_z(index, source, span))
+                pl.when(sends(source))(lambda: from_z(index, source, span))
 
             loop(0, z_count, one)
             part_ref[near(span)] = grad_ref[index, local(span), z, y].astype(single)
 
             def more(source):
-                @pl.when(source != z)
+                @pl.when(sends(source))
                 def _():
                     part_ref[near(span)] = part_ref[near(span)] + z_buf[index, near(span), source].astype(single)
 
@@ -418,12 +492,14 @@
             final_split(index).wait_recv()
 
         final_c(index).start()
+        values = out_ref[index, pl.ds(2 * c, 2)].astype(single)
+        sum_ref[...] += jnp.sum((values * values).reshape(-1, 8, width), axis=0)
 
     def reduce_tick(step):
-        for lag, stage in zip(REDUCE, (stage_c, stage_x, stage_y)):
+        for lag, stage in zip(REDUCE, (stage_c, stage_x, stage_y, stage_r)):
             unit = step - lag
             pl.when(jnp.logical_and(unit >= 0, unit < units))(functools.partial(stage, unit))
-        for lag, stage in zip(REDUCE[3:], (stage_z, stage_f)):
+        for lag, stage in zip(REDUCE[4:], (stage_z, stage_f)):
             turn = step - lag
             whole = lax.div(turn, z_count)
             pl.when(jnp.logical_and(jnp.logical_and(turn >= 0, turn < units), turn == whole * z_count + z_count - 1))(
@@ -475,51 +551,75 @@
             total_ref[...] = lax.fori_loop(0, z_count, gather, jnp.zeros(total_ref.shape, single))
 
 
-    def home(index, carry):
-        for block in range(2):
-            w_ref[index, 2 * c + block, z, y] = shard_ref[index, 2 * c + block]
-        return carry
-
-    lax.fori_loop(0, mats, home, 0)
     for first in range(AHEAD):
         own(matrix_at(first))
-
-    tags_row = meta_ref[0:1, :]
-    counts_row = meta_ref[1:2, :]
-    columns = meta_ref[...].T
-    tags_col = columns[:, 0:1]
-    counts_col = columns[:, 1:2]
-
-    group_col = lax.broadcasted_iota(jnp.int32, (rows, groups), 1).astype(single)
-    onehot = (group_col == tags_col).astype(single)
-    x_ref[...] = lax.dot_general(
+    for copy in inputs:
+        copy.wait()
+    sum_ref[...] = jnp.zeros_like(sum_ref)
+
+    def upright(row):
+        down = lax.broadcasted_iota(jnp.int32, (entries, entries), 0)
+        along = lax.broadcasted_iota(jnp.int32, (entries, entries), 1)
+        return jnp.sum(jnp.where(down == along, row, 0.0), axis=1, keepdims=True)
+
+    def half_of(values, part):
+        return values[part * group : (part + 1) * group]
+
+    def spread_slots(values):
+        return jnp.concatenate([half_of(values, part) for part in range(2) for _ in range(SLOTS)], axis=0)
+
+    def sum_slots(values):
+        sums = []
+        for part in range(2):
+            total = values[part * half : part * half + group]
+            for slot in range(1, SLOTS):
+                at = part * half + slot * group
+                total = total + values[at : at + group]
+            sums.append(total)
+        return jnp.concatenate(sums, axis=0)
+
+    tags_row = tags_ref[...].astype(single)
+    counts_col = upright(counts_ref[...].astype(single))
+    group_col = lax.broadcasted_iota(jnp.int32, (entries, groups), 1).astype(single)
+    onehot = (group_col == upright(tags_row)).astype(single)
+    table_rows = lax.dot_general(
         onehot, table_ref[...], (((1,), (0,)), ((), ())), precision=highest, preferred_element_type=single
     )
-    for entry in range(entries):
-        at = entry * SLOTS
-        x_ref[at : at + PIECES, :] = x_ref[at : at + PIECES, :] + pieces_ref[entry].astype(single)
+    for part in range(2):
+        mine = half_of(table_rows, part)
+        for slot in range(SLOTS):
+            at = part * half + slot * group
+            if slot < PIECES:
+                x_ref[at : at + group, :] = mine + pieces_ref[slot, part * group : (part + 1) * group, :].astype(single)
+            else:
+                x_ref[at : at + group, :] = mine
 
     row_at = lax.broadcasted_iota(jnp.int32, (half, 2 * half), 0)
     key_at = lax.rem(lax.broadcasted_iota(jnp.int32, (half, 2 * half), 1), half)
-    same = lax.div(row_at, SLOTS) == lax.div(key_at, SLOTS)
-    key_slot = lax.rem(key_at, SLOTS).astype(single)
+    same = lax.rem(row_at, group) == lax.rem(key_at, group)
+    key_slot = lax.div(key_at, group).astype(single)
     low_lane = lax.broadcasted_iota(jnp.int32, (half, 128), 1) < HD
 
     def key_mask(part):
-        piece = counts_row[:, part * half : (part + 1) * half]
-        counts_here = jnp.concatenate([piece, piece], axis=1)
+        counts_here = jnp.concatenate([half_of(counts_col, part)] * SLOTS, axis=0)
         return jnp.logical_and(same, key_slot < counts_here)
 
     def split_pair(values):
         zero = jnp.zeros_like(values)
         return jnp.concatenate([jnp.where(low_lane, values, zero), jnp.where(low_lane, zero, values)], axis=0)
+
+    def gain_at(norm):
+        return gain_ref[pl.ds(norm, 1), :]
+
+    def bias_at(norm):
+        return bias_ref[pl.ds(norm, 1), :]
 
     def front(layer):
         values = x_ref[...]
         unit, scale = normalize(values)
         unit_ref[2 * layer] = unit
         scale_ref[2 * layer] = scale
-        a = (unit * gain_ref[2 * layer] + bias_ref[2 * layer]).astype(bfloat)
+        a = (unit * gain_at(2 * layer) + bias_at(2 * layer)).astype(bfloat)
         a_ref[layer] = a
         for part in range(3):
             qkv_ref[layer, part] = dot_nn(a, block_of(3 * layer, part)).astype(bfloat)
@@ -546,7 +646,7 @@
         unit, scale = normalize(middle)
         unit_ref[2 * layer + 1] = unit
         scale_ref[2 * layer + 1] = scale
-        b_ref[layer] = (unit * gain_ref[2 * layer + 1] + bias_ref[2 * layer + 1]).astype(bfloat)
+        b_ref[layer] = (unit * gain_at(2 * layer + 1) + bias_at(2 * layer + 1)).astype(bfloat)
         x_ref[...] = middle
 
     def rise(layer):
@@ -594,24 +694,24 @@
 
 
     unit, scale = normalize(x_ref[...])
-    normed = unit * gain_ref[final] + bias_ref[final]
-    slot_col = lax.rem(lax.broadcasted_iota(jnp.int32, (rows, 1), 0), SLOTS).astype(single)
-    used_col = (slot_col < counts_col).astype(single)
-    pooled = jnp.sum((normed * used_col).reshape(entries, SLOTS, width), axis=1)
-    counts_entry = counts_col.reshape(entries, SLOTS, 1)[:, 0, :]
-    pooled_low = (pooled / counts_entry).astype(bfloat)
+    normed = unit * gain_at(final) + bias_at(final)
+    slot_col = lax.div(lax.rem(lax.broadcasted_iota(jnp.int32, (rows, 1), 0), half), group).astype(single)
+    used_col = (slot_col < spread_slots(counts_col)).astype(single)
+    pooled_low = (sum_slots(normed * used_col) / counts_col).astype(bfloat)
     for block in range(BLOCKS):
         lanes = slice(block * width, (block + 1) * width)
         emb_ref[:, lanes] = dot_nn(pooled_low, block_of(proj, block))
         put_grad(proj, block, dot_tn(pooled_low, cot_ref[:, lanes]))
     lax.fori_loop(0, mats, lambda index, carry: (gather_sent(index), carry)[1], 0)
     start_matrix(proj)
-    grad_pooled = dpool_ref[...] / counts_entry
-    grad_normed = jnp.broadcast_to(grad_pooled[:, None, :], (entries, SLOTS, width)).reshape(rows, width) * used_col
+    give_credit(proj, (1, 2))
+    emb_out = pltpu.make_async_copy(emb_ref, emb_hbm, store_sem.at[0])
+    emb_out.start()
+    grad_normed = spread_slots(dpool_ref[...] / counts_col) * used_col
     small_ref[...] = jnp.zeros_like(small_ref)
     small_ref[pl.ds(final, 1), :] = jnp.sum(grad_normed * unit, axis=0, keepdims=True)
     small_ref[pl.ds(SLOTS + final, 1), :] = jnp.sum(grad_normed, axis=0, keepdims=True)
-    acc_ref[...] = normalize_back(grad_normed, unit, scale, gain_ref[final])
+    acc_ref[...] = normalize_back(grad_normed, unit, scale, gain_at(final))
 
     def backward(step, carry):
         layer = layers - 1 - step
@@ -622,23 +722,30 @@
         turn_ref[1] = b_ref[layer].astype(single).T.astype(bfloat)
         x_ref[...] = jnp.zeros_like(x_ref)
 
-        def hidden(block, carry):
+        def hidden(turn, carry):
+            block = lax.rem(turn + 2 * (1 - c), BLOCKS)
             put_grad(3 * layer + 2, block, dot_nn(turn_ref[0], g_ref[layer, block]))
             grad_act = dot_nn(do_ref[...], block_of(3 * layer + 2, block))
             du = (grad_act * slope_ref[layer, block]).astype(bfloat)
             put_grad(3 * layer + 1, block, dot_nn(turn_ref[1], du))
             x_ref[...] += dot_nt(du, block_of(3 * layer + 1, block))
-            spread_ticks(tick, z_count, block, BLOCKS)
+
+            @pl.when(turn == 1)
+            def _():
+                start_matrix(3 * layer + 2)
+                start_matrix(3 * layer + 1)
+
+            spread_ticks(tick - SHIFT, z_count, turn, BLOCKS)
             return carry
 
         lax.fori_loop(0, BLOCKS, hidden, 0)
-        start_matrix(3 * layer + 2)
-        start_matrix(3 * layer + 1)
+        give_credit(3 * layer + 2, (1, 2))
+        give_credit(3 * layer + 1, (1, 2))
         grad_b = x_ref[...]
         unit = unit_ref[2 * layer + 1]
         small_ref[pl.ds(2 * layer + 1, 1), :] = jnp.sum(grad_b * unit, axis=0, keepdims=True)
         small_ref[pl.ds(SLOTS + 2 * layer + 1, 1), :] = jnp.sum(grad_b, axis=0, keepdims=True)
-        grad_middle = grad_next + normalize_back(grad_b, unit, scale_ref[2 * layer + 1], gain_ref[2 * layer + 1])
+        grad_middle = grad_next + normalize_back(grad_b, unit, scale_ref[2 * layer + 1], gain_at(2 * layer + 1))
         acc_ref[...] = grad_middle
         dy = grad_middle.astype(bfloat)
         put_grad(3 * layer, 3, dot_nn(grad_middle.T.astype(bfloat), o_ref[layer]))
@@ -667,7 +774,7 @@
                 dqkv_ref[0, here, lanes] = (dq * HD ** (-0.5)).astype(bfloat)
                 dqkv_ref[1, here, lanes] = (jnp.where(low_lane, dk[:half], dk[half:]) * HD ** (-0.5)).astype(bfloat)
                 dqkv_ref[2, here, lanes] = jnp.where(low_lane, dv[:half], dv[half:]).astype(bfloat)
-            spread_ticks(tick + z_count, 2 * z_count, pair, pairs)
+            spread_ticks(tick + z_count - SHIFT, 2 * z_count, pair, pairs)
             return carry
 
         lax.fori_loop(0, pairs, attend, 0)
@@ -677,71 +784,71 @@
             put_grad(3 * layer, part, dot_nn(turned, dqkv_ref[part]))
             grad_a += dot_nt(dqkv_ref[part], block_of(3 * layer, part))
         start_matrix(3 * layer)
+        give_credit(3 * layer, (1, 2))
         unit = unit_ref[2 * layer]
         small_ref[pl.ds(2 * layer, 1), :] = jnp.sum(grad_a * unit, axis=0, keepdims=True)
         small_ref[pl.ds(SLOTS + 2 * layer, 1), :] = jnp.sum(grad_a, axis=0, keepdims=True)
-        acc_ref[...] += normalize_back(grad_a, unit, scale_ref[2 * layer], gain_ref[2 * layer])
+        acc_ref[...] += normalize_back(grad_a, unit, scale_ref[2 * layer], gain_at(2 * layer))
         return carry
 
     lax.fori_loop(0, layers, backward, 0)
-    group_row = lax.broadcasted_iota(jnp.int32, (groups, rows), 0).astype(single)
+    group_row = lax.broadcasted_iota(jnp.int32, (groups, entries), 0).astype(single)
     spread = (group_row == tags_row).astype(single)
     small_ref[2 * SLOTS : 2 * SLOTS + groups, :] = lax.dot_general(
-        spread, acc_ref[...], (((1,), (0,)), ((), ())), precision=highest, preferred_element_type=single
+        spread, sum_slots(acc_ref[...]), (((1,), (0,)), ((), ())), precision=highest, preferred_element_type=single
     )
     small_step(0)
-    for entry in range(entries):
-        at = entry * SLOTS
-        dx_ref[entry] = acc_ref[at : at + PIECES, :]
+    for part in range(2):
+        for slot in range(PIECES):
+            at = part * half + slot * group
+            dx_ref[slot, part * group : (part + 1) * group, :] = acc_ref[at : at + group, :]
+    dx_out = pltpu.make_async_copy(dx_ref, dx_hbm, store_sem.at[1])
+    dx_out.start()
 
     def tail_tick(step, carry):
         reduce_tick(step)
         return carry
 
-    last = units - z_count
-    small_step(1)
-    lax.fori_loop(last, last + 2, tail_tick, 0)
-    small_step(2)
-    lax.fori_loop(last + 2, last + 4, tail_tick, 0)
-    small_step(3)
-    lax.fori_loop(last + 4, units + REDUCE[-1], tail_tick, 0)
-    small_step(4)
-
-    def arrive(index, carry):
+    first, end = units - z_count - SHIFT, units + REDUCE[-1]
+    marks = [first, *(min(first + mark, end) for mark in MARKS), end]
+    for stage in range(4):
+        lax.fori_loop(marks[stage], marks[stage + 1], tail_tick, 0)
+        small_step(stage + 1)
+    lax.fori_loop(marks[4], marks[5], tail_tick, 0)
+
+    place_here = me * 2 + c
+    n_buf[place_here] = functools.reduce(jnp.add, [sum_ref[:, at * 128 : (at + 1) * 128] for at in range(width // 128)])
+
+    def send_norm(step):
+        other = lax.rem(place_here + step, 2 * dp)
+        return remote(
+            n_buf.at[place_here], n_buf.at[place_here], n_ss.at[other], n_rs.at[place_here],
+            (lax.div(other, 2), x * 2 + lax.rem(other, 2)),
+        )
+
+    def take_norm(step):
+        other = lax.rem(place_here + step, 2 * dp)
+        await_arrival(n_buf.at[other], n_ss.at[other], n_rs.at[other], (lax.div(other, 2), x * 2 + lax.rem(other, 2)))
+
+    def arrive(index):
         pair = out_ref.at[index, pl.ds(2 * (1 - c), 2)]
-        remote(pair, pair, fc_ss.at[index], fc_rs.at[index], c_side).wait_recv()
-        return carry
-
-    lax.fori_loop(0, mats, arrive, 0)
-
-    def squares(index, carry):
-        values = out_ref[index].astype(single)
-        return carry + jnp.sum(jnp.sum(values * values, axis=0), axis=0, keepdims=True)
-
-    squared = lax.fori_loop(0, mats, squares, jnp.zeros((1, out_ref.shape[3]), single))
-    n_buf[me] = jnp.broadcast_to(squared, n_buf.shape[1:])
-
-    def send_norm(step, carry):
-        other = lax.rem(me + step, dp)
-        remote(n_buf.at[me], n_buf.at[me], n_ss.at[other], n_rs.at[me], (other, x * 2 + c)).start()
-        return carry
-
-    lax.fori_loop(1, dp, send_norm, 0)
-
-    def wait_norm(step, carry):
-        other = lax.rem(me + step, dp)
-        remote(n_buf.at[other], n_buf.at[other], n_ss.at[other], n_rs.at[other], (other, x * 2 + c)).wait_recv()
-        return carry
-
-    lax.fori_loop(1, dp, wait_norm, 0)
+        await_arrival(pair, fc_ss.at[index], fc_rs.at[index], c_side)
+
+    def many(low, high, body):
+        lax.fori_loop(low, high, lambda step, carry: (body(step), carry)[1], 0)
+
+    many(1, 2 * dp, lambda step: send_norm(step).start())
+    many(0, mats, arrive)
+    many(1, 2 * dp, take_norm)
 
     def sum_norm(step, carry):
         return carry + n_buf[step]
 
-    spread = lax.fori_loop(0, dp, sum_norm, jnp.zeros(n_buf.shape[1:], single))
+    spread = lax.fori_loop(0, 2 * dp, sum_norm, jnp.zeros(n_buf.shape[1:], single))
     smalls = total_ref[...]
     norm_ref[...] = jnp.broadcast_to(
-        jnp.sum(spread[0:1], axis=1, keepdims=True) + jnp.sum(jnp.sum(smalls * smalls, axis=0, keepdims=True), axis=1, keepdims=True),
+        jnp.sum(jnp.sum(spread, axis=0, keepdims=True), axis=1, keepdims=True)
+        + jnp.sum(jnp.sum(smalls * smalls, axis=0, keepdims=True), axis=1, keepdims=True),
         norm_ref.shape,
     )
 
@@ -779,36 +886,45 @@
 
     lax.fori_loop(1, z_count, done_z, 0)
 
-    def done_norm(step, carry):
-        other = lax.rem(me + step, dp)
-        remote(n_buf.at[me], n_buf.at[me], n_ss.at[other], n_rs.at[me], (other, x * 2 + c)).wait_send()
-        return carry
-
-    lax.fori_loop(1, dp, done_norm, 0)
-
-
-def train_step(pieces, meta, cotangent, packed, gain, bias, table, layers, dp):
-    entries, _, width = pieces.shape
-    mats, blocks, shard_rows, _ = packed.shape
+    many(1, 2 * dp, lambda step: send_norm(step).wait_send())
+    emb_out.wait()
+    dx_out.wait()
+
+
+def train_step(pieces, tags, counts, cotangent, weights, gain, bias, table, layers, dp):
+    _, entries, width = pieces.shape
+    shard_rows = weights[0].shape[2]
+    mats = 3 * layers + 1
     rows = entries * SLOTS
     pairs = width // 128
     z_count = dp // 2
     small = (SMALL_ROWS, width)
     vmem = pl.BlockSpec(memory_space=VMEM)
+    where_it_is = pl.BlockSpec(memory_space=pltpu.HBM)
     dma = pltpu.SemaphoreType.DMA
-    whole = (mats, blocks, z_count, 2, shard_rows, width)
+    whole = (mats, BLOCKS, z_count, 2, shard_rows, width)
     return pl.pallas_call(
         functools.partial(step_kernel, layers, z_count),
         out_shape=(
             jax.ShapeDtypeStruct(cotangent.shape, single),
             jax.ShapeDtypeStruct(pieces.shape, single),
-            jax.ShapeDtypeStruct(packed.shape, bfloat),
+            jax.ShapeDtypeStruct((mats, BLOCKS, shard_rows, width), bfloat),
             jax.ShapeDtypeStruct(small, single),
             jax.ShapeDtypeStruct((8, 128), single),
         ),
-        in_specs=[vmem] * 7,
-        out_specs=(vmem,) * 5,
+        in_specs=[where_it_is] * 12,
+        out_specs=(where_it_is, where_it_is, vmem, vmem, vmem),
         scratch_shapes=[
+            VMEM(pieces.shape, bfloat),
+            VMEM(tags.shape, jnp.int32),
+            VMEM(counts.shape, jnp.int32),
+            VMEM(cotangent.shape, bfloat),
+            VMEM(gain.shape, single),
+            VMEM(bias.shape, single),
+            VMEM(table.shape, single),
+            VMEM(cotangent.shape, single),
+            VMEM(pieces.shape, single),
+            VMEM((8, width), single),
             VMEM(whole, bfloat),
             VMEM(whole, bfloat),
             VMEM((mats, 2, z_count, shard_rows, width), bfloat),
@@ -835,7 +951,7 @@
             VMEM(small, single),
             VMEM((z_count, *small), single),
             VMEM((2, *small), single),
-            VMEM((dp, 8, width), single),
+            VMEM((2 * dp, 8, 128), single),
             dma((mats, z_count, 2)),
             dma((mats,)),
             dma((mats, 2, z_count, 2)),
@@ -844,13 +960,105 @@
             *[dma((mats,))] * 4,
             dma((3 + z_count,)),
             dma((3 + z_count,)),
-            dma((dp,)),
-            dma((dp,)),
+            dma((2 * dp,)),
+            dma((2 * dp,)),
             pltpu.SemaphoreType.REGULAR((3, mats)),
+            dma((7,)),
+            dma((mats, 2)),
+            dma((2,)),
         ],
         compiler_params=pltpu.CompilerParams(collective_id=1, has_side_effects=True, vmem_limit_bytes=60 * 2**20),
         name="train_step",
-    )(pieces, meta, cotangent, packed, gain, bias, table)
+    )(pieces, tags, counts, cotangent, *weights, gain, bias, table)
+
+
+def update_kernel(layers, norms, *refs):
+    norm_ref, grad_ref, small_ref, emb_in, dx_in = refs[:5]
+    state_in, (emb_out, dx_out, root_ref), state_out = refs[5:29], refs[29:32], refs[32:56]
+    held, (emb_ref, dx_ref, load_sem, store_sem, pass_sem) = refs[56:80], refs[80:]
+    passing = [pltpu.make_async_copy(emb_in, emb_ref, pass_sem.at[0]), pltpu.make_async_copy(dx_in, dx_ref, pass_sem.at[1])]
+    passed = [pltpu.make_async_copy(emb_ref, emb_out, pass_sem.at[2]), pltpu.make_async_copy(dx_ref, dx_out, pass_sem.at[3])]
+    loads = [pltpu.make_async_copy(state_in[at], held[at], load_sem.at[at]) for at in range(24)]
+    stores = [pltpu.make_async_copy(held[at], state_out[at], store_sem.at[at]) for at in range(24)]
+    for copy in loads + passing:
+        copy.start()
+    root = jnp.sqrt(norm_ref[0:1, 0:1])
+    root_ref[...] = root
+    clip_scale = jnp.minimum(1.0, clip_level / (root + 1e-06))
+    width = grad_ref.shape[3]
+    proj = 3 * layers
+
+    def piece(base, at, gradient, decay, rate):
+        weight, first, second = (held[3 * base + kind] for kind in range(3))
+        new = adam_update(weight[at], first[at], second[at], gradient.astype(single), clip_scale, decay, rate)
+        weight[at], first[at], second[at] = new
+
+    def group(base, work):
+        for copy in loads[3 * base : 3 * base + 3]:
+            copy.wait()
+        work()
+        for copy in stores[3 * base : 3 * base + 3]:
+            copy.start()
+
+    def each_layer(body):
+        def wrapped(layer, carry):
+            body(layer)
+            return carry
+
+        return lambda: lax.fori_loop(0, layers, wrapped, 0)
+
+    def lanes(block):
+        return slice(block * width, (block + 1) * width)
+
+    def front(layer):
+        for part in range(3):
+            piece(0, (layer, part), grad_ref[3 * layer, part], decay_rate, learn_rate)
+
+    def outward(layer):
+        piece(1, (layer,), grad_ref[3 * layer, 3], decay_rate, learn_rate)
+
+    def rise(layer):
+        for block in range(BLOCKS):
+            piece(2, (layer, slice(None), lanes(block)), grad_ref[3 * layer + 1, block], decay_rate, learn_rate)
+
+    def fall(layer):
+        for block in range(BLOCKS):
+            piece(3, (layer, slice(None), lanes(block)), grad_ref[3 * layer + 2, block], decay_rate, learn_rate)
+
+    def project():
+        for block in range(BLOCKS):
+            piece(4, (slice(None), lanes(block)), grad_ref[proj, block], decay_rate, learn_rate)
+
+    group(0, each_layer(front))
+    group(1, each_layer(outward))
+    for arrived, copy in zip(passing, passed):
+        arrived.wait()
+        copy.start()
+    group(2, each_layer(rise))
+    group(3, each_layer(fall))
+    group(4, project)
+    whole = (slice(None), slice(None))
+    group(5, lambda: piece(5, whole, small_ref[:norms], 0.0, small_rate))
+    group(6, lambda: piece(6, whole, small_ref[SLOTS : SLOTS + norms], 0.0, small_rate))
+    group(7, lambda: piece(7, whole, small_ref[2 * SLOTS : 2 * SLOTS + held[21].shape[0]], 0.0, small_rate))
+    for copy in stores + passed:
+        copy.wait()
+
+
+def update(square_total, reduced, small_total, embeddings, input_grad, state, layers, norms):
+    vmem = pl.BlockSpec(memory_space=VMEM)
+    where_it_is = pl.BlockSpec(memory_space=pltpu.HBM)
+    dma = pltpu.SemaphoreType.DMA
+    like = lambda array: jax.ShapeDtypeStruct(array.shape, single)
+    return pl.pallas_call(
+        functools.partial(update_kernel, layers, norms),
+        out_shape=(like(embeddings), like(input_grad), jax.ShapeDtypeStruct((1, 1), single), *map(like, state)),
+        in_specs=[vmem] * 3 + [where_it_is] * 26,
+        out_specs=(where_it_is, where_it_is, vmem) + (where_it_is,) * 24,
+        scratch_shapes=[*[VMEM(array.shape, single) for array in (*state, embeddings, input_grad)], dma((24,)), dma((24,)), dma((4,))],
+        compiler_params=pltpu.CompilerParams(vmem_limit_bytes=60 * 2**20),
+        name="update",
+    )(square_total, reduced, small_total, embeddings, input_grad, *state)
 
 
 def adam_update(weight, first, second, gradient, clip_scale, decay, step_rate):
@@ -861,28 +1069,6 @@
     second_hat = second_new / (1.0 - beta_second**STEP)
     weight_new = weight - step_rate * (first_hat / (jnp.sqrt(second_hat) + adam_eps) + decay * weight)
     return (weight_new, first_new, second_new)
-
-
-def pack(qkv, out, up, down, proj):
-    layers, _, rows, width = qkv.shape
-    parts = []
-    front = jnp.concatenate([qkv, jnp.swapaxes(out, 1, 2)[:, None]], axis=1)
-    rise = jnp.swapaxes(up.reshape(layers, rows, BLOCKS, width), 1, 2)
-    fall = jnp.swapaxes(jnp.swapaxes(down, 1, 2).reshape(layers, rows, BLOCKS, width), 1, 2)
-    body = jnp.stack([front, rise, fall], axis=1).reshape(3 * layers, BLOCKS, rows, width)
-    last = jnp.swapaxes(proj.reshape(rows, BLOCKS, width), 0, 1)[None]
-    return jnp.concatenate([body, last], axis=0)
-
-
-def unpack(packed, layers):
-    _, _, rows, width = packed.shape
-    body = packed[: 3 * layers].reshape(layers, 3, BLOCKS, rows, width)
-    qkv = body[:, 0, :3]
-    out = jnp.swapaxes(body[:, 0, 3], 1, 2)
-    up = jnp.swapaxes(body[:, 1], 1, 2).reshape(layers, rows, BLOCKS * width)
-    down = jnp.swapaxes(jnp.swapaxes(body[:, 2], 1, 2).reshape(layers, rows, BLOCKS * width), 1, 2)
-    proj = jnp.swapaxes(packed[3 * layers], 0, 1).reshape(rows, BLOCKS * width)
-    return qkv, out, up, down, proj
 
 
 def per_device(
@@ -897,40 +1083,32 @@
     group_table, table_first, table_second,
 ):
     layers = qkv_weight.shape[0]
-    width = pieces.shape[2]
     dp = lax.axis_size("dp")
     norms = norm_gain.shape[0]
-    groups = group_table.shape[0]
-    packed = pack(
-        qkv_weight.astype(bfloat), out_weight.astype(bfloat), up_weight.astype(bfloat), down_weight.astype(bfloat), proj_weight.astype(bfloat)
+
+    def turn(array):
+        return jnp.swapaxes(array, 1, 2)
+
+    state = (
+        qkv_weight, qkv_first, qkv_second,
+        turn(out_weight), turn(out_first), turn(out_second),
+        up_weight, up_first, up_second,
+        turn(down_weight), turn(down_first), turn(down_second),
+        proj_weight, proj_first, proj_second,
+        norm_gain, gain_first, gain_second,
+        norm_bias, bias_first, bias_second,
+        group_table, table_first, table_second,
     )
-    meta = jnp.stack([jnp.repeat(script_tags, SLOTS), jnp.repeat(counts, SLOTS)]).astype(single)
-    meta = jnp.concatenate([meta, jnp.zeros((SLOTS - 2, meta.shape[1]), single)], axis=0)
     embeddings, input_grad, reduced, small_total, square_total = train_step(
-        pieces, meta, cotangent, packed,
-        norm_gain.reshape(norms, 1, width), norm_bias.reshape(norms, 1, width), group_table, layers, dp,
+        jnp.swapaxes(pieces, 0, 1), script_tags.reshape(1, -1), counts.reshape(1, -1), cotangent, state[0:15:3],
+        norm_gain, norm_bias, group_table, layers, dp,
     )
-    grad_norm = jnp.sqrt(square_total[0, 0])
-    clip_scale = jnp.minimum(1.0, clip_level / (grad_norm + 1e-06))
-    grad_qkv, grad_out, grad_up, grad_down, grad_proj = unpack(reduced.astype(single), layers)
-    grad_gain = small_total[:norms]
-    grad_bias = small_total[SLOTS : SLOTS + norms]
-    grad_table = small_total[2 * SLOTS : 2 * SLOTS + groups]
-    big = functools.partial(adam_update, clip_scale=clip_scale, decay=decay_rate, step_rate=learn_rate)
-    little = functools.partial(adam_update, clip_scale=clip_scale, decay=0.0, step_rate=small_rate)
-    return (
-        embeddings,
-        input_grad,
-        grad_norm,
-        *big(qkv_weight, qkv_first, qkv_second, grad_qkv),
-        *big(out_weight, out_first, out_second, grad_out),
-        *big(up_weight, up_first, up_second, grad_up),
-        *big(down_weight, down_first, down_second, grad_down),
-        *big(proj_weight, proj_first, proj_second, grad_proj),
-        *little(norm_gain, gain_first, gain_second, grad_gain),
-        *little(norm_bias, bias_first, bias_second, grad_bias),
-        *little(group_table, table_first, table_second, grad_table),
+    embeddings, input_grad, grad_norm, *state = update(
+        square_total, reduced, small_total, embeddings, input_grad, state, layers, norms
     )
+    state[3:6] = map(turn, state[3:6])
+    state[9:12] = map(turn, state[9:12])
+    return (embeddings, jnp.swapaxes(input_grad, 0, 1), grad_norm.reshape(()), *state)
 
 
 def solution(mesh):

time: 238 us -> 201 us (0.84)
  local copies, waits for them, and re-layouts: 18.6 us -> 0 us
  other arithmetic: 16.2 us -> 0 us
    pallas_call x0 -> x1, Pallas kernels: none -> 12.2 us  [update(): pl.pallas_call(functools.partial(update_kernel, layers, norms), out_shape...]
    pallas_call x1, Pallas kernels: 200 us -> 188 us  [train_step(): pl.pallas_call(functools.partial(step_kernel, layers, z_count), out_shape...]
    sub x7 -> x0, other arithmetic: 11.5 us -> none  [adam_update(): weight - step_rate * (first_hat / (jnp.sqrt(second_hat) + adam_eps) + dec...]
    unnamed x55 -> x0, local copies, waits for them, and re-layouts: 10.2 us -> none
    slice x2 -> x0, local copies, waits for them, and re-layouts: 3.07 us -> none  [the longest x1 1.89 us: unpack(): body = packed[:3 * layers].reshape(layers, 3, BLOCKS, rows, width)]
    reshape x3 -> x0, local copies, waits for them, and re-layouts: 2.74 us -> none  [the longest x1 1.4 us: per_device(): norm_gain.reshape(norms, 1, width)]
where the time goes in v3:
time: 201 us
  Pallas kernels  200 us (100%)
    pallas_call x1, Pallas kernels, train_step(): pl.pallas_call(functools.partial(step_kernel, layers, z_count), out_shape...  188 us
    pallas_call x1, Pallas kernels, update(): pl.pallas_call(functools.partial(update_kernel, layers, norms), out_shape...  12.2 us

profile of v3, /device:TPU:0, one launch (start us, length us, event | category | flops | bytes accessed | tf_op | source)
XLA Modules:
  0.0 200.9 jit_solution(3580611026142015238)
XLA Ops:
  0.7 187.9 %train_step.1 = (f32[32,2048]{1,0:T(8,128)}, f32[7,32,512]{2,1,0:T(8,128)}, bf16[7,4,64,512]{3,2,1,0:T(8,128)(2,1)}, f32[32,512]{1,0:T(8,128)}, f32[8,128]{1,0:T(8,128)}) custom-call(bf16[7,32,512]{2,1,0:T(8,128)(2,1)} %bitcast.25, s32[1,32]{1,0:T(1,128)} %bitcast.26, s32[1,32]{1,0:T(1,128)} %bitcast.27, bf16[32,2048]{1,0:T(8,128)(2,1)} %cot_hbm.1, ...), custom_call_target="tpu_custom_call" | custom-call | tf_op jit(solution)/shard_map/train_step/pallas_call | solution.py:906
  188.6 12.2 %update.1 = (f32[32,2048]{1,0:T(8,128)}, f32[7,32,512]{2,1,0:T(8,128)}, f32[1,1]{1,0:T(1,128)}, f32[2,3,64,512]{3,2,1,0:T(8,128)}, f32[2,3,64,512]{3,2,1,0:T(8,1...) custom-call(f32[8,128]{1,0:T(8,128)} %get-tuple-element.59.refs_0_, ...), custom_call_target="tpu_custom_call" | custom-call | tf_op jit(solution)/shard_map/update/pallas_call | solution.py:1053

commit v4 on v3

--- a/solution.py
+++ b/solution.py
@@ -122,32 +122,33 @@
     return scale * (grad_unit - first - unit * second)
 
 
-def shared_gather(index, zz):
-    return lax.rem(index + zz, 4) == 0
+def shared_gather(layers, index, zz):
+    return jnp.logical_or(index == 3 * layers - 1, lax.rem(index * 4 + zz, 8) == 0)
 
 
 def shared_reduce(index, target):
     return lax.rem(index + target, 2) == 1
 
 
-AHEAD = 2
+AHEAD = 1
 LAGS = (1, 2, 3)
 REDUCE = (0, 3, 6, 8, 9, 11)
 SHIFT = 0
-MARKS = (2, 5, 8, 11)
+MARKS = (3, 7, 10, 13)
 
 
 def step_kernel(
     layers, z_count,
     pieces_hbm, tags_hbm, counts_hbm, cot_hbm, qkv_hbm, outward_hbm, rise_hbm, fall_hbm, proj_hbm, gain_hbm, bias_hbm, table_hbm,
-    emb_hbm, dx_hbm, out_ref, total_ref, norm_ref,
+    emb_hbm, dx_hbm, out_hbm, total_ref, norm_ref,
+    out_ref,
     pieces_ref, tags_ref, counts_ref, cot_ref, gain_ref, bias_ref, table_ref, emb_ref, dx_ref, sum_ref,
     w_ref, grad_ref, z_buf, f_buf, part_ref,
     x_ref, unit_ref, scale_ref, a_ref, b_ref, qkv_ref, prob_ref, o_ref, g_ref, slope_ref, dqkv_ref, do_ref, acc_ref, turn_ref, dpool_ref,
     small_ref, s_c, s_x, s_y, s_z, s_cur, n_buf,
     gx_ss, gc_ss, g_rs, gc_rs,
     c_ss, c_rs, x_ss, x_rs, y_ss, y_rs, z_ss, z_rs, fx_ss, fx_rs, fc_ss, fc_rs, s_ss, s_rs, n_ss, n_rs, credit,
-    in_sem, load_sem, store_sem,
+    in_sem, load_sem, store_sem, out_sem,
 ):
     mats = 3 * layers + 1
     proj = 3 * layers
@@ -214,7 +215,7 @@
         return jnp.where(turn < early, turn, jnp.where(turn == early, proj, turn - 1))
 
     def by_type(index, zz, body):
-        shared = shared_gather(index, zz)
+        shared = shared_gather(layers, index, zz)
         when(shared, lambda: body(pl.ds(2 * c, 2), False))
         when(otherwise(shared), lambda: body(pl.ds(2 * c + x, 1), True))
 
@@ -253,9 +254,9 @@
         def one(zz):
             def pass_on(span, cross):
                 arrived(index, zz, y, span)
-                gather_y(index, zz, span).start()
                 if cross:
                     gather_x(index, zz, y, span).start()
+                gather_y(index, zz, span).start()
 
             pl.when(z != zz)(lambda: by_type(index, zz, pass_on))
 
@@ -282,7 +283,7 @@
                 pl.when(zz != z)(lambda: one(y))
                 one(1 - y)
 
-            when(otherwise(shared_gather(index, zz)), two)
+            when(otherwise(shared_gather(layers, index, zz)), two)
 
         loop(0, z_count, each)
         gather_c(index).start()
@@ -724,6 +725,7 @@
 
         def hidden(turn, carry):
             block = lax.rem(turn + 2 * (1 - c), BLOCKS)
+            spread_ticks(tick - SHIFT, z_count, turn, BLOCKS)
             put_grad(3 * layer + 2, block, dot_nn(turn_ref[0], g_ref[layer, block]))
             grad_act = dot_nn(do_ref[...], block_of(3 * layer + 2, block))
             du = (grad_act * slope_ref[layer, block]).astype(bfloat)
@@ -735,7 +737,6 @@
                 start_matrix(3 * layer + 2)
                 start_matrix(3 * layer + 1)
 
-            spread_ticks(tick - SHIFT, z_count, turn, BLOCKS)
             return carry
 
         lax.fori_loop(0, BLOCKS, hidden, 0)
@@ -753,6 +754,7 @@
 
         def attend(pair, carry):
             lanes = pl.ds(pl.multiple_of(pair * 128, 128), 128)
+            spread_ticks(tick + z_count - SHIFT, 2 * z_count, pair, pairs)
             for part in range(2):
                 here = slice(part * half, (part + 1) * half)
                 q = qkv_ref[layer, 0, here, lanes]
@@ -774,7 +776,6 @@
                 dqkv_ref[0, here, lanes] = (dq * HD ** (-0.5)).astype(bfloat)
                 dqkv_ref[1, here, lanes] = (jnp.where(low_lane, dk[:half], dk[half:]) * HD ** (-0.5)).astype(bfloat)
                 dqkv_ref[2, here, lanes] = jnp.where(low_lane, dv[:half], dv[half:]).astype(bfloat)
-            spread_ticks(tick + z_count - SHIFT, 2 * z_count, pair, pairs)
             return carry
 
         lax.fori_loop(0, pairs, attend, 0)
@@ -830,9 +831,13 @@
         other = lax.rem(place_here + step, 2 * dp)
         await_arrival(n_buf.at[other], n_ss.at[other], n_rs.at[other], (lax.div(other, 2), x * 2 + lax.rem(other, 2)))
 
+    def out_copy(index):
+        return pltpu.make_async_copy(out_ref.at[index], out_hbm.at[index], out_sem.at[index])
+
     def arrive(index):
         pair = out_ref.at[index, pl.ds(2 * (1 - c), 2)]
         await_arrival(pair, fc_ss.at[index], fc_rs.at[index], c_side)
+        out_copy(index).start()
 
     def many(low, high, body):
         lax.fori_loop(low, high, lambda step, carry: (body(step), carry)[1], 0)
@@ -889,6 +894,7 @@
     many(1, 2 * dp, lambda step: send_norm(step).wait_send())
     emb_out.wait()
     dx_out.wait()
+    many(0, mats, lambda index: out_copy(index).wait())
 
 
 def train_step(pieces, tags, counts, cotangent, weights, gain, bias, table, layers, dp):
@@ -913,8 +919,9 @@
             jax.ShapeDtypeStruct((8, 128), single),
         ),
         in_specs=[where_it_is] * 12,
-        out_specs=(where_it_is, where_it_is, vmem, vmem, vmem),
+        out_specs=(where_it_is, where_it_is, where_it_is, vmem, vmem),
         scratch_shapes=[
+            VMEM((mats, BLOCKS, shard_rows, width), bfloat),
             VMEM(pieces.shape, bfloat),
             VMEM(tags.shape, jnp.int32),
             VMEM(counts.shape, jnp.int32),
@@ -966,6 +973,7 @@
             dma((7,)),
             dma((mats, 2)),
             dma((2,)),
+            dma((mats,)),
         ],
         compiler_params=pltpu.CompilerParams(collective_id=1, has_side_effects=True, vmem_limit_bytes=60 * 2**20),
         name="train_step",
@@ -973,14 +981,16 @@
 
 
 def update_kernel(layers, norms, *refs):
-    norm_ref, grad_ref, small_ref, emb_in, dx_in = refs[:5]
+    norm_ref, grad_in, small_ref, emb_in, dx_in = refs[:5]
     state_in, (emb_out, dx_out, root_ref), state_out = refs[5:29], refs[29:32], refs[32:56]
-    held, (emb_ref, dx_ref, load_sem, store_sem, pass_sem) = refs[56:80], refs[80:]
+    held, (emb_ref, dx_ref, grad_ref, load_sem, store_sem, pass_sem) = refs[56:80], refs[80:]
     passing = [pltpu.make_async_copy(emb_in, emb_ref, pass_sem.at[0]), pltpu.make_async_copy(dx_in, dx_ref, pass_sem.at[1])]
     passed = [pltpu.make_async_copy(emb_ref, emb_out, pass_sem.at[2]), pltpu.make_async_copy(dx_ref, dx_out, pass_sem.at[3])]
     loads = [pltpu.make_async_copy(state_in[at], held[at], load_sem.at[at]) for at in range(24)]
     stores = [pltpu.make_async_copy(held[at], state_out[at], store_sem.at[at]) for at in range(24)]
-    for copy in loads + passing:
+    grads = pltpu.make_async_copy(grad_in, grad_ref, pass_sem.at[4])
+    grads.start()
+    for copy in loads[:9]:
         copy.start()
     root = jnp.sqrt(norm_ref[0:1, 0:1])
     root_ref[...] = root
@@ -993,9 +1003,11 @@
         new = adam_update(weight[at], first[at], second[at], gradient.astype(single), clip_scale, decay, rate)
         weight[at], first[at], second[at] = new
 
-    def group(base, work):
+    def group(base, work, ahead=()):
         for copy in loads[3 * base : 3 * base + 3]:
             copy.wait()
+        for copy in ahead:
+            copy.start()
         work()
         for copy in stores[3 * base : 3 * base + 3]:
             copy.start()
@@ -1029,13 +1041,14 @@
         for block in range(BLOCKS):
             piece(4, (slice(None), lanes(block)), grad_ref[proj, block], decay_rate, learn_rate)
 
-    group(0, each_layer(front))
-    group(1, each_layer(outward))
+    grads.wait()
+    group(0, each_layer(front), loads[9:12])
+    group(1, each_layer(outward), loads[12:15])
+    group(2, each_layer(rise), passing + loads[15:])
+    group(3, each_layer(fall))
     for arrived, copy in zip(passing, passed):
         arrived.wait()
         copy.start()
-    group(2, each_layer(rise))
-    group(3, each_layer(fall))
     group(4, project)
     whole = (slice(None), slice(None))
     group(5, lambda: piece(5, whole, small_ref[:norms], 0.0, small_rate))
@@ -1053,9 +1066,9 @@
     return pl.pallas_call(
         functools.partial(update_kernel, layers, norms),
         out_shape=(like(embeddings), like(input_grad), jax.ShapeDtypeStruct((1, 1), single), *map(like, state)),
-        in_specs=[vmem] * 3 + [where_it_is] * 26,
+        in_specs=[vmem, where_it_is, vmem] + [where_it_is] * 26,
         out_specs=(where_it_is, where_it_is, vmem) + (where_it_is,) * 24,
-        scratch_shapes=[*[VMEM(array.shape, single) for array in (*state, embeddings, input_grad)], dma((24,)), dma((24,)), dma((4,))],
+        scratch_shapes=[*[VMEM(array.shape, single) for array in (*state, embeddings, input_grad)], VMEM(reduced.shape, bfloat), dma((24,)), dma((24,)), dma((5,))],
         compiler_params=pltpu.CompilerParams(vmem_limit_bytes=60 * 2**20),
         name="update",
     )(square_total, reduced, small_total, embeddings, input_grad, *state)

time: 201 us -> 185 us (0.920)
  Pallas kernels: 200 us -> 184 us
    pallas_call x1, Pallas kernels: 188 us -> 172 us  [train_step(): pl.pallas_call(functools.partial(step_kernel, layers, z_count), out_shape...]
where the time goes in v4:
time: 185 us
  Pallas kernels  184 us (99%)
    pallas_call x1, Pallas kernels, train_step(): pl.pallas_call(functools.partial(step_kernel, layers, z_count), out_shape...  172 us
    pallas_call x1, Pallas kernels, update(): pl.pallas_call(functools.partial(update_kernel, layers, norms), out_shape...  11.4 us

profile of v4, /device:TPU:0, one launch (start us, length us, event | category | flops | bytes accessed | tf_op | source)
XLA Modules:
  0.0 184.6 jit_solution(15054733459836658188)
XLA Ops:
  0.7 172.3 %train_step.1 = (f32[32,2048]{1,0:T(8,128)}, f32[7,32,512]{2,1,0:T(8,128)}, bf16[7,4,64,512]{3,2,1,0:T(8,128)(2,1)}, f32[32,512]{1,0:T(8,128)}, f32[8,128]{1,0:T(8,128)}) custom-call(bf16[7,32,512]{2,1,0:T(8,128)(2,1)} %bitcast.25, s32[1,32]{1,0:T(1,128)} %bitcast.26, s32[1,32]{1,0:T(1,128)} %bitcast.27, bf16[32,2048]{1,0:T(8,128)(2,1)} %cot_hbm.1, ...), custom_call_target="tpu_custom_call" | custom-call | tf_op jit(solution)/shard_map/train_step/pallas_call | solution.py:912
  173.0 11.4 %update.1 = (f32[32,2048]{1,0:T(8,128)}, f32[7,32,512]{2,1,0:T(8,128)}, f32[1,1]{1,0:T(1,128)}, f32[2,3,64,512]{3,2,1,0:T(8,128)}, f32[2,3,64,512]{3,2,1,0:T(8,1...) custom-call(f32[8,128]{1,0:T(8,128)} %get-tuple-element.59.refs_0_, ...), custom_call_target="tpu_custom_call" | custom-call | tf_op jit(solution)/shard_map/update/pallas_call | solution.py:1066

commit v5 on v4

--- a/solution.py
+++ b/solution.py
@@ -132,9 +132,9 @@
 
 AHEAD = 1
 LAGS = (1, 2, 3)
-REDUCE = (0, 3, 6, 8, 9, 11)
+REDUCE = (0, 3, 6, 8, 11, 15)
 SHIFT = 0
-MARKS = (3, 7, 10, 13)
+MARKS = (4, 8, 12, 16)
 
 
 def step_kernel(
@@ -497,7 +497,7 @@
         sum_ref[...] += jnp.sum((values * values).reshape(-1, 8, width), axis=0)
 
     def reduce_tick(step):
-        for lag, stage in zip(REDUCE, (stage_c, stage_x, stage_y, stage_r)):
+        for lag, stage in reversed(list(zip(REDUCE, (stage_c, stage_x, stage_y, stage_r)))):
             unit = step - lag
             pl.when(jnp.logical_and(unit >= 0, unit < units))(functools.partial(stage, unit))
         for lag, stage in zip(REDUCE[4:], (stage_z, stage_f)):
@@ -680,7 +680,7 @@
         def _():
             own(matrix_at(step + AHEAD))
 
-        for lag, stage in zip((0, *LAGS), (line, beside, opposite, finish)):
+        for lag, stage in [list(zip((0, *LAGS), (line, beside, opposite, finish)))[q] for q in (2, 1, 0, 3)]:
             turn = step - lag
             pl.when(jnp.logical_and(turn >= 0, turn < mats))(lambda: stage(matrix_at(turn)))
         index = matrix_at(step - depth)

time: 185 us -> 180 us (0.973)
  Pallas kernels: 184 us -> 179 us
    pallas_call x1, Pallas kernels: 172 us -> 168 us  [train_step(): pl.pallas_call(functools.partial(step_kernel, layers, z_count), out_shape...]
where the time goes in v5:
time: 180 us
  Pallas kernels  179 us (99%)
    pallas_call x1, Pallas kernels, train_step(): pl.pallas_call(functools.partial(step_kernel, layers, z_count), out_shape...  168 us
    pallas_call x1, Pallas kernels, update(): pl.pallas_call(functools.partial(update_kernel, layers, norms), out_shape...  11.4 us

profile of v5, /device:TPU:0, one launch (start us, length us, event | category | flops | bytes accessed | tf_op | source)
XLA Modules:
  0.0 179.9 jit_solution(8314802262589338892)
XLA Ops:
  0.7 167.6 %train_step.1 = (f32[32,2048]{1,0:T(8,128)}, f32[7,32,512]{2,1,0:T(8,128)}, bf16[7,4,64,512]{3,2,1,0:T(8,128)(2,1)}, f32[32,512]{1,0:T(8,128)}, f32[8,128]{1,0:T(8,128)}) custom-call(bf16[7,32,512]{2,1,0:T(8,128)(2,1)} %bitcast.25, s32[1,32]{1,0:T(1,128)} %bitcast.26, s32[1,32]{1,0:T(1,128)} %bitcast.27, bf16[32,2048]{1,0:T(8,128)(2,1)} %cot_hbm.1, ...), custom_call_target="tpu_custom_call" | custom-call | tf_op jit(solution)/shard_map/train_step/pallas_call | solution.py:912
  168.3 11.4 %update.1 = (f32[32,2048]{1,0:T(8,128)}, f32[7,32,512]{2,1,0:T(8,128)}, f32[1,1]{1,0:T(1,128)}, f32[2,3,64,512]{3,2,1,0:T(8,128)}, f32[2,3,64,512]{3,2,1,0:T(8,1...) custom-call(f32[8,128]{1,0:T(8,128)} %get-tuple-element.59.refs_0_, ...), custom_call_target="tpu_custom_call" | custom-call | tf_op jit(solution)/shard_map/update/pallas_call | solution.py:1066
